TPU v7x, 256 devices: a whole 4x4x8 slice. The times are simulated.
256 devices in a mesh: samp: 8 (over y, core), ty: 8 (over z), tx: 4 (over x).
Axes of the slice: x: 4, y: 4, z: 8, core: 2. Of those that a mesh axis runs over, the one named last changes fastest.
Arguments:
- radiance: float32 [8, 3, 1024, 512], P('samp', None, 'ty', 'tx'), may hold values from 0 to 64
- moment: float32 [8, 1024, 512], P('samp', 'ty', 'tx'), may hold values from 0 to 128
- normal: float32 [8, 3, 1024, 512], P('samp', None, 'ty', 'tx'), may hold values from -192 to 192
- depth_sum: float32 [8, 1024, 512], P('samp', 'ty', 'tx'), may hold values from 0 to 64
- counts: int32 [8, 64, 32], P('samp', 'ty', 'tx'), may hold values from 1 to 64
Outputs:
- denoised: float32 [3, 1024, 512], P(None, 'ty', 'tx')
- variance: float32 [1024, 512], P('ty', 'tx')
All inputs are finite; a program needn't handle non-finite values.
Results may differ from a plain program's by a relative error of at most 0.0001.
Values sent between devices are 32-bit elements; how exact they have to be, the bound alone decides.
No kernel may reach another device: no remote copies, remote signals or barrier semaphores. Data moves between devices by JAX's collectives and lax.ppermute only.
A program may use at most 64 MiB of HBM per device.

v0:
```python
import jax
import jax.numpy as jnp
from jax import lax
from jax.sharding import PartitionSpec as P

LEVELS = 4
BLK = 16


TAPS = (0.0625, 0.25, 0.375, 0.25, 0.0625)
SIGMA_DEPTH = 0.5
SIGMA_NORMAL = 1.0
SIGMA_LUMA = 4.0
LUMA_FLOOR = 0.5


def padded_2(value, sides, width):
    for axis, dim in sides:
        size, length = (lax.axis_size(axis), value.shape[dim])
        up = [(i, (i + 1) % size) for i in range(size - 1)]
        down = [(j, i) for i, j in up]
        last = lax.slice_in_dim(value, length - width, length, axis=dim)
        first = lax.slice_in_dim(value, 0, width, axis=dim)
        before = lax.ppermute(last, axis, up)
        after = lax.ppermute(first, axis, down)
        value = jnp.concatenate([before, value, after], axis=dim)
    return value


def luminance(colour):
    return 0.2126 * colour[0] + 0.7152 * colour[1] + 0.0722 * colour[2]


def atrous_level(colour_pad, var_pad, normal_pad, depth_pad, inside_pad, dilation, height, breadth):
    rim_rows = 2 * dilation

    def centre(source):
        return source[..., rim_rows : rim_rows + height, rim_rows : rim_rows + breadth]

    colour_mid = centre(colour_pad)
    normal_mid = centre(normal_pad)
    depth_mid = centre(depth_pad)
    luma_mid = luminance(colour_mid)
    spread = SIGMA_LUMA * jnp.sqrt(centre(var_pad)) + LUMA_FLOOR
    weight_sum = jnp.zeros((height, breadth), jnp.float32)
    colour_acc = jnp.zeros((3, height, breadth), jnp.float32)
    var_acc = jnp.zeros((height, breadth), jnp.float32)
    for tap_row in range(5):
        for tap_col in range(5):
            top_row = tap_row * dilation
            left_col = tap_col * dilation

            def window(source):
                return source[..., top_row : top_row + height, left_col : left_col + breadth]

            colour_tap = window(colour_pad)
            exponent = jnp.abs(window(depth_pad) - depth_mid) / SIGMA_DEPTH
            exponent = (
                exponent
                + jnp.sum(jnp.square(window(normal_pad) - normal_mid), axis=0) / SIGMA_NORMAL
            )
            exponent = exponent + jnp.abs(luminance(colour_tap) - luma_mid) / spread
            weight = TAPS[tap_row] * TAPS[tap_col] * window(inside_pad) * jnp.exp(-exponent)
            weight_sum = weight_sum + weight
            colour_acc = colour_acc + weight[None] * colour_tap
            var_acc = var_acc + weight * weight * window(var_pad)
    return (colour_acc / weight_sum[None], var_acc / (weight_sum * weight_sum))


def inside_mask(row_first, col_first, rows_len, cols_len, full_rows, full_cols):
    row_ids = row_first + jnp.arange(rows_len, dtype=jnp.int32)
    col_ids = col_first + jnp.arange(cols_len, dtype=jnp.int32)
    row_ok = ((row_ids >= 0) & (row_ids < full_rows)).astype(jnp.float32)
    col_ok = ((col_ids >= 0) & (col_ids < full_cols)).astype(jnp.float32)
    return row_ok[:, None] * col_ok[None, :]


def per_device(radiance, moment, normal, depth_sum, counts):
    stacked = jnp.concatenate([radiance[0], moment, normal[0], depth_sum], axis=0)
    count_block = counts.astype(jnp.float32)
    tile_rows = stacked.shape[1]
    tile_cols = stacked.shape[2]
    full_rows = tile_rows * lax.axis_size("ty")
    full_cols = tile_cols * lax.axis_size("tx")
    col_start = lax.axis_index("tx") * tile_cols
    totals, samples = lax.psum((stacked, count_block), "samp")
    row_start = lax.axis_index("ty") * tile_rows
    samples = jnp.repeat(jnp.repeat(samples[0], BLK, axis=0), BLK, axis=1)
    mean_values = totals / samples[None]
    colour = mean_values[0:3]
    second = mean_values[3]
    normals = mean_values[4:7]
    depth_map = mean_values[7]
    variance = jnp.maximum(second - jnp.square(luminance(colour)), 0.0)
    for level_idx in range(LEVELS):
        dilation = 2**level_idx
        rim_rows = 2 * dilation
        current = jnp.concatenate([colour, variance[None], normals, depth_map[None]], axis=0)
        padded = padded_2(current, (("ty", 1), ("tx", 2)), rim_rows)
        feature_now = padded[4:8]
        inside = inside_mask(
            row_start - rim_rows,
            col_start - rim_rows,
            tile_rows + 2 * rim_rows,
            tile_cols + 2 * rim_rows,
            full_rows,
            full_cols,
        )
        colour, variance = atrous_level(
            padded[0:3],
            padded[3],
            feature_now[0:3],
            feature_now[3],
            inside,
            dilation,
            tile_rows,
            tile_cols,
        )
    return (colour, variance)


def solution(mesh):
    placed = (
        P("samp", None, "ty", "tx"),
        P("samp", "ty", "tx"),
        P("samp", None, "ty", "tx"),
        P("samp", "ty", "tx"),
        P("samp", "ty", "tx"),
    )
    return jax.shard_map(
        per_device,
        mesh=mesh,
        in_specs=placed,
        out_specs=(P(None, "ty", "tx"), P("ty", "tx")),
        check_vma=False,
    )
```

profile of v0, /device:TPU:32, one launch (start us, length us, event | category | flops | bytes accessed | tf_op | source)
XLA Modules:
  0.0 196.9 jit_solution(225790759534100620)
XLA Ops:
  7.2 1.9 pad_maximum_fusion.16
  9.3 14.9 %psum.15 = f32[8,8]{1,0:T(8,128)S(1)} all-reduce(f32[8,8]{1,0:T(8,128)S(1)} %convert_bitcast_fusion), channel_id=1, replica_groups=mesh['samp'=8,'ty'=8,'tx'=4] {'samp'}, use_global_device_ids=true, to_apply=%region_1.0 | all-reduce | flops 64 | bytes 512 | tf_op jit(solution)/shard_map/psum | solution.py:86
  24.6 54.3 %all-reduce.2.cloned.1.call-done = f32[8,128,128]{2,1,0:T(8,128)} async-done(((f32[8,128,128]{2,1,0:T(8,128)}), f32[8,128,128]{2,1,0:T(8,128)}) %all-reduce.2.cloned.1.call-update) | async-done | bytes 524304 | tf_op jit(solution)/shard_map/psum | solution.py:86
  80.8 3.5 %collective-permute-start = (f32[8,2,128]{2,1,0:T(2,128)S(1)}, f32[8,2,128]{2,1,0:T(2,128)S(1)}, u32[]{:S(2)}, u32[]{:S(2)}) collective-permute-start(f32[8,2,128]{2,1,0:T(2,128)S(1)} %get-tuple-element.277), channel_id=1, source_target_pairs={{0,4},{4,8},{8,12},{12,16},{16,20},{20,24},{24,28},{1,5},{5,9},{9,... | collective-permute-start | bytes 24584 | tf_op jit(solution)/shard_map/ppermute | solution.py:24
  84.2 2.4 %collective-permute-start.1 = (f32[8,2,128]{2,1,0:T(2,128)S(1)}, f32[8,2,128]{2,1,0:T(2,128)S(1)}, u32[]{:S(2)}, u32[]{:S(2)}) collective-permute-start(f32[8,2,128]{2,1,0:T(2,128)S(1)} %get-tuple-element.278), channel_id=1, source_target_pairs={{4,0},{8,4},{12,8},{16,12},{20,16},{24,20},{28,24},{5,1},{9,5},{13... | collective-permute-start | bytes 24584 | tf_op jit(solution)/shard_map/ppermute | solution.py:25
  87.2 2.6 %collective-permute-done.1 = f32[8,2,128]{2,1,0:T(2,128)S(1)} collective-permute-done((f32[8,2,128]{2,1,0:T(2,128)S(1)}, f32[8,2,128]{2,1,0:T(2,128)S(1)}, u32[]{:S(2)}, u32[]{:S(2)}) %collective-permute-start.1) | collective-permute-done | bytes 8224 | tf_op jit(solution)/shard_map/ppermute | solution.py:25
  90.4 3.4 %collective-permute-start.2 = (f32[8,132,2]{1,0,2:T(8,128)S(1)}, f32[8,132,2]{1,0,2:T(8,128)S(1)}, u32[]{:S(2)}, u32[]{:S(2)}) collective-permute-start(f32[8,132,2]{1,0,2:T(8,128)S(1)} %copy.175), channel_id=1, source_target_pairs={{0,1},{1,2},{2,3},{4,5},{5,6},{6,7},{8,9},{9,10},{10,11},{12,13},{... | collective-permute-start | bytes 25352 | tf_op jit(solution)/shard_map/ppermute | solution.py:24
  95.8 4.1 %collective-permute-done.3 = f32[8,132,2]{1,0,2:T(8,128)} collective-permute-done((f32[8,132,2]{1,0,2:T(8,128)S(1)}, f32[8,132,2]{1,0,2:T(8,128)}, u32[]{:S(2)}, u32[]{:S(2)}) %collective-permute-start.3) | collective-permute-done | bytes 8480 | tf_op jit(solution)/shard_map/ppermute | solution.py:25
  107.3 4.2 %collective-permute-start.4 = (f32[8,4,128]{2,1,0:T(4,128)S(1)}, f32[8,4,128]{2,1,0:T(4,128)S(1)}, u32[]{:S(2)}, u32[]{:S(2)}) collective-permute-start(f32[8,4,128]{2,1,0:T(4,128)S(1)} %get-tuple-element.273), channel_id=1, source_target_pairs={{0,4},{4,8},{8,12},{12,16},{16,20},{20,24},{24,28},{1,5},{5,9},{9,... | collective-permute-start | bytes 49160 | tf_op jit(solution)/shard_map/ppermute | solution.py:24
  111.5 1.9 collective-permute-start.5
  113.6 4.8 %collective-permute-done.5 = f32[8,4,128]{2,1,0:T(4,128)S(1)} collective-permute-done((f32[8,4,128]{2,1,0:T(4,128)S(1)}, f32[8,4,128]{2,1,0:T(4,128)S(1)}, u32[]{:S(2)}, u32[]{:S(2)}) %collective-permute-start.5) | collective-permute-done | bytes 16416 | tf_op jit(solution)/shard_map/ppermute | solution.py:25
  119.0 3.4 %collective-permute-start.6 = (f32[8,136,4]{1,0,2:T(8,128)S(1)}, f32[8,136,4]{1,0,2:T(8,128)S(1)}, u32[]{:S(2)}, u32[]{:S(2)}) collective-permute-start(f32[8,136,4]{1,0,2:T(8,128)S(1)} %copy.181), channel_id=1, source_target_pairs={{0,1},{1,2},{2,3},{4,5},{5,6},{6,7},{8,9},{9,10},{10,11},{12,13},{... | collective-permute-start | bytes 52232 | tf_op jit(solution)/shard_map/ppermute | solution.py:24
  124.5 4.0 %collective-permute-done.7 = f32[8,136,4]{1,0,2:T(8,128)S(1)} collective-permute-done((f32[8,136,4]{1,0,2:T(8,128)S(1)}, f32[8,136,4]{1,0,2:T(8,128)S(1)}, u32[]{:S(2)}, u32[]{:S(2)}) %collective-permute-start.7) | collective-permute-done | bytes 17440 | tf_op jit(solution)/shard_map/ppermute | solution.py:25
  136.3 3.9 %collective-permute-start.8 = (f32[8,8,128]{2,1,0:T(8,128)S(1)}, f32[8,8,128]{2,1,0:T(8,128)S(1)}, u32[]{:S(2)}, u32[]{:S(2)}) collective-permute-start(f32[8,8,128]{2,1,0:T(8,128)S(1)} %get-tuple-element.269), channel_id=1, source_target_pairs={{0,4},{4,8},{8,12},{12,16},{16,20},{20,24},{24,28},{1,5},{5,9},{9,... | collective-permute-start | bytes 98312 | tf_op jit(solution)/shard_map/ppermute | solution.py:24
  140.2 1.9 collective-permute-start.9
  142.2 3.9 %collective-permute-done.9 = f32[8,8,128]{2,1,0:T(8,128)S(1)} collective-permute-done((f32[8,8,128]{2,1,0:T(8,128)S(1)}, f32[8,8,128]{2,1,0:T(8,128)S(1)}, u32[]{:S(2)}, u32[]{:S(2)}) %collective-permute-start.9) | collective-permute-done | bytes 32800 | tf_op jit(solution)/shard_map/ppermute | solution.py:25
  146.6 3.1 %collective-permute-start.10 = (f32[8,144,8]{1,2,0:T(8,128)S(1)}, f32[8,144,8]{1,2,0:T(8,128)S(1)}, u32[]{:S(2)}, u32[]{:S(2)}) collective-permute-start(f32[8,144,8]{1,2,0:T(8,128)S(1)} %copy.187), channel_id=1, source_target_pairs={{0,1},{1,2},{2,3},{4,5},{5,6},{6,7},{8,9},{9,10},{10,11},{12,13},{... | collective-permute-start | bytes 110600 | tf_op jit(solution)/shard_map/ppermute | solution.py:24
  151.8 4.3 %collective-permute-done.11 = f32[8,144,8]{1,2,0:T(8,128)S(1)} collective-permute-done((f32[8,144,8]{1,2,0:T(8,128)S(1)}, f32[8,144,8]{1,2,0:T(8,128)S(1)}, u32[]{:S(2)}, u32[]{:S(2)}) %collective-permute-start.11) | collective-permute-done | bytes 36896 | tf_op jit(solution)/shard_map/ppermute | solution.py:25
  163.2 3.1 %collective-permute-start.12 = (f32[8,16,128]{2,1,0:T(8,128)S(1)}, f32[8,16,128]{2,1,0:T(8,128)S(1)}, u32[]{:S(2)}, u32[]{:S(2)}) collective-permute-start(f32[8,16,128]{2,1,0:T(8,128)S(1)} %get-tuple-element.265), channel_id=1, source_target_pairs={{0,4},{4,8},{8,12},{12,16},{16,20},{20,24},{24,28},{1,5},{5,9},{9,... | collective-permute-start | bytes 196616 | tf_op jit(solution)/shard_map/ppermute | solution.py:24
  166.3 2.7 %collective-permute-start.13 = (f32[8,16,128]{2,1,0:T(8,128)S(1)}, f32[8,16,128]{2,1,0:T(8,128)S(1)}, u32[]{:S(2)}, u32[]{:S(2)}) collective-permute-start(f32[8,16,128]{2,1,0:T(8,128)S(1)} %get-tuple-element.266), channel_id=1, source_target_pairs={{4,0},{8,4},{12,8},{16,12},{20,16},{24,20},{28,24},{5,1},{9,5},{13... | collective-permute-start | bytes 196616 | tf_op jit(solution)/shard_map/ppermute | solution.py:25
  169.4 3.1 %collective-permute-done.13 = f32[8,16,128]{2,1,0:T(8,128)S(1)} collective-permute-done((f32[8,16,128]{2,1,0:T(8,128)S(1)}, f32[8,16,128]{2,1,0:T(8,128)S(1)}, u32[]{:S(2)}, u32[]{:S(2)}) %collective-permute-start.13) | collective-permute-done | bytes 65568 | tf_op jit(solution)/shard_map/ppermute | solution.py:25
  173.1 1.9 collective-permute-start.14
  178.0 4.3 %collective-permute-done.15 = f32[8,160,16]{1,2,0:T(8,128)} collective-permute-done((f32[8,160,16]{1,2,0:T(8,128)S(1)}, f32[8,160,16]{1,2,0:T(8,128)}, u32[]{:S(2)}, u32[]{:S(2)}) %collective-permute-start.15) | collective-permute-done | bytes 81952 | tf_op jit(solution)/shard_map/ppermute | solution.py:25
  185.7 2.7 %fusion.297 = (f32[128,128]{1,0:T(8,128)}, f32[128,128]{1,0:T(8,128)S(1)}, f32[128,128]{1,0:T(8,128)S(1)}, f32[128,128]{1,0:T(8,128)S(1)}, f32[128,128]{1,0:T(8,...) fusion(f32[160,160]{1,0:T(8,128)S(1)} %get-tuple-element.216, ...), kind=kLoop, calls=%fused_computation.549 | loop fusion | flops 8224768 | bytes 13172736 | tf_op jit(solution)/shard_map/div | solution.py:67
  (125 shorter events, 42.0 us)
Async XLA Ops:
  7.2 2.0 %copy-start.14 = (s32[1,8,8]{2,1,0:T(8,128)S(1)}, s32[1,8,8]{2,1,0:T(8,128)}, u32[]{:S(2)}) copy-start(s32[1,8,8]{2,1,0:T(8,128)} %param.9) | copy-start | bytes 772
  7.2 71.8 %all-reduce.2.cloned.1.call-start = ((), (), s32[]{:S(2)}) async-start(), calls=%async_computation | async-start | bytes 1048576 | tf_op jit(solution)/shard_map/psum | solution.py:86
  80.7 14.7 %copy-start.3 = (f32[1,128,128]{2,1,0:T(8,128)}, f32[1,128,128]{2,1,0:T(8,128)S(1)}, u32[]{:S(2)}) copy-start(f32[1,128,128]{2,1,0:T(8,128)S(1)} %get-tuple-element.213) | copy-start | bytes 196612
  80.8 6.4 %collective-permute-start = (f32[8,2,128]{2,1,0:T(2,128)S(1)}, f32[8,2,128]{2,1,0:T(2,128)S(1)}, u32[]{:S(2)}, u32[]{:S(2)}) collective-permute-start(f32[8,2,128]{2,1,0:T(2,128)S(1)} %get-tuple-element.277), channel_id=1, source_target_pairs={{0,4},{4,8},{8,12},{12,16},{16,20},{20,24},{24,28},{1,5},{5,9},{9,... | collective-permute-start | bytes 24584 | tf_op jit(solution)/shard_map/ppermute | solution.py:24
  84.2 5.5 %collective-permute-start.1 = (f32[8,2,128]{2,1,0:T(2,128)S(1)}, f32[8,2,128]{2,1,0:T(2,128)S(1)}, u32[]{:S(2)}, u32[]{:S(2)}) collective-permute-start(f32[8,2,128]{2,1,0:T(2,128)S(1)} %get-tuple-element.278), channel_id=1, source_target_pairs={{4,0},{8,4},{12,8},{16,12},{20,16},{24,20},{28,24},{5,1},{9,5},{13... | collective-permute-start | bytes 24584 | tf_op jit(solution)/shard_map/ppermute | solution.py:25
  87.2 8.2 %copy-start.8 = (f32[8,2,128]{2,1,0:T(2,128)}, f32[8,2,128]{2,1,0:T(2,128)S(1)}, u32[]{:S(2)}) copy-start(f32[8,2,128]{2,1,0:T(2,128)S(1)} %collective-permute-done) | copy-start | bytes 24580
  89.8 5.6 %copy-start.10 = (f32[8,2,128]{2,1,0:T(2,128)}, f32[8,2,128]{2,1,0:T(2,128)S(1)}, u32[]{:S(2)}) copy-start(f32[8,2,128]{2,1,0:T(2,128)S(1)} %collective-permute-done.1) | copy-start | bytes 24580
  90.4 5.1 %collective-permute-start.2 = (f32[8,132,2]{1,0,2:T(8,128)S(1)}, f32[8,132,2]{1,0,2:T(8,128)S(1)}, u32[]{:S(2)}, u32[]{:S(2)}) collective-permute-start(f32[8,132,2]{1,0,2:T(8,128)S(1)} %copy.175), channel_id=1, source_target_pairs={{0,1},{1,2},{2,3},{4,5},{5,6},{6,7},{8,9},{9,10},{10,11},{12,13},{... | collective-permute-start | bytes 25352 | tf_op jit(solution)/shard_map/ppermute | solution.py:24
  94.1 5.7 %collective-permute-start.3 = (f32[8,132,2]{1,0,2:T(8,128)S(1)}, f32[8,132,2]{1,0,2:T(8,128)}, u32[]{:S(2)}, u32[]{:S(2)}) collective-permute-start(f32[8,132,2]{1,0,2:T(8,128)S(1)} %copy.176), channel_id=1, source_target_pairs={{1,0},{2,1},{3,2},{5,4},{6,5},{7,6},{9,8},{10,9},{11,10},{13,12},{... | collective-permute-start | bytes 25352 | tf_op jit(solution)/shard_map/ppermute | solution.py:25
  102.5 1.1 copy-start.5
  106.4 7.1 %copy-start.12 = (f32[136]{0:T(256)S(1)}, f32[136]{0:T(256)}, u32[]{:S(2)}) copy-start(f32[136]{0:T(256)} %get-tuple-element.281) | copy-start | bytes 1636
  106.4 7.1 %copy-start.13 = (f32[136]{0:T(256)S(1)}, f32[136]{0:T(256)}, u32[]{:S(2)}) copy-start(f32[136]{0:T(256)} %get-tuple-element.282) | copy-start | bytes 1636
  107.3 6.3 %collective-permute-start.4 = (f32[8,4,128]{2,1,0:T(4,128)S(1)}, f32[8,4,128]{2,1,0:T(4,128)S(1)}, u32[]{:S(2)}, u32[]{:S(2)}) collective-permute-start(f32[8,4,128]{2,1,0:T(4,128)S(1)} %get-tuple-element.273), channel_id=1, source_target_pairs={{0,4},{4,8},{8,12},{12,16},{16,20},{20,24},{24,28},{1,5},{5,9},{9,... | collective-permute-start | bytes 49160 | tf_op jit(solution)/shard_map/ppermute | solution.py:24
  111.5 6.8 %collective-permute-start.5 = (f32[8,4,128]{2,1,0:T(4,128)S(1)}, f32[8,4,128]{2,1,0:T(4,128)S(1)}, u32[]{:S(2)}, u32[]{:S(2)}) collective-permute-start(f32[8,4,128]{2,1,0:T(4,128)S(1)} %get-tuple-element.274), channel_id=1, source_target_pairs={{4,0},{8,4},{12,8},{16,12},{20,16},{24,20},{28,24},{5,1},{9,5},{13... | collective-permute-start | bytes 49160 | tf_op jit(solution)/shard_map/ppermute | solution.py:25
  119.0 5.3 %collective-permute-start.6 = (f32[8,136,4]{1,0,2:T(8,128)S(1)}, f32[8,136,4]{1,0,2:T(8,128)S(1)}, u32[]{:S(2)}, u32[]{:S(2)}) collective-permute-start(f32[8,136,4]{1,0,2:T(8,128)S(1)} %copy.181), channel_id=1, source_target_pairs={{0,1},{1,2},{2,3},{4,5},{5,6},{6,7},{8,9},{9,10},{10,11},{12,13},{... | collective-permute-start | bytes 52232 | tf_op jit(solution)/shard_map/ppermute | solution.py:24
  122.7 5.8 %collective-permute-start.7 = (f32[8,136,4]{1,0,2:T(8,128)S(1)}, f32[8,136,4]{1,0,2:T(8,128)S(1)}, u32[]{:S(2)}, u32[]{:S(2)}) collective-permute-start(f32[8,136,4]{1,0,2:T(8,128)S(1)} %copy.182), channel_id=1, source_target_pairs={{1,0},{2,1},{3,2},{5,4},{6,5},{7,6},{9,8},{10,9},{11,10},{13,12},{... | collective-permute-start | bytes 52232 | tf_op jit(solution)/shard_map/ppermute | solution.py:25
  136.3 5.9 %collective-permute-start.8 = (f32[8,8,128]{2,1,0:T(8,128)S(1)}, f32[8,8,128]{2,1,0:T(8,128)S(1)}, u32[]{:S(2)}, u32[]{:S(2)}) collective-permute-start(f32[8,8,128]{2,1,0:T(8,128)S(1)} %get-tuple-element.269), channel_id=1, source_target_pairs={{0,4},{4,8},{8,12},{12,16},{16,20},{20,24},{24,28},{1,5},{5,9},{9,... | collective-permute-start | bytes 98312 | tf_op jit(solution)/shard_map/ppermute | solution.py:24
  140.2 5.8 %collective-permute-start.9 = (f32[8,8,128]{2,1,0:T(8,128)S(1)}, f32[8,8,128]{2,1,0:T(8,128)S(1)}, u32[]{:S(2)}, u32[]{:S(2)}) collective-permute-start(f32[8,8,128]{2,1,0:T(8,128)S(1)} %get-tuple-element.270), channel_id=1, source_target_pairs={{4,0},{8,4},{12,8},{16,12},{20,16},{24,20},{28,24},{5,1},{9,5},{13... | collective-permute-start | bytes 98312 | tf_op jit(solution)/shard_map/ppermute | solution.py:25
  146.6 5.0 %collective-permute-start.10 = (f32[8,144,8]{1,2,0:T(8,128)S(1)}, f32[8,144,8]{1,2,0:T(8,128)S(1)}, u32[]{:S(2)}, u32[]{:S(2)}) collective-permute-start(f32[8,144,8]{1,2,0:T(8,128)S(1)} %copy.187), channel_id=1, source_target_pairs={{0,1},{1,2},{2,3},{4,5},{5,6},{6,7},{8,9},{9,10},{10,11},{12,13},{... | collective-permute-start | bytes 110600 | tf_op jit(solution)/shard_map/ppermute | solution.py:24
  150.0 6.2 %collective-permute-start.11 = (f32[8,144,8]{1,2,0:T(8,128)S(1)}, f32[8,144,8]{1,2,0:T(8,128)S(1)}, u32[]{:S(2)}, u32[]{:S(2)}) collective-permute-start(f32[8,144,8]{1,2,0:T(8,128)S(1)} %copy.188), channel_id=1, source_target_pairs={{1,0},{2,1},{3,2},{5,4},{6,5},{7,6},{9,8},{10,9},{11,10},{13,12},{... | collective-permute-start | bytes 110600 | tf_op jit(solution)/shard_map/ppermute | solution.py:25
  163.2 6.2 %collective-permute-start.12 = (f32[8,16,128]{2,1,0:T(8,128)S(1)}, f32[8,16,128]{2,1,0:T(8,128)S(1)}, u32[]{:S(2)}, u32[]{:S(2)}) collective-permute-start(f32[8,16,128]{2,1,0:T(8,128)S(1)} %get-tuple-element.265), channel_id=1, source_target_pairs={{0,4},{4,8},{8,12},{12,16},{16,20},{20,24},{24,28},{1,5},{5,9},{9,... | collective-permute-start | bytes 196616 | tf_op jit(solution)/shard_map/ppermute | solution.py:24
  166.3 6.2 %collective-permute-start.13 = (f32[8,16,128]{2,1,0:T(8,128)S(1)}, f32[8,16,128]{2,1,0:T(8,128)S(1)}, u32[]{:S(2)}, u32[]{:S(2)}) collective-permute-start(f32[8,16,128]{2,1,0:T(8,128)S(1)} %get-tuple-element.266), channel_id=1, source_target_pairs={{4,0},{8,4},{12,8},{16,12},{20,16},{24,20},{28,24},{5,1},{9,5},{13... | collective-permute-start | bytes 196616 | tf_op jit(solution)/shard_map/ppermute | solution.py:25
  173.1 4.6 %collective-permute-start.14 = (f32[8,160,16]{1,2,0:T(8,128)S(1)}, f32[8,160,16]{1,2,0:T(8,128)S(1)}, u32[]{:S(2)}, u32[]{:S(2)}) collective-permute-start(f32[8,160,16]{1,2,0:T(8,128)S(1)} %copy.193), channel_id=1, source_target_pairs={{0,1},{1,2},{2,3},{4,5},{5,6},{6,7},{8,9},{9,10},{10,11},{12,13},{... | collective-permute-start | bytes 245768 | tf_op jit(solution)/shard_map/ppermute | solution.py:24
  175.3 7.0 %collective-permute-start.15 = (f32[8,160,16]{1,2,0:T(8,128)S(1)}, f32[8,160,16]{1,2,0:T(8,128)}, u32[]{:S(2)}, u32[]{:S(2)}) collective-permute-start(f32[8,160,16]{1,2,0:T(8,128)S(1)} %copy.194), channel_id=1, source_target_pairs={{1,0},{2,1},{3,2},{5,4},{6,5},{7,6},{9,8},{10,9},{11,10},{13,12},{... | collective-permute-start | bytes 245768 | tf_op jit(solution)/shard_map/ppermute | solution.py:25
  (8 other events, 7.4 us)
Sparse Core Ops, SparseCore 0:
  10.3 68.5 all-reduce.1
where the time goes:
time: 198 us; the launch traced here: 197 us
  waiting for transfers between devices  85.8 us (43%)
  starting transfers between devices  41 us (21%)
  other arithmetic  28.4 us (14%)
  blocking collectives  14.9 us (8%)
  between operations  14.7 us (7%)
  local copies, waits for them, and re-layouts  12.1 us (6%)
    psum x1, waiting for transfers between devices, per_device(): totals, samples = lax.psum((stacked, count_block), 'samp')  54.3 us
    ppermute x8, waiting for transfers between devices, padded_2(): after = lax.ppermute(first, axis, down)  31 us
    ppermute x8, starting transfers between devices, padded_2(): before = lax.ppermute(last, axis, up)  26.5 us
    psum x1, blocking collectives, per_device(): totals, samples = lax.psum((stacked, count_block), 'samp')  14.9 us
    ppermute x8, starting transfers between devices, padded_2(): after = lax.ppermute(first, axis, down)  14.5 us
    div x5, other arithmetic, atrous_level(): return (colour_acc / weight_sum[None], var_acc / (weight_sum * weight_sum))  6.87 us
    concatenate x12, other arithmetic, padded_2(): value = jnp.concatenate([before, value, after], axis=dim)  5.99 us
    add x4, other arithmetic, atrous_level(): weight_sum = weight_sum + weight  5.03 us
  transfers between devices with their start and end apart: 17, of which 11 were waited for; matrix products, arithmetic and copies ran while one was open for 2% of the time, Pallas kernels for 0%

commit v1 on v0

v1 whole, which is shorter than its diff:
```python
import functools

import jax
import jax.numpy as jnp
from jax import lax
from jax.experimental import pallas as pl
from jax.experimental.pallas import tpu as pltpu
from jax.sharding import PartitionSpec as P

TAPS = (0.0625, 0.25, 0.375, 0.25, 0.0625)
LUMA = (0.2126, 0.7152, 0.0722)
SIGMA_DEPTH = 0.5
SIGMA_NORMAL = 1.0
SIGMA_LUMA = 4.0
LUMA_FLOOR = 0.5
FAR = 1e30

TILE = 128
HALF = 64
RIM = 32
WIN = 96
BLK = 16
AXES = ("samp", "ty", "tx")


def place():
    samp = lax.axis_index("samp")
    ty = lax.axis_index("ty")
    tx = lax.axis_index("tx")
    core = lax.rem(samp, 2)
    y = samp // 2
    half_row = lax.rem(y // 2 + ty, 2)
    half_col = lax.rem(lax.rem(y, 2) + tx, 2)
    return core, half_row, half_col, ty, tx


def luminance(c0, c1, c2):
    return LUMA[0] * c0 + LUMA[1] * c1 + LUMA[2] * c2


def rows(start, count):
    return pl.ds(start, count)


def aligned(value):
    return pl.multiple_of(value, 8)


def pack_kernel(rad, mom, nor, dep, cnt, keep, send):
    core = place()[0]

    def fill(colour_ref, normal_ref):
        for ch in range(3):
            colour_ref[ch * TILE : (ch + 1) * TILE, :] = rad[0, ch]
            normal_ref[ch * TILE : (ch + 1) * TILE, :] = nor[0, ch]
        colour_ref[3 * TILE : 4 * TILE, :] = mom[0]
        normal_ref[3 * TILE : 4 * TILE, :] = dep[0]

    @pl.when(core == 0)
    def _():
        fill(keep, send)

    @pl.when(core == 1)
    def _():
        fill(send, keep)

    blocks = cnt[0].astype(jnp.float32)
    for ref in (keep, send):
        ref[4 * TILE :, :] = jnp.zeros((8, TILE), jnp.float32)
        ref[4 * TILE :, 0:8] = blocks


def pair_kernel(keep, recv, near, far):
    half_row = place()[1]
    for ref, part in ((near, half_row), (far, 1 - half_row)):
        for ch in range(4):
            at = rows(aligned(ch * TILE + 32 * part), WIN)
            ref[ch * WIN : (ch + 1) * WIN, :] = keep[at, :] + recv[at, :]
        ref[4 * WIN :, :] = keep[4 * TILE :, :] + recv[4 * TILE :, :]


def mean_kernel(own, r1, r2, r3, field, rim_x, rim_z, rim_d, samples):
    core, half_row, half_col, _, _ = place()
    lane = lax.broadcasted_iota(jnp.int32, (8, TILE), 1)

    def total(at):
        return (own[at, :] + r1[at, :]) + (r2[at, :] + r3[at, :])

    blocks = total(rows(4 * WIN, 8))
    spread = jnp.zeros((8, TILE), jnp.float32)
    for j in range(8):
        spread = jnp.where(lane // BLK == j, blocks[:, j : j + 1], spread)
    samples[...] = spread
    for i in range(WIN // BLK):
        count = jnp.broadcast_to(samples[rows(2 * half_row + i, 1), :], (BLK, TILE))
        mean = [total(rows(ch * WIN + i * BLK, BLK)) / count for ch in range(4)]
        variance = jnp.maximum(mean[3] - jnp.square(luminance(*mean[:3])), 0.0)
        mean[3] = jnp.where(core == 0, variance, mean[3])
        for ch in range(4):
            field[rows(ch * WIN + i * BLK, BLK), :] = mean[ch]
        lanes = lax.broadcasted_iota(jnp.int32, (BLK, TILE), 1)
        packed = jnp.zeros((BLK, TILE), jnp.float32)
        for ch in range(4):
            moved = pltpu.roll(mean[ch], lax.rem(32 * ch + TILE - 96 * half_col, TILE), 1)
            packed = jnp.where(lanes // 32 == ch, moved, packed)
        rim_x[rows(i * BLK, BLK), :] = packed
    first = aligned(64 * half_row)
    for ch in range(4):
        rim_z[ch * RIM : (ch + 1) * RIM, :] = field[rows(aligned(ch * WIN + first), RIM), :]
    rim_d[...] = rim_x[rows(first, RIM), :]


NF = 9
PAD = 32


def filter_kernel(*refs):
    (f0, x0, z0, d0, f1, x1, z1, d1, out, cur, geo, shifted) = refs
    core, half_row, half_col, ty, tx = place()
    lanes = lax.broadcasted_iota(jnp.int32, (RIM, TILE), 1)
    n_ty, n_tx = lax.axis_size("ty"), lax.axis_size("tx")
    x_out = ((half_col == 0) & (tx == 0)) | ((half_col == 1) & (tx == n_tx - 1))
    z_out = ((half_row == 0) & (ty == 0)) | ((half_row == 1) & (ty == n_ty - 1))
    rim_lane = (lanes // 32) == 3 * half_col
    into = jnp.where(half_col == 0, 32, 96)
    rim_at = 96 * half_col

    def cell(body, rim, ch):
        return jnp.where(
            rim_lane,
            pltpu.roll(rim, lax.rem(rim_at + TILE - 32 * ch, TILE), 1),
            pltpu.roll(body, into, 1),
        )

    body_row = PAD + 32 * (1 - half_row) - 32 * core
    edge_row = PAD + 96 * half_row - 32 * core

    def assemble(is_geo, f, x, z, d):
        for ch in range(4):
            for part in range(4):
                if part < 3:
                    value = cell(
                        f[ch * WIN + part * RIM : ch * WIN + (part + 1) * RIM, :],
                        x[part * RIM : (part + 1) * RIM, :],
                        ch,
                    )
                    at = rows(aligned(body_row + part * RIM), RIM)
                else:
                    value = cell(z[ch * RIM : (ch + 1) * RIM, :], d[...], ch)
                    at = rows(aligned(edge_row), RIM)
                if is_geo:
                    if ch == 3:
                        value = value * (1.0 / SIGMA_DEPTH)
                        outside = rim_lane & x_out
                        if part == 3:
                            outside = outside | z_out
                        value = jnp.where(outside, FAR, value)
                    geo[ch, at, :] = value
                else:
                    cur[0, ch, at, :] = value

    @pl.when(core == 0)
    def _():
        assemble(False, f0, x0, z0, d0)
        assemble(True, f1, x1, z1, d1)

    @pl.when(core == 1)
    def _():
        assemble(True, f0, x0, z0, d0)
        assemble(False, f1, x1, z1, d1)

    def add_luma(i, carry):
        at = rows(aligned(i * 8), 8)
        cur[0, 4, at, :] = luminance(cur[0, 0, at, :], cur[0, 1, at, :], cur[0, 2, at, :])
        return carry

    lax.fori_loop(0, (WIN + 2 * PAD) // 8, add_luma, 0)

    for level, (low, high) in enumerate(((0, 96), (8, 88), (16, 80), (32, 64))):
        dil = 2**level
        src, dst = level % 2, 1 - level % 2
        reach = -(-2 * dil // 8) * 8
        start, stop = PAD + low - reach, PAD + high + reach

        def shift(i, carry, src=src, start=start, dil=dil):
            at = rows(aligned(start + i * 8), 8)
            for f in range(NF):
                value = geo[f, at, :] if f < 4 else cur[src, f - 4, at, :]
                for b in range(5):
                    moved = value if b == 2 else pltpu.roll(value, (-(b - 2) * dil) % TILE, 1)
                    shifted[b, f, at, :] = moved
            return carry

        lax.fori_loop(0, (stop - start) // 8, shift, 0)

        def step(i, carry, src=src, dst=dst, low=low, dil=dil, level=level):
            base = PAD + low + i * 8
            here = rows(aligned(base), 8)
            n0, n1, n2, depth = (geo[f, here, :] for f in range(4))
            luma = cur[src, 4, here, :]
            slope = -1.0 / (SIGMA_LUMA * jnp.sqrt(cur[src, 3, here, :]) + LUMA_FLOOR)
            total = c0 = c1 = c2 = var = None
            for a in range(5):
                for b in range(5):
                    at = rows(base + (a - 2) * dil, 8)
                    tap = [shifted[b, f, at, :] for f in range(NF)]
                    e = jnp.abs(tap[8] - luma) * slope - jnp.abs(tap[3] - depth)
                    e = e - jnp.square(tap[0] - n0) - jnp.square(tap[1] - n1)
                    e = e - jnp.square(tap[2] - n2)
                    w = (TAPS[a] * TAPS[b]) * jnp.exp(e)
                    parts = (w, w * tap[4], w * tap[5], w * tap[6], w * w * tap[7])
                    if total is None:
                        total, c0, c1, c2, var = parts
                    else:
                        total, c0, c1, c2, var = (
                            p + q for p, q in zip((total, c0, c1, c2, var), parts)
                        )
            inv = 1.0 / total
            c0, c1, c2, var = c0 * inv, c1 * inv, c2 * inv, var * (inv * inv)
            if level < 3:
                for f, value in enumerate((c0, c1, c2, var, luminance(c0, c1, c2))):
                    cur[dst, f, here, :] = value
            else:
                lane = lax.broadcasted_iota(jnp.int32, (8, TILE), 1)
                for k, (p, q) in enumerate(((c0, c1), (c2, var))):
                    out[rows(aligned(k * 32 + i * 8), 8), :] = jnp.where(
                        lane < HALF, pltpu.roll(p, TILE - 32, 1), pltpu.roll(q, 32, 1)
                    )
            return carry

        lax.fori_loop(0, (high - low) // 8, step, 0)


def tile_kernel(*refs):
    ins, colour, variance = refs[:8], refs[8], refs[9]
    core, half_row, half_col, _, _ = place()
    lane = lax.broadcasted_iota(jnp.int32, (32, TILE), 1)
    low = lane < HALF
    for side in range(2):
        which = core if side == 0 else 1 - core
        for r in range(2):
            row = aligned(64 * (half_row if r == 0 else 1 - half_row) + 32 * which)
            near, other = ins[side * 4 + 2 * r], ins[side * 4 + 2 * r + 1]
            for k in range(2):
                p, q = near[k * 32 : (k + 1) * 32, :], other[k * 32 : (k + 1) * 32, :]
                left = jnp.where(half_col == 0, p, q)
                right = jnp.where(half_col == 0, q, p)
                first = jnp.where(low, left, pltpu.roll(right, HALF, 1))
                second = jnp.where(low, pltpu.roll(left, HALF, 1), right)
                at = rows(row, 32)
                colour[2 * k, at, :] = first
                if k == 0:
                    colour[1, at, :] = second
                else:
                    variance[at, :] = second


def call(kernel, shapes, scratch=()):
    return pl.pallas_call(
        kernel,
        out_shape=[jax.ShapeDtypeStruct(s, jnp.float32) for s in shapes],
        scratch_shapes=list(scratch),
        compiler_params=pltpu.CompilerParams(vmem_limit_bytes=24 * 2**20),
    )


def pairs(sizes, partner):
    n_samp, n_ty, n_tx = sizes
    out = []
    for samp in range(n_samp):
        for ty in range(n_ty):
            for tx in range(n_tx):
                to = partner(samp, ty, tx)
                if 0 <= to[1] < n_ty and 0 <= to[2] < n_tx:
                    out.append(
                        ((samp * n_ty + ty) * n_tx + tx, (to[0] * n_ty + to[1]) * n_tx + to[2])
                    )
    return out


def step_of(samp, ty, tx):
    y = samp // 2
    row = 1 if (y // 2 + ty) % 2 else -1
    col = 1 if (y % 2 + tx) % 2 else -1
    return row, col


def per_device(sizes, radiance, moment, normal, depth_sum, counts):
    def send(value, partner):
        return lax.ppermute(value, AXES, pairs(sizes, partner))

    def other_core(value):
        return send(value, lambda s, ty, tx: (s ^ 1, ty, tx))

    def other_y(value, k):
        return send(value, lambda s, ty, tx: (s ^ (2 * k), ty, tx))

    packed = (4 * TILE + 8, TILE)
    window = (4 * WIN + 8, TILE)
    keep, give = call(pack_kernel, [packed, packed])(radiance, moment, normal, depth_sum, counts)
    near, far = call(pair_kernel, [window, window])(keep, other_core(give))
    r1, r2, r3 = other_y(near, 1), other_y(far, 2), other_y(far, 3)
    field, rim_x, rim_z, rim_d = call(
        mean_kernel,
        [(4 * WIN, TILE), (WIN, TILE), (4 * RIM, TILE), (RIM, TILE)],
        [pltpu.VMEM((8, TILE), jnp.float32)],
    )(near, r1, r2, r3)
    field_1 = other_core(field)
    rim_x = send(rim_x, lambda s, ty, tx: (s, ty, tx + step_of(s, ty, tx)[1]))
    rim_z = send(rim_z, lambda s, ty, tx: (s, ty + step_of(s, ty, tx)[0], tx))
    rim_d = send(
        rim_d, lambda s, ty, tx: (s, ty + step_of(s, ty, tx)[0], tx + step_of(s, ty, tx)[1])
    )
    rims = (rim_x, rim_z, rim_d)
    rims_1 = [other_core(r) for r in rims]
    (mine,) = call(
        filter_kernel,
        [(HALF, TILE)],
        [
            pltpu.VMEM((2, 5, WIN + 2 * PAD, TILE), jnp.float32),
            pltpu.VMEM((4, WIN + 2 * PAD, TILE), jnp.float32),
            pltpu.VMEM((5, NF, WIN + 2 * PAD, TILE), jnp.float32),
        ],
    )(field, *rims, field_1, *rims_1)
    got = [mine] + [other_y(mine, k) for k in (1, 2, 3)]
    theirs = [other_core(g) for g in got]
    return tuple(call(tile_kernel, [(3, TILE, TILE), (TILE, TILE)])(*got, *theirs))


def solution(mesh):
    sizes = tuple(mesh.shape[axis] for axis in AXES)
    placed = (
        P("samp", None, "ty", "tx"),
        P("samp", "ty", "tx"),
        P("samp", None, "ty", "tx"),
        P("samp", "ty", "tx"),
        P("samp", "ty", "tx"),
    )
    return jax.shard_map(
        functools.partial(per_device, sizes),
        mesh=mesh,
        in_specs=placed,
        out_specs=(P(None, "ty", "tx"), P("ty", "tx")),
        check_vma=False,
    )
```

time: 198 us -> 59.8 us (0.30)
  the two profiles are of different devices: /device:TPU:32 before, /device:TPU:1 now
where the time goes in v1:
time: 59.8 us; the launch traced here: 59.4 us
  starting transfers between devices  30.3 us (51%)
  waiting for transfers between devices  13.2 us (22%)
  Pallas kernels  11 us (18%)
  local copies, waits for them, and re-layouts  4.21 us (7%)
  between operations  0.73 us (1%)
    ppermute x18, starting transfers between devices, send(): return lax.ppermute(value, AXES, pairs(sizes, partner))  30.3 us
    ppermute x18, waiting for transfers between devices, send(): return lax.ppermute(value, AXES, pairs(sizes, partner))  13.2 us
    pallas_call x1, Pallas kernels, per_device(): call(filter_kernel, [(HALF, TILE)], [pltpu.VMEM((2, 5, WIN + 2 * PAD, TIL...  9.86 us
    unnamed x10, local copies, waits for them, and re-layouts  4.21 us
  transfers between devices with their start and end apart: 18, of which 8 were waited for; matrix products, arithmetic and copies ran while one was open for 0% of the time, Pallas kernels for 0%

profile of v1, /device:TPU:1, one launch (start us, length us, event | category | flops | bytes accessed | tf_op | source)
XLA Modules:
  0.0 59.4 jit_solution(8158091359511962452)
XLA Ops:
  0.6 0.9 %copy-done = f32[1,3,128,128]{3,2,1,0:T(8,128)S(1)} copy-done((f32[1,3,128,128]{3,2,1,0:T(8,128)S(1)}, f32[1,3,128,128]{3,2,1,0:T(8,128)}, u32[]{:S(2)}) %copy-start) | copy-done | bytes 196632
  1.6 0.9 %copy-done.1 = f32[1,3,128,128]{3,2,1,0:T(8,128)S(1)} copy-done((f32[1,3,128,128]{3,2,1,0:T(8,128)S(1)}, f32[1,3,128,128]{3,2,1,0:T(8,128)}, u32[]{:S(2)}) %copy-start.1) | copy-done | bytes 196632
  2.5 0.8 %copy-done.2 = f32[1,128,128]{2,1,0:T(8,128)S(1)} copy-done((f32[1,128,128]{2,1,0:T(8,128)S(1)}, f32[1,128,128]{2,1,0:T(8,128)}, u32[]{:S(2)}) %copy-start.2) | copy-done | bytes 65560
  3.3 0.8 %copy-done.3 = f32[1,128,128]{2,1,0:T(8,128)S(1)} copy-done((f32[1,128,128]{2,1,0:T(8,128)S(1)}, f32[1,128,128]{2,1,0:T(8,128)}, u32[]{:S(2)}) %copy-start.3) | copy-done | bytes 65560
  4.2 0.7 %copy-done.4 = s32[1,8,8]{2,1,0:T(8,128)S(1)} copy-done((s32[1,8,8]{2,1,0:T(8,128)S(1)}, s32[1,8,8]{2,1,0:T(8,128)}, u32[]{:S(2)}) %copy-start.4) | copy-done | bytes 280
  4.9 3.3 %collective-permute-start = (f32[520,128]{1,0:T(8,128)S(1)}, f32[520,128]{1,0:T(8,128)S(1)}, u32[]{:S(2)}, u32[]{:S(2)}) collective-permute-start(f32[520,128]{1,0:T(8,128)S(1)} %get-tuple-element.11), channel_id=1, source_target_pairs={{0,32},{1,33},{2,34},{3,35},{4,36},{5,37},{6,38},{7,39},{8,40},{9,... | collective-permute-start | bytes 798728 | tf_op jit(solution)/shard_map/ppermute | solution.py:290
  8.2 1.2 %collective-permute-done.recv = f32[520,128]{1,0:T(8,128)S(1)} collective-permute-done((f32[520,128]{1,0:T(8,128)S(1)}, f32[520,128]{1,0:T(8,128)S(1)}, u32[]{:S(2)}, u32[]{:S(2)}) %collective-permute-start) | collective-permute-done | bytes 266272 | tf_op jit(solution)/shard_map/ppermute | solution.py:290
  9.6 1.4 %collective-permute-start.3 = (f32[392,128]{1,0:T(8,128)S(1)}, f32[392,128]{1,0:T(8,128)S(1)}, u32[]{:S(2)}, u32[]{:S(2)}) collective-permute-start(f32[392,128]{1,0:T(8,128)S(1)} %get-tuple-element.13), channel_id=1, source_target_pairs={{0,192},{1,193},{2,194},{3,195},{4,196},{5,197},{6,198},{7,199},{8... | collective-permute-start | bytes 602120 | tf_op jit(solution)/shard_map/ppermute | solution.py:290
  11.0 1.8 %collective-permute-start.2 = (f32[392,128]{1,0:T(8,128)S(1)}, f32[392,128]{1,0:T(8,128)S(1)}, u32[]{:S(2)}, u32[]{:S(2)}) collective-permute-start(f32[392,128]{1,0:T(8,128)S(1)} %get-tuple-element.13), channel_id=1, source_target_pairs={{0,128},{1,129},{2,130},{3,131},{4,132},{5,133},{6,134},{7,135},{8... | collective-permute-start | bytes 602120 | tf_op jit(solution)/shard_map/ppermute | solution.py:290
  12.8 2.9 %collective-permute-done.1.r1 = f32[392,128]{1,0:T(8,128)S(1)} collective-permute-done((f32[392,128]{1,0:T(8,128)S(1)}, f32[392,128]{1,0:T(8,128)S(1)}, u32[]{:S(2)}, u32[]{:S(2)}) %collective-permute-start.1) | collective-permute-done | bytes 200736 | tf_op jit(solution)/shard_map/ppermute | solution.py:290
  15.7 1.9 %collective-permute-done.3.r3 = f32[392,128]{1,0:T(8,128)S(1)} collective-permute-done((f32[392,128]{1,0:T(8,128)S(1)}, f32[392,128]{1,0:T(8,128)S(1)}, u32[]{:S(2)}, u32[]{:S(2)}) %collective-permute-start.3) | collective-permute-done | bytes 200736 | tf_op jit(solution)/shard_map/ppermute | solution.py:290
  17.6 3.2 %collective-permute-done.2.r2 = f32[392,128]{1,0:T(8,128)S(1)} collective-permute-done((f32[392,128]{1,0:T(8,128)S(1)}, f32[392,128]{1,0:T(8,128)S(1)}, u32[]{:S(2)}, u32[]{:S(2)}) %collective-permute-start.2) | collective-permute-done | bytes 200736 | tf_op jit(solution)/shard_map/ppermute | solution.py:290
  21.0 1.8 %collective-permute-start.7 = (f32[384,128]{1,0:T(8,128)S(1)}, f32[384,128]{1,0:T(8,128)S(1)}, u32[]{:S(2)}, u32[]{:S(2)}) collective-permute-start(f32[384,128]{1,0:T(8,128)S(1)} %get-tuple-element.14.refs_0_), channel_id=1, source_target_pairs={{0,32},{1,33},{2,34},{3,35},{4,36},{5,37},{6,38},{7,39},{8,40},{9,... | collective-permute-start | bytes 589832 | tf_op jit(solution)/shard_map/ppermute | solution.py:290
  23.5 0.7 %collective-permute-start.4 = (f32[96,128]{1,0:T(8,128)S(1)}, f32[96,128]{1,0:T(8,128)S(1)}, u32[]{:S(2)}, u32[]{:S(2)}) collective-permute-start(f32[96,128]{1,0:T(8,128)S(1)} %get-tuple-element.15), channel_id=1, source_target_pairs={{1,2},{2,1},{5,6},{6,5},{9,10},{10,9},{13,14},{14,13},{17,18},{18,... | collective-permute-start | bytes 147464 | tf_op jit(solution)/shard_map/ppermute | solution.py:290
  25.7 1.1 %collective-permute-done.10.refs_7_ = f32[32,128]{1,0:T(8,128)S(1)} collective-permute-done((f32[32,128]{1,0:T(8,128)S(1)}, f32[32,128]{1,0:T(8,128)S(1)}, u32[]{:S(2)}, u32[]{:S(2)}) %collective-permute-start.10) | collective-permute-done | bytes 16416 | tf_op jit(solution)/shard_map/ppermute | solution.py:290
  26.8 9.9 %shard_map.71.refs_0_ = f32[64,128]{1,0:T(8,128)S(1)} custom-call(f32[384,128]{1,0:T(8,128)S(1)} %get-tuple-element.14.refs_0_, f32[96,128]{1,0:T(8,128)S(1)} %collective-permute-done.4.refs_1_, f32[128,128]{1,0:T(8,128)S(1)} %collective-permute-done.5.refs_2_, f32[32,128]{1,0:T(8,128)S(1)} %collective-permute-done.6.refs_3_, ...), custom_call_target="tpu_custom_call" | custom-call | tf_op jit(solution)/shard_map/pallas_call | solution.py:316
  36.6 14.7 %collective-permute-start.13 = (f32[64,128]{1,0:T(8,128)S(1)}, f32[64,128]{1,0:T(8,128)S(1)}, u32[]{:S(2)}, u32[]{:S(2)}) collective-permute-start(f32[64,128]{1,0:T(8,128)S(1)} %shard_map.71.refs_0_), channel_id=1, source_target_pairs={{0,192},{1,193},{2,194},{3,195},{4,196},{5,197},{6,198},{7,199},{8... | collective-permute-start | bytes 98312 | tf_op jit(solution)/shard_map/ppermute | solution.py:290
  51.4 0.7 %collective-permute-start.11 = (f32[64,128]{1,0:T(8,128)S(1)}, f32[64,128]{1,0:T(8,128)S(1)}, u32[]{:S(2)}, u32[]{:S(2)}) collective-permute-start(f32[64,128]{1,0:T(8,128)S(1)} %shard_map.71.refs_0_), channel_id=1, source_target_pairs={{0,64},{1,65},{2,66},{3,67},{4,68},{5,69},{6,70},{7,71},{8,72},{9,... | collective-permute-start | bytes 98312 | tf_op jit(solution)/shard_map/ppermute | solution.py:290
  52.0 0.9 %collective-permute-start.14 = (f32[64,128]{1,0:T(8,128)S(1)}, f32[64,128]{1,0:T(8,128)S(1)}, u32[]{:S(2)}, u32[]{:S(2)}) collective-permute-start(f32[64,128]{1,0:T(8,128)S(1)} %shard_map.71.refs_0_), channel_id=1, source_target_pairs={{0,32},{1,33},{2,34},{3,35},{4,36},{5,37},{6,38},{7,39},{8,40},{9,... | collective-permute-start | bytes 98312 | tf_op jit(solution)/shard_map/ppermute | solution.py:290
  52.9 0.9 %collective-permute-start.17 = (f32[64,128]{1,0:T(8,128)S(1)}, f32[64,128]{1,0:T(8,128)S(1)}, u32[]{:S(2)}, u32[]{:S(2)}) collective-permute-start(f32[64,128]{1,0:T(8,128)S(1)} %collective-permute-done.13.refs_3_), channel_id=1, source_target_pairs={{0,32},{1,33},{2,34},{3,35},{4,36},{5,37},{6,38},{7,39},{8,40},{9,... | collective-permute-start | bytes 98312 | tf_op jit(solution)/shard_map/ppermute | solution.py:290
  53.9 1.7 %collective-permute-done.12.refs_2_ = f32[64,128]{1,0:T(8,128)S(1)} collective-permute-done((f32[64,128]{1,0:T(8,128)S(1)}, f32[64,128]{1,0:T(8,128)S(1)}, u32[]{:S(2)}, u32[]{:S(2)}) %collective-permute-start.12) | collective-permute-done | bytes 32800 | tf_op jit(solution)/shard_map/ppermute | solution.py:290
  55.6 1.8 %collective-permute-start.16 = (f32[64,128]{1,0:T(8,128)S(1)}, f32[64,128]{1,0:T(8,128)S(1)}, u32[]{:S(2)}, u32[]{:S(2)}) collective-permute-start(f32[64,128]{1,0:T(8,128)S(1)} %collective-permute-done.12.refs_2_), channel_id=1, source_target_pairs={{0,32},{1,33},{2,34},{3,35},{4,36},{5,37},{6,38},{7,39},{8,40},{9,... | collective-permute-start | bytes 98312 | tf_op jit(solution)/shard_map/ppermute | solution.py:290
  57.4 0.8 %collective-permute-done.16.refs_6_ = f32[64,128]{1,0:T(8,128)S(1)} collective-permute-done((f32[64,128]{1,0:T(8,128)S(1)}, f32[64,128]{1,0:T(8,128)S(1)}, u32[]{:S(2)}, u32[]{:S(2)}) %collective-permute-start.16) | collective-permute-done | bytes 32800 | tf_op jit(solution)/shard_map/ppermute | solution.py:290
  58.6 0.8 %shard_map.72 = (f32[3,128,128]{2,1,0:T(8,128)}, f32[128,128]{1,0:T(8,128)}) custom-call(f32[64,128]{1,0:T(8,128)S(1)} %shard_map.71.refs_0_, f32[64,128]{1,0:T(8,128)S(1)} %collective-permute-done.11.refs_1_, f32[64,128]{1,0:T(8,128)S(1)} %collective-permute-done.12.refs_2_, f32[64,128]{1,0:T(8,128)S(1)} %collective-permute-done.13.refs_3_, ...), custom_call_target="tpu_custom_call" | custom-call | tf_op jit(solution)/shard_map/pallas_call | solution.py:327
  (27 shorter events, 2.9 us)
Async XLA Ops:
  0.6 0.9 %copy-start = (f32[1,3,128,128]{3,2,1,0:T(8,128)S(1)}, f32[1,3,128,128]{3,2,1,0:T(8,128)}, u32[]{:S(2)}) copy-start(f32[1,3,128,128]{3,2,1,0:T(8,128)} %rad.1) | copy-start | bytes 589828
  1.6 0.9 %copy-start.1 = (f32[1,3,128,128]{3,2,1,0:T(8,128)S(1)}, f32[1,3,128,128]{3,2,1,0:T(8,128)}, u32[]{:S(2)}) copy-start(f32[1,3,128,128]{3,2,1,0:T(8,128)} %nor.1) | copy-start | bytes 589828
  2.5 0.8 %copy-start.2 = (f32[1,128,128]{2,1,0:T(8,128)S(1)}, f32[1,128,128]{2,1,0:T(8,128)}, u32[]{:S(2)}) copy-start(f32[1,128,128]{2,1,0:T(8,128)} %mom.1) | copy-start | bytes 196612
  3.3 0.8 %copy-start.3 = (f32[1,128,128]{2,1,0:T(8,128)S(1)}, f32[1,128,128]{2,1,0:T(8,128)}, u32[]{:S(2)}) copy-start(f32[1,128,128]{2,1,0:T(8,128)} %dep.1) | copy-start | bytes 196612
  4.2 0.7 %copy-start.4 = (s32[1,8,8]{2,1,0:T(8,128)S(1)}, s32[1,8,8]{2,1,0:T(8,128)}, u32[]{:S(2)}) copy-start(s32[1,8,8]{2,1,0:T(8,128)} %cnt.1) | copy-start | bytes 772
  4.9 4.5 %collective-permute-start = (f32[520,128]{1,0:T(8,128)S(1)}, f32[520,128]{1,0:T(8,128)S(1)}, u32[]{:S(2)}, u32[]{:S(2)}) collective-permute-start(f32[520,128]{1,0:T(8,128)S(1)} %get-tuple-element.11), channel_id=1, source_target_pairs={{0,32},{1,33},{2,34},{3,35},{4,36},{5,37},{6,38},{7,39},{8,40},{9,... | collective-permute-start | bytes 798728 | tf_op jit(solution)/shard_map/ppermute | solution.py:290
  9.5 6.3 %collective-permute-start.1 = (f32[392,128]{1,0:T(8,128)S(1)}, f32[392,128]{1,0:T(8,128)S(1)}, u32[]{:S(2)}, u32[]{:S(2)}) collective-permute-start(f32[392,128]{1,0:T(8,128)S(1)} %get-tuple-element.12.own), channel_id=1, source_target_pairs={{0,64},{1,65},{2,66},{3,67},{4,68},{5,69},{6,70},{7,71},{8,72},{9,... | collective-permute-start | bytes 602120 | tf_op jit(solution)/shard_map/ppermute | solution.py:290
  9.6 8.1 %collective-permute-start.3 = (f32[392,128]{1,0:T(8,128)S(1)}, f32[392,128]{1,0:T(8,128)S(1)}, u32[]{:S(2)}, u32[]{:S(2)}) collective-permute-start(f32[392,128]{1,0:T(8,128)S(1)} %get-tuple-element.13), channel_id=1, source_target_pairs={{0,192},{1,193},{2,194},{3,195},{4,196},{5,197},{6,198},{7,199},{8... | collective-permute-start | bytes 602120 | tf_op jit(solution)/shard_map/ppermute | solution.py:290
  11.0 9.8 %collective-permute-start.2 = (f32[392,128]{1,0:T(8,128)S(1)}, f32[392,128]{1,0:T(8,128)S(1)}, u32[]{:S(2)}, u32[]{:S(2)}) collective-permute-start(f32[392,128]{1,0:T(8,128)S(1)} %get-tuple-element.13), channel_id=1, source_target_pairs={{0,128},{1,129},{2,130},{3,131},{4,132},{5,133},{6,134},{7,135},{8... | collective-permute-start | bytes 602120 | tf_op jit(solution)/shard_map/ppermute | solution.py:290
  21.0 5.7 %collective-permute-start.7 = (f32[384,128]{1,0:T(8,128)S(1)}, f32[384,128]{1,0:T(8,128)S(1)}, u32[]{:S(2)}, u32[]{:S(2)}) collective-permute-start(f32[384,128]{1,0:T(8,128)S(1)} %get-tuple-element.14.refs_0_), channel_id=1, source_target_pairs={{0,32},{1,33},{2,34},{3,35},{4,36},{5,37},{6,38},{7,39},{8,40},{9,... | collective-permute-start | bytes 589832 | tf_op jit(solution)/shard_map/ppermute | solution.py:290
  22.9 1.3 %collective-permute-start.5 = (f32[128,128]{1,0:T(8,128)S(1)}, f32[128,128]{1,0:T(8,128)S(1)}, u32[]{:S(2)}, u32[]{:S(2)}) collective-permute-start(f32[128,128]{1,0:T(8,128)S(1)} %get-tuple-element.16), channel_id=1, source_target_pairs={{4,8},{5,9},{6,10},{7,11},{8,4},{9,5},{10,6},{11,7},{12,16},{13,17... | collective-permute-start | bytes 196616 | tf_op jit(solution)/shard_map/ppermute | solution.py:290
  23.5 0.8 %collective-permute-start.4 = (f32[96,128]{1,0:T(8,128)S(1)}, f32[96,128]{1,0:T(8,128)S(1)}, u32[]{:S(2)}, u32[]{:S(2)}) collective-permute-start(f32[96,128]{1,0:T(8,128)S(1)} %get-tuple-element.15), channel_id=1, source_target_pairs={{1,2},{2,1},{5,6},{6,5},{9,10},{10,9},{13,14},{14,13},{17,18},{18,... | collective-permute-start | bytes 147464 | tf_op jit(solution)/shard_map/ppermute | solution.py:290
  24.2 2.5 %collective-permute-start.9 = (f32[128,128]{1,0:T(8,128)S(1)}, f32[128,128]{1,0:T(8,128)S(1)}, u32[]{:S(2)}, u32[]{:S(2)}) collective-permute-start(f32[128,128]{1,0:T(8,128)S(1)} %collective-permute-done.5.refs_2_), channel_id=1, source_target_pairs={{0,32},{1,33},{2,34},{3,35},{4,36},{5,37},{6,38},{7,39},{8,40},{9,... | collective-permute-start | bytes 196616 | tf_op jit(solution)/shard_map/ppermute | solution.py:290
  24.3 2.4 %collective-permute-start.8 = (f32[96,128]{1,0:T(8,128)S(1)}, f32[96,128]{1,0:T(8,128)S(1)}, u32[]{:S(2)}, u32[]{:S(2)}) collective-permute-start(f32[96,128]{1,0:T(8,128)S(1)} %collective-permute-done.4.refs_1_), channel_id=1, source_target_pairs={{0,32},{1,33},{2,34},{3,35},{4,36},{5,37},{6,38},{7,39},{8,40},{9,... | collective-permute-start | bytes 147464 | tf_op jit(solution)/shard_map/ppermute | solution.py:290
  24.8 0.7 %collective-permute-start.6 = (f32[32,128]{1,0:T(8,128)S(1)}, f32[32,128]{1,0:T(8,128)S(1)}, u32[]{:S(2)}, u32[]{:S(2)}) collective-permute-start(f32[32,128]{1,0:T(8,128)S(1)} %get-tuple-element.17), channel_id=1, source_target_pairs={{5,10},{6,9},{9,6},{10,5},{13,18},{14,17},{17,14},{18,13},{21,26},... | collective-permute-start | bytes 49160 | tf_op jit(solution)/shard_map/ppermute | solution.py:290
  25.5 1.3 %collective-permute-start.10 = (f32[32,128]{1,0:T(8,128)S(1)}, f32[32,128]{1,0:T(8,128)S(1)}, u32[]{:S(2)}, u32[]{:S(2)}) collective-permute-start(f32[32,128]{1,0:T(8,128)S(1)} %collective-permute-done.6.refs_3_), channel_id=1, source_target_pairs={{0,32},{1,33},{2,34},{3,35},{4,36},{5,37},{6,38},{7,39},{8,40},{9,... | collective-permute-start | bytes 49160 | tf_op jit(solution)/shard_map/ppermute | solution.py:290
  36.6 16.3 %collective-permute-start.13 = (f32[64,128]{1,0:T(8,128)S(1)}, f32[64,128]{1,0:T(8,128)S(1)}, u32[]{:S(2)}, u32[]{:S(2)}) collective-permute-start(f32[64,128]{1,0:T(8,128)S(1)} %shard_map.71.refs_0_), channel_id=1, source_target_pairs={{0,192},{1,193},{2,194},{3,195},{4,196},{5,197},{6,198},{7,199},{8... | collective-permute-start | bytes 98312 | tf_op jit(solution)/shard_map/ppermute | solution.py:290
  51.3 4.3 %collective-permute-start.12 = (f32[64,128]{1,0:T(8,128)S(1)}, f32[64,128]{1,0:T(8,128)S(1)}, u32[]{:S(2)}, u32[]{:S(2)}) collective-permute-start(f32[64,128]{1,0:T(8,128)S(1)} %shard_map.71.refs_0_), channel_id=1, source_target_pairs={{0,128},{1,129},{2,130},{3,131},{4,132},{5,133},{6,134},{7,135},{8... | collective-permute-start | bytes 98312 | tf_op jit(solution)/shard_map/ppermute | solution.py:290
  51.4 6.0 %collective-permute-start.11 = (f32[64,128]{1,0:T(8,128)S(1)}, f32[64,128]{1,0:T(8,128)S(1)}, u32[]{:S(2)}, u32[]{:S(2)}) collective-permute-start(f32[64,128]{1,0:T(8,128)S(1)} %shard_map.71.refs_0_), channel_id=1, source_target_pairs={{0,64},{1,65},{2,66},{3,67},{4,68},{5,69},{6,70},{7,71},{8,72},{9,... | collective-permute-start | bytes 98312 | tf_op jit(solution)/shard_map/ppermute | solution.py:290
  52.0 5.4 %collective-permute-start.14 = (f32[64,128]{1,0:T(8,128)S(1)}, f32[64,128]{1,0:T(8,128)S(1)}, u32[]{:S(2)}, u32[]{:S(2)}) collective-permute-start(f32[64,128]{1,0:T(8,128)S(1)} %shard_map.71.refs_0_), channel_id=1, source_target_pairs={{0,32},{1,33},{2,34},{3,35},{4,36},{5,37},{6,38},{7,39},{8,40},{9,... | collective-permute-start | bytes 98312 | tf_op jit(solution)/shard_map/ppermute | solution.py:290
  52.9 4.5 %collective-permute-start.17 = (f32[64,128]{1,0:T(8,128)S(1)}, f32[64,128]{1,0:T(8,128)S(1)}, u32[]{:S(2)}, u32[]{:S(2)}) collective-permute-start(f32[64,128]{1,0:T(8,128)S(1)} %collective-permute-done.13.refs_3_), channel_id=1, source_target_pairs={{0,32},{1,33},{2,34},{3,35},{4,36},{5,37},{6,38},{7,39},{8,40},{9,... | collective-permute-start | bytes 98312 | tf_op jit(solution)/shard_map/ppermute | solution.py:290
  55.6 2.6 %collective-permute-start.16 = (f32[64,128]{1,0:T(8,128)S(1)}, f32[64,128]{1,0:T(8,128)S(1)}, u32[]{:S(2)}, u32[]{:S(2)}) collective-permute-start(f32[64,128]{1,0:T(8,128)S(1)} %collective-permute-done.12.refs_2_), channel_id=1, source_target_pairs={{0,32},{1,33},{2,34},{3,35},{4,36},{5,37},{6,38},{7,39},{8,40},{9,... | collective-permute-start | bytes 98312 | tf_op jit(solution)/shard_map/ppermute | solution.py:290
  57.4 1.2 %collective-permute-start.15 = (f32[64,128]{1,0:T(8,128)S(1)}, f32[64,128]{1,0:T(8,128)S(1)}, u32[]{:S(2)}, u32[]{:S(2)}) collective-permute-start(f32[64,128]{1,0:T(8,128)S(1)} %collective-permute-done.11.refs_1_), channel_id=1, source_target_pairs={{0,32},{1,33},{2,34},{3,35},{4,36},{5,37},{6,38},{7,39},{8,40},{9,... | collective-permute-start | bytes 98312 | tf_op jit(solution)/shard_map/ppermute | solution.py:290

commit v2 on v1

--- a/solution.py
+++ b/solution.py
@@ -46,15 +46,22 @@
     return pl.multiple_of(value, 8)
 
 
-def pack_kernel(rad, mom, nor, dep, cnt, keep, send):
+def pack_kernel(rad, mom, nor, dep, cnt, keep, send, blocks, sems):
     core = place()[0]
+    count = pltpu.make_async_copy(cnt.at[0], blocks, sems.at[8])
+    count.start()
 
     def fill(colour_ref, normal_ref):
-        for ch in range(3):
-            colour_ref[ch * TILE : (ch + 1) * TILE, :] = rad[0, ch]
-            normal_ref[ch * TILE : (ch + 1) * TILE, :] = nor[0, ch]
-        colour_ref[3 * TILE : 4 * TILE, :] = mom[0]
-        normal_ref[3 * TILE : 4 * TILE, :] = dep[0]
+        copies = []
+        for ch in range(4):
+            at = rows(ch * TILE, TILE)
+            colour, normal = (rad.at[0, ch], nor.at[0, ch]) if ch < 3 else (mom.at[0], dep.at[0])
+            copies.append(pltpu.make_async_copy(colour, colour_ref.at[at, :], sems.at[ch]))
+            copies.append(pltpu.make_async_copy(normal, normal_ref.at[at, :], sems.at[4 + ch]))
+        for copy in copies:
+            copy.start()
+        for copy in copies:
+            copy.wait()
 
     @pl.when(core == 0)
     def _():
@@ -64,10 +71,11 @@
     def _():
         fill(send, keep)
 
-    blocks = cnt[0].astype(jnp.float32)
+    count.wait()
+    number = blocks[...].astype(jnp.float32)
     for ref in (keep, send):
         ref[4 * TILE :, :] = jnp.zeros((8, TILE), jnp.float32)
-        ref[4 * TILE :, 0:8] = blocks
+        ref[4 * TILE :, 0:8] = number
 
 
 def pair_kernel(keep, recv, near, far):
@@ -110,12 +118,12 @@
     rim_d[...] = rim_x[rows(first, RIM), :]
 
 
-NF = 9
+SPANS = ((0, 96), (8, 88), (16, 80), (32, 64))
 PAD = 32
 
 
 def filter_kernel(*refs):
-    (f0, x0, z0, d0, f1, x1, z1, d1, out, cur, geo, shifted) = refs
+    (f0, x0, z0, d0, f1, x1, z1, d1, out, cur, geo, cur_moved, geo_moved) = refs
     core, half_row, half_col, ty, tx = place()
     lanes = lax.broadcasted_iota(jnp.int32, (RIM, TILE), 1)
     n_ty, n_tx = lax.axis_size("ty"), lax.axis_size("tx")
@@ -169,66 +177,65 @@
         assemble(True, f0, x0, z0, d0)
         assemble(False, f1, x1, z1, d1)
 
-    def add_luma(i, carry):
-        at = rows(aligned(i * 8), 8)
+    for r in range(PAD, PAD + WIN, 8):
+        at = rows(r, 8)
         cur[0, 4, at, :] = luminance(cur[0, 0, at, :], cur[0, 1, at, :], cur[0, 2, at, :])
-        return carry
-
-    lax.fori_loop(0, (WIN + 2 * PAD) // 8, add_luma, 0)
-
-    for level, (low, high) in enumerate(((0, 96), (8, 88), (16, 80), (32, 64))):
+
+    moved_by = (-16, -8, -4, -2, -1, 1, 2, 4, 8, 16)
+    made = set()
+
+    def roll(value, by):
+        return pltpu.roll(value, -by % TILE, 1)
+
+    for level, (low, high) in enumerate(SPANS):
         dil = 2**level
         src, dst = level % 2, 1 - level % 2
         reach = -(-2 * dil // 8) * 8
-        start, stop = PAD + low - reach, PAD + high + reach
-
-        def shift(i, carry, src=src, start=start, dil=dil):
-            at = rows(aligned(start + i * 8), 8)
-            for f in range(NF):
-                value = geo[f, at, :] if f < 4 else cur[src, f - 4, at, :]
-                for b in range(5):
-                    moved = value if b == 2 else pltpu.roll(value, (-(b - 2) * dil) % TILE, 1)
-                    shifted[b, f, at, :] = moved
-            return carry
-
-        lax.fori_loop(0, (stop - start) // 8, shift, 0)
-
-        def step(i, carry, src=src, dst=dst, low=low, dil=dil, level=level):
-            base = PAD + low + i * 8
-            here = rows(aligned(base), 8)
+        start, stop = PAD + max(low - reach, 0), PAD + min(high + reach, WIN)
+        for r in range(start, stop, 8):
+            at = rows(r, 8)
+            for b in (-2, -1, 1, 2):
+                if (b * dil, r) not in made:
+                    made.add((b * dil, r))
+                    for f in range(4):
+                        geo_moved[moved_by.index(b * dil), f, at, :] = roll(geo[f, at, :], b * dil)
+                moved = [roll(cur[src, f, at, :], b * dil) for f in range(4)]
+                moved.append(luminance(*moved[:3]))
+                for f in range(5):
+                    cur_moved[b + 2, f, at, :] = moved[f]
+
+        for r in range(PAD + low, PAD + high, 8):
+            here = rows(r, 8)
             n0, n1, n2, depth = (geo[f, here, :] for f in range(4))
             luma = cur[src, 4, here, :]
             slope = -1.0 / (SIGMA_LUMA * jnp.sqrt(cur[src, 3, here, :]) + LUMA_FLOOR)
-            total = c0 = c1 = c2 = var = None
-            for a in range(5):
-                for b in range(5):
-                    at = rows(base + (a - 2) * dil, 8)
-                    tap = [shifted[b, f, at, :] for f in range(NF)]
-                    e = jnp.abs(tap[8] - luma) * slope - jnp.abs(tap[3] - depth)
-                    e = e - jnp.square(tap[0] - n0) - jnp.square(tap[1] - n1)
-                    e = e - jnp.square(tap[2] - n2)
-                    w = (TAPS[a] * TAPS[b]) * jnp.exp(e)
-                    parts = (w, w * tap[4], w * tap[5], w * tap[6], w * w * tap[7])
-                    if total is None:
-                        total, c0, c1, c2, var = parts
+            sums = None
+            for a in range(-2, 3):
+                at = rows(r + a * dil, 8)
+                for b in range(-2, 3):
+                    if b == 0:
+                        g = [geo[f, at, :] for f in range(4)]
+                        t = [cur[src, f, at, :] for f in range(5)]
                     else:
-                        total, c0, c1, c2, var = (
-                            p + q for p, q in zip((total, c0, c1, c2, var), parts)
-                        )
-            inv = 1.0 / total
-            c0, c1, c2, var = c0 * inv, c1 * inv, c2 * inv, var * (inv * inv)
-            if level < 3:
+                        g = [geo_moved[moved_by.index(b * dil), f, at, :] for f in range(4)]
+                        t = [cur_moved[b + 2, f, at, :] for f in range(5)]
+                    e = jnp.abs(t[4] - luma) * slope - jnp.abs(g[3] - depth)
+                    e = e - jnp.square(g[0] - n0) - jnp.square(g[1] - n1)
+                    e = e - jnp.square(g[2] - n2)
+                    w = (TAPS[a + 2] * TAPS[b + 2]) * jnp.exp(e)
+                    parts = (w, w * t[0], w * t[1], w * t[2], w * w * t[3])
+                    sums = parts if sums is None else [p + q for p, q in zip(sums, parts)]
+            inv = 1.0 / sums[0]
+            c0, c1, c2, var = sums[1] * inv, sums[2] * inv, sums[3] * inv, sums[4] * (inv * inv)
+            if level < len(SPANS) - 1:
                 for f, value in enumerate((c0, c1, c2, var, luminance(c0, c1, c2))):
                     cur[dst, f, here, :] = value
             else:
                 lane = lax.broadcasted_iota(jnp.int32, (8, TILE), 1)
                 for k, (p, q) in enumerate(((c0, c1), (c2, var))):
-                    out[rows(aligned(k * 32 + i * 8), 8), :] = jnp.where(
-                        lane < HALF, pltpu.roll(p, TILE - 32, 1), pltpu.roll(q, 32, 1)
+                    out[rows(k * 32 + r - PAD - low, 8), :] = jnp.where(
+                        lane < HALF, roll(p, 32), roll(q, -32)
                     )
-            return carry
-
-        lax.fori_loop(0, (high - low) // 8, step, 0)
 
 
 def tile_kernel(*refs):
@@ -255,9 +262,10 @@
                     variance[at, :] = second
 
 
-def call(kernel, shapes, scratch=()):
+def call(kernel, shapes, scratch=(), space=None):
     return pl.pallas_call(
         kernel,
+        **({"in_specs": [pl.BlockSpec(memory_space=pltpu.HBM)] * space} if space else {}),
         out_shape=[jax.ShapeDtypeStruct(s, jnp.float32) for s in shapes],
         scratch_shapes=list(scratch),
         compiler_params=pltpu.CompilerParams(vmem_limit_bytes=24 * 2**20),
@@ -297,7 +305,17 @@
 
     packed = (4 * TILE + 8, TILE)
     window = (4 * WIN + 8, TILE)
-    keep, give = call(pack_kernel, [packed, packed])(radiance, moment, normal, depth_sum, counts)
+    keep, give = call(
+        pack_kernel,
+        [packed, packed],
+        [pltpu.VMEM((8, 8), jnp.int32), pltpu.SemaphoreType.DMA((9,))],
+        5,
+    )(
+        *(
+            pltpu.with_memory_space_constraint(value, pltpu.HBM)
+            for value in (radiance, moment, normal, depth_sum, counts)
+        )
+    )
     near, far = call(pair_kernel, [window, window])(keep, other_core(give))
     r1, r2, r3 = other_y(near, 1), other_y(far, 2), other_y(far, 3)
     field, rim_x, rim_z, rim_d = call(
@@ -311,7 +329,7 @@
     rim_d = send(
         rim_d, lambda s, ty, tx: (s, ty + step_of(s, ty, tx)[0], tx + step_of(s, ty, tx)[1])
     )
-    rims = (rim_x, rim_z, rim_d)
+    rims = lax.optimization_barrier((rim_x, rim_z, rim_d))
     rims_1 = [other_core(r) for r in rims]
     (mine,) = call(
         filter_kernel,
@@ -319,7 +337,8 @@
         [
             pltpu.VMEM((2, 5, WIN + 2 * PAD, TILE), jnp.float32),
             pltpu.VMEM((4, WIN + 2 * PAD, TILE), jnp.float32),
-            pltpu.VMEM((5, NF, WIN + 2 * PAD, TILE), jnp.float32),
+            pltpu.VMEM((5, 5, WIN + 2 * PAD, TILE), jnp.float32),
+            pltpu.VMEM((10, 4, WIN + 2 * PAD, TILE), jnp.float32),
         ],
     )(field, *rims, field_1, *rims_1)
     got = [mine] + [other_y(mine, k) for k in (1, 2, 3)]

time: 59.8 us -> 49.5 us (0.83)
  local copies, waits for them, and re-layouts: 4.21 us -> 0 us
  Pallas kernels: 11 us -> 7.12 us
  starting transfers between devices: 30.3 us -> 28.2 us
    pallas_call x1, Pallas kernels: 9.86 us -> 4.84 us  [per_device(): call(filter_kernel, [(HALF, TILE)], [pltpu.VMEM((2, 5, WIN + 2 * PAD, TIL...]
    unnamed x10 -> x0, local copies, waits for them, and re-layouts: 4.21 us -> none
    ppermute x18, starting transfers between devices: 30.3 us -> 28.2 us  [send(): return lax.ppermute(value, AXES, pairs(sizes, partner))]
    pallas_call x1, Pallas kernels: 0.04 us -> 1.17 us  [per_device(): call(pack_kernel, [packed, packed], [pltpu.VMEM((8, 8), jnp.int32), pltpu...]
where the time goes in v2:
time: 49.5 us; the launch traced here: 49.3 us
  starting transfers between devices  28.2 us (57%)
  waiting for transfers between devices  13.2 us (27%)
  Pallas kernels  7.12 us (14%)
  between operations  0.73 us (1%)
    ppermute x18, starting transfers between devices, send(): return lax.ppermute(value, AXES, pairs(sizes, partner))  28.2 us
    ppermute x18, waiting for transfers between devices, send(): return lax.ppermute(value, AXES, pairs(sizes, partner))  13.2 us
    pallas_call x1, Pallas kernels, per_device(): call(filter_kernel, [(HALF, TILE)], [pltpu.VMEM((2, 5, WIN + 2 * PAD, TIL...  4.84 us
    pallas_call x1, Pallas kernels, per_device(): call(pack_kernel, [packed, packed], [pltpu.VMEM((8, 8), jnp.int32), pltpu...  1.17 us
  transfers between devices with their start and end apart: 18, of which 8 were waited for; matrix products, arithmetic and copies ran while one was open for 0% of the time, Pallas kernels for 0%

profile of v2, /device:TPU:1, one launch (start us, length us, event | category | flops | bytes accessed | tf_op | source)
XLA Modules:
  0.0 49.3 jit_solution(6772192143211441607)
XLA Ops:
  0.6 1.2 %shard_map.68 = (f32[520,128]{1,0:T(8,128)S(1)}, f32[520,128]{1,0:T(8,128)S(1)}) custom-call(f32[1,3,128,128]{3,2,1,0:T(8,128)} %rad.1, f32[1,128,128]{2,1,0:T(8,128)} %mom.1, f32[1,3,128,128]{3,2,1,0:T(8,128)} %nor.1, f32[1,128,128]{2,1,0:T(8,128)} %dep.1, s32[1,8,8]{2,1,0:T(8,128)} %cnt.1), custom_call_target="tpu_custom_call" | custom-call | tf_op jit(solution)/shard_map/pallas_call | solution.py:308
  1.8 3.3 %collective-permute-start = (f32[520,128]{1,0:T(8,128)S(1)}, f32[520,128]{1,0:T(8,128)S(1)}, u32[]{:S(2)}, u32[]{:S(2)}) collective-permute-start(f32[520,128]{1,0:T(8,128)S(1)} %get-tuple-element.14), channel_id=1, source_target_pairs={{0,32},{1,33},{2,34},{3,35},{4,36},{5,37},{6,38},{7,39},{8,40},{9,... | collective-permute-start | bytes 798728 | tf_op jit(solution)/shard_map/ppermute | solution.py:298
  5.1 1.2 %collective-permute-done.recv = f32[520,128]{1,0:T(8,128)S(1)} collective-permute-done((f32[520,128]{1,0:T(8,128)S(1)}, f32[520,128]{1,0:T(8,128)S(1)}, u32[]{:S(2)}, u32[]{:S(2)}) %collective-permute-start) | collective-permute-done | bytes 266272 | tf_op jit(solution)/shard_map/ppermute | solution.py:298
  6.4 1.4 %collective-permute-start.3 = (f32[392,128]{1,0:T(8,128)S(1)}, f32[392,128]{1,0:T(8,128)S(1)}, u32[]{:S(2)}, u32[]{:S(2)}) collective-permute-start(f32[392,128]{1,0:T(8,128)S(1)} %get-tuple-element.16), channel_id=1, source_target_pairs={{0,192},{1,193},{2,194},{3,195},{4,196},{5,197},{6,198},{7,199},{8... | collective-permute-start | bytes 602120 | tf_op jit(solution)/shard_map/ppermute | solution.py:298
  7.9 1.8 %collective-permute-start.2 = (f32[392,128]{1,0:T(8,128)S(1)}, f32[392,128]{1,0:T(8,128)S(1)}, u32[]{:S(2)}, u32[]{:S(2)}) collective-permute-start(f32[392,128]{1,0:T(8,128)S(1)} %get-tuple-element.16), channel_id=1, source_target_pairs={{0,128},{1,129},{2,130},{3,131},{4,132},{5,133},{6,134},{7,135},{8... | collective-permute-start | bytes 602120 | tf_op jit(solution)/shard_map/ppermute | solution.py:298
  9.7 2.9 %collective-permute-done.1.r1 = f32[392,128]{1,0:T(8,128)S(1)} collective-permute-done((f32[392,128]{1,0:T(8,128)S(1)}, f32[392,128]{1,0:T(8,128)S(1)}, u32[]{:S(2)}, u32[]{:S(2)}) %collective-permute-start.1) | collective-permute-done | bytes 200736 | tf_op jit(solution)/shard_map/ppermute | solution.py:298
  12.6 1.9 %collective-permute-done.3.r3 = f32[392,128]{1,0:T(8,128)S(1)} collective-permute-done((f32[392,128]{1,0:T(8,128)S(1)}, f32[392,128]{1,0:T(8,128)S(1)}, u32[]{:S(2)}, u32[]{:S(2)}) %collective-permute-start.3) | collective-permute-done | bytes 200736 | tf_op jit(solution)/shard_map/ppermute | solution.py:298
  14.5 3.2 %collective-permute-done.2.r2 = f32[392,128]{1,0:T(8,128)S(1)} collective-permute-done((f32[392,128]{1,0:T(8,128)S(1)}, f32[392,128]{1,0:T(8,128)S(1)}, u32[]{:S(2)}, u32[]{:S(2)}) %collective-permute-start.2) | collective-permute-done | bytes 200736 | tf_op jit(solution)/shard_map/ppermute | solution.py:298
  17.9 1.8 %collective-permute-start.7 = (f32[384,128]{1,0:T(8,128)S(1)}, f32[384,128]{1,0:T(8,128)S(1)}, u32[]{:S(2)}, u32[]{:S(2)}) collective-permute-start(f32[384,128]{1,0:T(8,128)S(1)} %get-tuple-element.17.refs_0_), channel_id=1, source_target_pairs={{0,32},{1,33},{2,34},{3,35},{4,36},{5,37},{6,38},{7,39},{8,40},{9,... | collective-permute-start | bytes 589832 | tf_op jit(solution)/shard_map/ppermute | solution.py:298
  19.8 0.7 %collective-permute-start.5 = (f32[128,128]{1,0:T(8,128)S(1)}, f32[128,128]{1,0:T(8,128)S(1)}, u32[]{:S(2)}, u32[]{:S(2)}) collective-permute-start(f32[128,128]{1,0:T(8,128)S(1)} %get-tuple-element.19), channel_id=1, source_target_pairs={{4,8},{5,9},{6,10},{7,11},{8,4},{9,5},{10,6},{11,7},{12,16},{13,17... | collective-permute-start | bytes 196616 | tf_op jit(solution)/shard_map/ppermute | solution.py:298
  20.4 0.7 %collective-permute-start.4 = (f32[96,128]{1,0:T(8,128)S(1)}, f32[96,128]{1,0:T(8,128)S(1)}, u32[]{:S(2)}, u32[]{:S(2)}) collective-permute-start(f32[96,128]{1,0:T(8,128)S(1)} %get-tuple-element.18), channel_id=1, source_target_pairs={{1,2},{2,1},{5,6},{6,5},{9,10},{10,9},{13,14},{14,13},{17,18},{18,... | collective-permute-start | bytes 147464 | tf_op jit(solution)/shard_map/ppermute | solution.py:298
  21.1 0.7 %collective-permute-start.6 = (f32[32,128]{1,0:T(8,128)S(1)}, f32[32,128]{1,0:T(8,128)S(1)}, u32[]{:S(2)}, u32[]{:S(2)}) collective-permute-start(f32[32,128]{1,0:T(8,128)S(1)} %get-tuple-element.20), channel_id=1, source_target_pairs={{5,10},{6,9},{9,6},{10,5},{13,18},{14,17},{17,14},{18,13},{21,26},... | collective-permute-start | bytes 49160 | tf_op jit(solution)/shard_map/ppermute | solution.py:298
  21.9 0.5 collective-permute-start.8
  22.5 1.1 %collective-permute-done.10.refs_7_ = f32[32,128]{1,0:T(8,128)S(1)} collective-permute-done((f32[32,128]{1,0:T(8,128)S(1)}, f32[32,128]{1,0:T(8,128)S(1)}, u32[]{:S(2)}, u32[]{:S(2)}) %collective-permute-start.10) | collective-permute-done | bytes 16416 | tf_op jit(solution)/shard_map/ppermute | solution.py:298
  23.6 4.8 %shard_map.71.refs_0_ = f32[64,128]{1,0:T(8,128)S(1)} custom-call(f32[384,128]{1,0:T(8,128)S(1)} %get-tuple-element.17.refs_0_, f32[96,128]{1,0:T(8,128)S(1)} %collective-permute-done.4.refs_1_, f32[128,128]{1,0:T(8,128)S(1)} %collective-permute-done.5.refs_2_, f32[32,128]{1,0:T(8,128)S(1)} %collective-permute-done.6.refs_3_, ...), custom_call_target="tpu_custom_call" | custom-call | tf_op jit(solution)/shard_map/pallas_call | solution.py:334
  28.4 12.7 %collective-permute-start.13 = (f32[64,128]{1,0:T(8,128)S(1)}, f32[64,128]{1,0:T(8,128)S(1)}, u32[]{:S(2)}, u32[]{:S(2)}) collective-permute-start(f32[64,128]{1,0:T(8,128)S(1)} %shard_map.71.refs_0_), channel_id=1, source_target_pairs={{0,192},{1,193},{2,194},{3,195},{4,196},{5,197},{6,198},{7,199},{8... | collective-permute-start | bytes 98312 | tf_op jit(solution)/shard_map/ppermute | solution.py:298
  41.2 0.7 %collective-permute-start.11 = (f32[64,128]{1,0:T(8,128)S(1)}, f32[64,128]{1,0:T(8,128)S(1)}, u32[]{:S(2)}, u32[]{:S(2)}) collective-permute-start(f32[64,128]{1,0:T(8,128)S(1)} %shard_map.71.refs_0_), channel_id=1, source_target_pairs={{0,64},{1,65},{2,66},{3,67},{4,68},{5,69},{6,70},{7,71},{8,72},{9,... | collective-permute-start | bytes 98312 | tf_op jit(solution)/shard_map/ppermute | solution.py:298
  41.9 0.9 %collective-permute-start.14 = (f32[64,128]{1,0:T(8,128)S(1)}, f32[64,128]{1,0:T(8,128)S(1)}, u32[]{:S(2)}, u32[]{:S(2)}) collective-permute-start(f32[64,128]{1,0:T(8,128)S(1)} %shard_map.71.refs_0_), channel_id=1, source_target_pairs={{0,32},{1,33},{2,34},{3,35},{4,36},{5,37},{6,38},{7,39},{8,40},{9,... | collective-permute-start | bytes 98312 | tf_op jit(solution)/shard_map/ppermute | solution.py:298
  42.8 0.9 %collective-permute-start.17 = (f32[64,128]{1,0:T(8,128)S(1)}, f32[64,128]{1,0:T(8,128)S(1)}, u32[]{:S(2)}, u32[]{:S(2)}) collective-permute-start(f32[64,128]{1,0:T(8,128)S(1)} %collective-permute-done.13.refs_3_), channel_id=1, source_target_pairs={{0,32},{1,33},{2,34},{3,35},{4,36},{5,37},{6,38},{7,39},{8,40},{9,... | collective-permute-start | bytes 98312 | tf_op jit(solution)/shard_map/ppermute | solution.py:298
  43.7 1.8 %collective-permute-done.12.refs_2_ = f32[64,128]{1,0:T(8,128)S(1)} collective-permute-done((f32[64,128]{1,0:T(8,128)S(1)}, f32[64,128]{1,0:T(8,128)S(1)}, u32[]{:S(2)}, u32[]{:S(2)}) %collective-permute-start.12) | collective-permute-done | bytes 32800 | tf_op jit(solution)/shard_map/ppermute | solution.py:298
  45.4 1.8 %collective-permute-start.16 = (f32[64,128]{1,0:T(8,128)S(1)}, f32[64,128]{1,0:T(8,128)S(1)}, u32[]{:S(2)}, u32[]{:S(2)}) collective-permute-start(f32[64,128]{1,0:T(8,128)S(1)} %collective-permute-done.12.refs_2_), channel_id=1, source_target_pairs={{0,32},{1,33},{2,34},{3,35},{4,36},{5,37},{6,38},{7,39},{8,40},{9,... | collective-permute-start | bytes 98312 | tf_op jit(solution)/shard_map/ppermute | solution.py:298
  47.2 0.8 %collective-permute-done.16.refs_6_ = f32[64,128]{1,0:T(8,128)S(1)} collective-permute-done((f32[64,128]{1,0:T(8,128)S(1)}, f32[64,128]{1,0:T(8,128)S(1)}, u32[]{:S(2)}, u32[]{:S(2)}) %collective-permute-start.16) | collective-permute-done | bytes 32800 | tf_op jit(solution)/shard_map/ppermute | solution.py:298
  48.1 0.4 collective-permute-done.15.refs_5_
  48.4 0.8 %shard_map.72 = (f32[3,128,128]{2,1,0:T(8,128)}, f32[128,128]{1,0:T(8,128)}) custom-call(f32[64,128]{1,0:T(8,128)S(1)} %shard_map.71.refs_0_, f32[64,128]{1,0:T(8,128)S(1)} %collective-permute-done.11.refs_1_, f32[64,128]{1,0:T(8,128)S(1)} %collective-permute-done.12.refs_2_, f32[64,128]{1,0:T(8,128)S(1)} %collective-permute-done.13.refs_3_, ...), custom_call_target="tpu_custom_call" | custom-call | tf_op jit(solution)/shard_map/pallas_call | solution.py:346
  (17 shorter events, 0.6 us)
Async XLA Ops:
  1.8 4.5 %collective-permute-start = (f32[520,128]{1,0:T(8,128)S(1)}, f32[520,128]{1,0:T(8,128)S(1)}, u32[]{:S(2)}, u32[]{:S(2)}) collective-permute-start(f32[520,128]{1,0:T(8,128)S(1)} %get-tuple-element.14), channel_id=1, source_target_pairs={{0,32},{1,33},{2,34},{3,35},{4,36},{5,37},{6,38},{7,39},{8,40},{9,... | collective-permute-start | bytes 798728 | tf_op jit(solution)/shard_map/ppermute | solution.py:298
  6.3 6.3 %collective-permute-start.1 = (f32[392,128]{1,0:T(8,128)S(1)}, f32[392,128]{1,0:T(8,128)S(1)}, u32[]{:S(2)}, u32[]{:S(2)}) collective-permute-start(f32[392,128]{1,0:T(8,128)S(1)} %get-tuple-element.15.own), channel_id=1, source_target_pairs={{0,64},{1,65},{2,66},{3,67},{4,68},{5,69},{6,70},{7,71},{8,72},{9,... | collective-permute-start | bytes 602120 | tf_op jit(solution)/shard_map/ppermute | solution.py:298
  6.4 8.1 %collective-permute-start.3 = (f32[392,128]{1,0:T(8,128)S(1)}, f32[392,128]{1,0:T(8,128)S(1)}, u32[]{:S(2)}, u32[]{:S(2)}) collective-permute-start(f32[392,128]{1,0:T(8,128)S(1)} %get-tuple-element.16), channel_id=1, source_target_pairs={{0,192},{1,193},{2,194},{3,195},{4,196},{5,197},{6,198},{7,199},{8... | collective-permute-start | bytes 602120 | tf_op jit(solution)/shard_map/ppermute | solution.py:298
  7.9 9.8 %collective-permute-start.2 = (f32[392,128]{1,0:T(8,128)S(1)}, f32[392,128]{1,0:T(8,128)S(1)}, u32[]{:S(2)}, u32[]{:S(2)}) collective-permute-start(f32[392,128]{1,0:T(8,128)S(1)} %get-tuple-element.16), channel_id=1, source_target_pairs={{0,128},{1,129},{2,130},{3,131},{4,132},{5,133},{6,134},{7,135},{8... | collective-permute-start | bytes 602120 | tf_op jit(solution)/shard_map/ppermute | solution.py:298
  17.9 5.7 %collective-permute-start.7 = (f32[384,128]{1,0:T(8,128)S(1)}, f32[384,128]{1,0:T(8,128)S(1)}, u32[]{:S(2)}, u32[]{:S(2)}) collective-permute-start(f32[384,128]{1,0:T(8,128)S(1)} %get-tuple-element.17.refs_0_), channel_id=1, source_target_pairs={{0,32},{1,33},{2,34},{3,35},{4,36},{5,37},{6,38},{7,39},{8,40},{9,... | collective-permute-start | bytes 589832 | tf_op jit(solution)/shard_map/ppermute | solution.py:298
  19.8 2.0 %collective-permute-start.5 = (f32[128,128]{1,0:T(8,128)S(1)}, f32[128,128]{1,0:T(8,128)S(1)}, u32[]{:S(2)}, u32[]{:S(2)}) collective-permute-start(f32[128,128]{1,0:T(8,128)S(1)} %get-tuple-element.19), channel_id=1, source_target_pairs={{4,8},{5,9},{6,10},{7,11},{8,4},{9,5},{10,6},{11,7},{12,16},{13,17... | collective-permute-start | bytes 196616 | tf_op jit(solution)/shard_map/ppermute | solution.py:298
  20.4 1.4 %collective-permute-start.4 = (f32[96,128]{1,0:T(8,128)S(1)}, f32[96,128]{1,0:T(8,128)S(1)}, u32[]{:S(2)}, u32[]{:S(2)}) collective-permute-start(f32[96,128]{1,0:T(8,128)S(1)} %get-tuple-element.18), channel_id=1, source_target_pairs={{1,2},{2,1},{5,6},{6,5},{9,10},{10,9},{13,14},{14,13},{17,18},{18,... | collective-permute-start | bytes 147464 | tf_op jit(solution)/shard_map/ppermute | solution.py:298
  21.1 0.7 %collective-permute-start.6 = (f32[32,128]{1,0:T(8,128)S(1)}, f32[32,128]{1,0:T(8,128)S(1)}, u32[]{:S(2)}, u32[]{:S(2)}) collective-permute-start(f32[32,128]{1,0:T(8,128)S(1)} %get-tuple-element.20), channel_id=1, source_target_pairs={{5,10},{6,9},{9,6},{10,5},{13,18},{14,17},{17,14},{18,13},{21,26},... | collective-permute-start | bytes 49160 | tf_op jit(solution)/shard_map/ppermute | solution.py:298
  21.8 1.8 %collective-permute-start.9 = (f32[128,128]{1,0:T(8,128)S(1)}, f32[128,128]{1,0:T(8,128)S(1)}, u32[]{:S(2)}, u32[]{:S(2)}) collective-permute-start(f32[128,128]{1,0:T(8,128)S(1)} %collective-permute-done.5.refs_2_), channel_id=1, source_target_pairs={{0,32},{1,33},{2,34},{3,35},{4,36},{5,37},{6,38},{7,39},{8,40},{9,... | collective-permute-start | bytes 196616 | tf_op jit(solution)/shard_map/ppermute | solution.py:298
  21.9 1.7 %collective-permute-start.8 = (f32[96,128]{1,0:T(8,128)S(1)}, f32[96,128]{1,0:T(8,128)S(1)}, u32[]{:S(2)}, u32[]{:S(2)}) collective-permute-start(f32[96,128]{1,0:T(8,128)S(1)} %collective-permute-done.4.refs_1_), channel_id=1, source_target_pairs={{0,32},{1,33},{2,34},{3,35},{4,36},{5,37},{6,38},{7,39},{8,40},{9,... | collective-permute-start | bytes 147464 | tf_op jit(solution)/shard_map/ppermute | solution.py:298
  22.4 1.2 %collective-permute-start.10 = (f32[32,128]{1,0:T(8,128)S(1)}, f32[32,128]{1,0:T(8,128)S(1)}, u32[]{:S(2)}, u32[]{:S(2)}) collective-permute-start(f32[32,128]{1,0:T(8,128)S(1)} %collective-permute-done.6.refs_3_), channel_id=1, source_target_pairs={{0,32},{1,33},{2,34},{3,35},{4,36},{5,37},{6,38},{7,39},{8,40},{9,... | collective-permute-start | bytes 49160 | tf_op jit(solution)/shard_map/ppermute | solution.py:298
  28.4 14.3 %collective-permute-start.13 = (f32[64,128]{1,0:T(8,128)S(1)}, f32[64,128]{1,0:T(8,128)S(1)}, u32[]{:S(2)}, u32[]{:S(2)}) collective-permute-start(f32[64,128]{1,0:T(8,128)S(1)} %shard_map.71.refs_0_), channel_id=1, source_target_pairs={{0,192},{1,193},{2,194},{3,195},{4,196},{5,197},{6,198},{7,199},{8... | collective-permute-start | bytes 98312 | tf_op jit(solution)/shard_map/ppermute | solution.py:298
  41.2 4.3 %collective-permute-start.12 = (f32[64,128]{1,0:T(8,128)S(1)}, f32[64,128]{1,0:T(8,128)S(1)}, u32[]{:S(2)}, u32[]{:S(2)}) collective-permute-start(f32[64,128]{1,0:T(8,128)S(1)} %shard_map.71.refs_0_), channel_id=1, source_target_pairs={{0,128},{1,129},{2,130},{3,131},{4,132},{5,133},{6,134},{7,135},{8... | collective-permute-start | bytes 98312 | tf_op jit(solution)/shard_map/ppermute | solution.py:298
  41.2 6.0 %collective-permute-start.11 = (f32[64,128]{1,0:T(8,128)S(1)}, f32[64,128]{1,0:T(8,128)S(1)}, u32[]{:S(2)}, u32[]{:S(2)}) collective-permute-start(f32[64,128]{1,0:T(8,128)S(1)} %shard_map.71.refs_0_), channel_id=1, source_target_pairs={{0,64},{1,65},{2,66},{3,67},{4,68},{5,69},{6,70},{7,71},{8,72},{9,... | collective-permute-start | bytes 98312 | tf_op jit(solution)/shard_map/ppermute | solution.py:298
  41.9 5.4 %collective-permute-start.14 = (f32[64,128]{1,0:T(8,128)S(1)}, f32[64,128]{1,0:T(8,128)S(1)}, u32[]{:S(2)}, u32[]{:S(2)}) collective-permute-start(f32[64,128]{1,0:T(8,128)S(1)} %shard_map.71.refs_0_), channel_id=1, source_target_pairs={{0,32},{1,33},{2,34},{3,35},{4,36},{5,37},{6,38},{7,39},{8,40},{9,... | collective-permute-start | bytes 98312 | tf_op jit(solution)/shard_map/ppermute | solution.py:298
  42.8 4.5 %collective-permute-start.17 = (f32[64,128]{1,0:T(8,128)S(1)}, f32[64,128]{1,0:T(8,128)S(1)}, u32[]{:S(2)}, u32[]{:S(2)}) collective-permute-start(f32[64,128]{1,0:T(8,128)S(1)} %collective-permute-done.13.refs_3_), channel_id=1, source_target_pairs={{0,32},{1,33},{2,34},{3,35},{4,36},{5,37},{6,38},{7,39},{8,40},{9,... | collective-permute-start | bytes 98312 | tf_op jit(solution)/shard_map/ppermute | solution.py:298
  45.4 2.6 %collective-permute-start.16 = (f32[64,128]{1,0:T(8,128)S(1)}, f32[64,128]{1,0:T(8,128)S(1)}, u32[]{:S(2)}, u32[]{:S(2)}) collective-permute-start(f32[64,128]{1,0:T(8,128)S(1)} %collective-permute-done.12.refs_2_), channel_id=1, source_target_pairs={{0,32},{1,33},{2,34},{3,35},{4,36},{5,37},{6,38},{7,39},{8,40},{9,... | collective-permute-start | bytes 98312 | tf_op jit(solution)/shard_map/ppermute | solution.py:298
  47.2 1.2 %collective-permute-start.15 = (f32[64,128]{1,0:T(8,128)S(1)}, f32[64,128]{1,0:T(8,128)S(1)}, u32[]{:S(2)}, u32[]{:S(2)}) collective-permute-start(f32[64,128]{1,0:T(8,128)S(1)} %collective-permute-done.11.refs_1_), channel_id=1, source_target_pairs={{0,32},{1,33},{2,34},{3,35},{4,36},{5,37},{6,38},{7,39},{8,40},{9,... | collective-permute-start | bytes 98312 | tf_op jit(solution)/shard_map/ppermute | solution.py:298

commit v3 on v2

v3 whole, which is shorter than its diff:
```python
import functools

import jax
import jax.numpy as jnp
from jax import lax
from jax.experimental import pallas as pl
from jax.experimental.pallas import tpu as pltpu
from jax.sharding import PartitionSpec as P

TAPS = (0.0625, 0.25, 0.375, 0.25, 0.0625)
LUMA = (0.2126, 0.7152, 0.0722)
SIGMA_DEPTH = 0.5
SIGMA_NORMAL = 1.0
SIGMA_LUMA = 4.0
LUMA_FLOOR = 0.5
FAR = 1e30

TILE = 128
HALF = 64
RIM = 32
WIN = 96
BLK = 16
AXES = ("samp", "ty", "tx")


def place():
    samp = lax.axis_index("samp")
    ty = lax.axis_index("ty")
    tx = lax.axis_index("tx")
    core = lax.rem(samp, 2)
    y = samp // 2
    half_row = lax.rem(y // 2 + ty, 2)
    half_col = lax.rem(lax.rem(y + 1, 4) // 2 + tx, 2)
    return core, half_row, half_col, ty, tx


def luminance(c0, c1, c2):
    return LUMA[0] * c0 + LUMA[1] * c1 + LUMA[2] * c2


def rows(start, count):
    return pl.ds(start, count)


def aligned(value):
    return pl.multiple_of(value, 8)


def pack_kernel(rad, mom, nor, dep, cnt, keep, send, blocks, sems):
    core = place()[0]
    count = pltpu.make_async_copy(cnt.at[0], blocks, sems.at[8])
    count.start()

    def fill(colour_ref, normal_ref):
        copies = []
        for ch in range(4):
            at = rows(ch * TILE, TILE)
            colour, normal = (rad.at[0, ch], nor.at[0, ch]) if ch < 3 else (mom.at[0], dep.at[0])
            copies.append(pltpu.make_async_copy(colour, colour_ref.at[at, :], sems.at[ch]))
            copies.append(pltpu.make_async_copy(normal, normal_ref.at[at, :], sems.at[4 + ch]))
        for copy in copies:
            copy.start()
        for copy in copies:
            copy.wait()

    @pl.when(core == 0)
    def _():
        fill(keep, send)

    @pl.when(core == 1)
    def _():
        fill(send, keep)

    count.wait()
    number = blocks[...].astype(jnp.float32)
    for ref in (keep, send):
        ref[4 * TILE :, :] = jnp.zeros((8, TILE), jnp.float32)
        ref[4 * TILE :, 0:8] = number


def side_by_side(half_col, lane, left, right):
    return jnp.where(
        lane < HALF,
        jnp.where(half_col == 0, left, pltpu.roll(left, HALF, 1)),
        jnp.where(half_col == 0, pltpu.roll(right, HALF, 1), right),
    )


def pair_kernel(keep, recv, *outs):
    _, half_row, half_col, _, _ = place()
    lane = lax.broadcasted_iota(jnp.int32, (HALF, TILE), 1)
    flips = ((0, 0), (0, 1), (1, 1), (1, 0))
    counts = keep[4 * TILE :, :] + recv[4 * TILE :, :]
    for row in range(2):
        total = []
        for ch in range(4):
            at = rows(aligned(ch * TILE + HALF * (half_row if row == 0 else 1 - half_row)), HALF)
            total.append(keep[at, :] + recv[at, :])
        for k in range(4):
            if flips[k][0] == row:
                col = half_col if flips[k][1] == 0 else 1 - half_col
                for p in range(2):
                    outs[k][p * HALF : (p + 1) * HALF, :] = side_by_side(
                        col, lane, total[2 * p], total[2 * p + 1]
                    )
                outs[k][TILE:, :] = counts


def mean_kernel(own, r1, r2, r3, field, samples):
    core, half_row, half_col, _, _ = place()
    lane = lax.broadcasted_iota(jnp.int32, (8, TILE), 1)

    def total(at):
        return (own[at, :] + r1[at, :]) + (r2[at, :] + r3[at, :])

    blocks = total(rows(TILE, 8))
    spread = jnp.zeros((8, TILE), jnp.float32)
    for j in range(8):
        spread = jnp.where(lane // BLK == j, blocks[:, j : j + 1], spread)
    samples[...] = side_by_side(half_col, lane, spread, spread)
    wide = lax.broadcasted_iota(jnp.int32, (BLK, TILE), 1)
    for i in range(HALF // BLK):
        count = jnp.broadcast_to(samples[rows(4 * half_row + i, 1), :], (BLK, TILE))
        first, second = (total(rows(p * HALF + i * BLK, BLK)) / count for p in range(2))
        luma = luminance(first, pltpu.roll(first, HALF, 1), second)
        variance = jnp.maximum(second - jnp.square(pltpu.roll(luma, HALF, 1)), 0.0)
        second = jnp.where((core == 0) & (wide >= HALF), variance, second)
        field[rows(i * BLK, BLK), :] = first
        field[rows(HALF + i * BLK, BLK), :] = second


def in_order(core, mine, theirs):
    return (
        jnp.where(core == 0, mine[...], theirs[...]),
        jnp.where(core == 0, theirs[...], mine[...]),
    )


def column_kernel(mine, theirs, rim):
    core = place()[0]
    lane = lax.broadcasted_iota(jnp.int32, (HALF, TILE), 1)
    for g, field in enumerate(in_order(core, mine, theirs)):
        packed = jnp.zeros((HALF, TILE), jnp.float32)
        for ch in range(4):
            pair = field[(ch // 2) * HALF : (ch // 2 + 1) * HALF, :]
            by = TILE + 32 * ch - HALF * (ch % 2) - 32 * core
            packed = jnp.where(lane // 32 == ch, pltpu.roll(pair, lax.rem(by, TILE), 1), packed)
        rim[g * HALF : (g + 1) * HALF, :] = packed


def row_kernel(mine, theirs, side, other_side, window, rim):
    core, _, half_col, _, tx = place()
    lane = lax.broadcasted_iota(jnp.int32, (HALF, TILE), 1)
    is_left, is_right = lane < 32, lane >= 96
    outside = (is_left & (half_col == 0) & (tx == 0)) | (
        is_right & (half_col == 1) & (tx == lax.axis_size("tx") - 1)
    )
    left, right = in_order(core, side, other_side)
    for g, field in enumerate(in_order(core, mine, theirs)):
        lhs, rhs = (v[g * HALF : (g + 1) * HALF, :] for v in (left, right))
        for ch in range(4):
            pair = field[(ch // 2) * HALF : (ch // 2 + 1) * HALF, :]
            value = pltpu.roll(pair, 32 if ch % 2 == 0 else TILE - 32, 1)
            value = jnp.where(is_left, pltpu.roll(lhs, (TILE - 32 * ch) % TILE, 1), value)
            value = jnp.where(is_right, pltpu.roll(rhs, 96 - 32 * ch, 1), value)
            if g == 1 and ch == 3:
                value = jnp.where(outside, FAR, value * (1.0 / SIGMA_DEPTH))
            window[4 * g + ch] = value
    for f in range(8):
        rim[f] = window[f, rows(aligned(32 * core), RIM), :]


MOVES = (-16, -8, -4, -2, -1, 1, 2, 4, 8, 16)


def roll(value, by):
    return pltpu.roll(value, -by % TILE, 1)


def run_level(level, first, last, cur, geo, cur_moved, geo_moved, made, emit):
    dil = 2**level
    for r in range((first - 2 * dil) // 8 * 8, last + 2 * dil, 8):
        at = rows(r, 8)
        for b in (-2, -1, 1, 2):
            if (b * dil, r) not in made:
                made.add((b * dil, r))
                for f in range(4):
                    geo_moved[MOVES.index(b * dil), f, at, :] = roll(geo[f, at, :], b * dil)
            moved = [roll(cur[level, f, at, :], b * dil) for f in range(4)]
            moved.append(luminance(*moved[:3]))
            for f in range(5):
                cur_moved[level, b + 2, f, at, :] = moved[f]

    for r in range(first, last, 8):
        here = rows(r, 8)
        n0, n1, n2, depth = (geo[f, here, :] for f in range(4))
        luma = cur[level, 4, here, :]
        slope = -1.0 / (SIGMA_LUMA * jnp.sqrt(cur[level, 3, here, :]) + LUMA_FLOOR)
        sums = None
        for a in range(-2, 3):
            at = rows(r + a * dil, 8)
            for b in range(-2, 3):
                if b == 0:
                    g = [geo[f, at, :] for f in range(4)]
                    t = [cur[level, f, at, :] for f in range(5)]
                else:
                    g = [geo_moved[MOVES.index(b * dil), f, at, :] for f in range(4)]
                    t = [cur_moved[level, b + 2, f, at, :] for f in range(5)]
                e = jnp.abs(t[4] - luma) * slope - jnp.abs(g[3] - depth)
                e = e - jnp.square(g[0] - n0) - jnp.square(g[1] - n1)
                e = e - jnp.square(g[2] - n2)
                w = (TAPS[a + 2] * TAPS[b + 2]) * jnp.exp(e)
                parts = (w, w * t[0], w * t[1], w * t[2], w * w * t[3])
                sums = parts if sums is None else [p + q for p, q in zip(sums, parts)]
        inv = 1.0 / sums[0]
        emit(r, sums[1] * inv, sums[2] * inv, sums[3] * inv, sums[4] * (inv * inv))


def into(cur, level):
    def emit(r, c0, c1, c2, var):
        for f, value in enumerate((c0, c1, c2, var, luminance(c0, c1, c2))):
            cur[level, f, rows(r, 8), :] = value

    return emit


def place_rows(cur, geo, at, source):
    for f in range(4):
        cur[0, f, at, :] = source[f]
        geo[f, at, :] = source[4 + f]
    cur[0, 4, at, :] = luminance(source[0], source[1], source[2])


INNER = ((4, 60), (8, 56), (16, 48))
OUTER = (
    ((4, 36), (8, 40), (16, 48), (32, 64)),
    ((60, 92), (56, 88), (48, 80), (32, 64)),
)


def inner_kernel(body, near, middle, far, cur, geo, cur_moved, geo_moved):
    core = place()[0]
    place_rows(cur, geo, rows(0, HALF), body)
    made = set()
    for level, (first, last) in enumerate(INNER):
        run_level(
            level, first, last, cur, geo, cur_moved, geo_moved, made, into(cur, level + 1)
        )
    for f in range(5):
        near[f] = jnp.where(core == 0, cur[1, f, 4:12, :], cur[1, f, 52:60, :])
        middle[f] = jnp.where(core == 0, cur[2, f, 8:24, :], cur[2, f, 40:56, :])
        far[f] = cur[3, f, 16:48, :]


def outer_kernel(body, edge, near, middle, far, out, cur, geo, cur_moved, geo_moved):
    core, half_row, _, ty, _ = place()

    def work(this):
        outside = (half_row == this) & (ty == (lax.axis_size("ty") - 1 if this else 0))
        place_rows(cur, geo, rows(RIM * (1 - this), HALF), body)
        edge_at = rows(HALF * this, RIM)
        place_rows(cur, geo, edge_at, edge)
        geo[3, edge_at, :] = jnp.where(outside, FAR, edge[7])
        for f in range(5):
            cur[1, f, rows(52 if this else 36, 8), :] = near[f]
            cur[2, f, rows(40, 16), :] = middle[f]
            cur[3, f, rows(16 if this else 48, 32), :] = far[f]
        made = set()

        def finish(r, c0, c1, c2, var):
            lane = lax.broadcasted_iota(jnp.int32, (8, TILE), 1)
            for k, (p, q) in enumerate(((c0, c1), (c2, var))):
                out[rows(k * 32 + r - 32, 8), :] = jnp.where(lane < HALF, roll(p, 32), roll(q, -32))

        for level, (first, last) in enumerate(OUTER[this]):
            emit = into(cur, level + 1) if level < 3 else finish
            run_level(level, first, last, cur, geo, cur_moved, geo_moved, made, emit)

    for this in range(2):
        pl.when(core == this)(functools.partial(work, this))


def tile_kernel(*refs):
    ins, colour, variance = refs[:8], refs[8], refs[9]
    core, half_row, half_col, _, _ = place()
    lane = lax.broadcasted_iota(jnp.int32, (32, TILE), 1)
    low = lane < HALF
    for side in range(2):
        which = core if side == 0 else 1 - core
        for r in range(2):
            row = aligned(64 * (half_row if r == 0 else 1 - half_row) + 32 * which)
            near, other = (ins[side * 4 + k] for k in ((0, 1) if r == 0 else (3, 2)))
            for k in range(2):
                p, q = near[k * 32 : (k + 1) * 32, :], other[k * 32 : (k + 1) * 32, :]
                left = jnp.where(half_col == 0, p, q)
                right = jnp.where(half_col == 0, q, p)
                first = jnp.where(low, left, pltpu.roll(right, HALF, 1))
                second = jnp.where(low, pltpu.roll(left, HALF, 1), right)
                at = rows(row, 32)
                colour[2 * k, at, :] = first
                if k == 0:
                    colour[1, at, :] = second
                else:
                    variance[at, :] = second


def estimate(units, levels):
    taps = units * 25 * 8 * TILE
    return pl.CostEstimate(flops=27 * taps, transcendentals=taps, bytes_accessed=levels * 2**16)


def call(kernel, shapes, scratch=(), space=None, cost=None):
    return pl.pallas_call(
        kernel,
        **({"in_specs": [pl.BlockSpec(memory_space=pltpu.HBM)] * space} if space else {}),
        out_shape=[jax.ShapeDtypeStruct(s, jnp.float32) for s in shapes],
        scratch_shapes=list(scratch),
        **({"cost_estimate": estimate(*cost)} if cost else {}),
        compiler_params=pltpu.CompilerParams(vmem_limit_bytes=24 * 2**20),
    )


def run_filter(body, send_edge):
    edge = send_edge()

    def scratch(depth):
        return [
            pltpu.VMEM(shape, jnp.float32)
            for shape in (
                (4, 5, depth, TILE),
                (4, depth, TILE),
                (4, 5, 5, depth, TILE),
                (10, 4, depth, TILE),
            )
        ]

    inner = call(
        inner_kernel, [(5, 8, TILE), (5, 16, TILE), (5, 32, TILE)], scratch(HALF), cost=(17, 3)
    )(body)
    return call(outer_kernel, [(HALF, TILE)], scratch(WIN), cost=(16, 4))(body, edge, *inner)[0]


def pairs(sizes, partner):
    n_samp, n_ty, n_tx = sizes
    out = []
    for samp in range(n_samp):
        for ty in range(n_ty):
            for tx in range(n_tx):
                to = partner(samp, ty, tx)
                if 0 <= to[1] < n_ty and 0 <= to[2] < n_tx:
                    out.append(
                        ((samp * n_ty + ty) * n_tx + tx, (to[0] * n_ty + to[1]) * n_tx + to[2])
                    )
    return out


def beside(samp, ty, tx):
    y, core = samp // 2, samp % 2
    half_col = ((y + 1) % 4 // 2 + tx) % 2
    if half_col == core:
        return samp ^ 1, ty, tx + (1 if core else -1)
    return samp ^ 3, ty, tx


def above(samp, ty, tx):
    y, core = samp // 2, samp % 2
    half_row = (y // 2 + ty) % 2
    if half_row == core:
        return samp ^ 1, ty + (1 if core else -1), tx
    return samp ^ 7, ty, tx


def per_device(sizes, radiance, moment, normal, depth_sum, counts):
    def send(value, partner):
        return lax.ppermute(value, AXES, pairs(sizes, partner))

    def other_core(value):
        return send(value, lambda s, ty, tx: (s ^ 1, ty, tx))

    def other_y(value, k):
        return send(value, lambda s, ty, tx: (s ^ (2 * k), ty, tx))

    packed = (4 * TILE + 8, TILE)
    keep, give = call(
        pack_kernel,
        [packed, packed],
        [pltpu.VMEM((8, 8), jnp.int32), pltpu.SemaphoreType.DMA((9,))],
        5,
    )(
        *(
            pltpu.with_memory_space_constraint(value, pltpu.HBM)
            for value in (radiance, moment, normal, depth_sum, counts)
        )
    )
    quarter = (TILE + 8, TILE)
    parts = list(call(pair_kernel, [quarter] * 4)(keep, other_core(give)))
    parts = parts[:1] + [other_y(parts[k], k) for k in (1, 2, 3)]
    (mine,) = call(mean_kernel, [(TILE, TILE)], [pltpu.VMEM((8, TILE), jnp.float32)])(*parts)
    theirs = other_core(mine)
    (rim,) = call(column_kernel, [(TILE, TILE)])(mine, theirs)
    rim = send(rim, beside)
    body, edge = call(row_kernel, [(8, HALF, TILE), (8, RIM, TILE)])(
        mine, theirs, rim, other_core(rim)
    )
    done = run_filter(body, lambda: send(edge, above))
    got = [done] + [other_y(done, k) for k in (1, 2, 3)]
    theirs = [other_core(g) for g in got]
    return tuple(call(tile_kernel, [(3, TILE, TILE), (TILE, TILE)])(*got, *theirs))


def solution(mesh):
    sizes = tuple(mesh.shape[axis] for axis in AXES)
    placed = (
        P("samp", None, "ty", "tx"),
        P("samp", "ty", "tx"),
        P("samp", None, "ty", "tx"),
        P("samp", "ty", "tx"),
        P("samp", "ty", "tx"),
    )
    return jax.shard_map(
        functools.partial(per_device, sizes),
        mesh=mesh,
        in_specs=placed,
        out_specs=(P(None, "ty", "tx"), P("ty", "tx")),
        check_vma=False,
    )
```

time: 49.5 us -> 43.2 us (0.87)
  starting transfers between devices: 28.2 us -> 20.3 us
  waiting for transfers between devices: 13.2 us -> 14.4 us
    ppermute x18 -> x15, starting transfers between devices: 28.2 us -> 20.3 us  [send(): return lax.ppermute(value, AXES, pairs(sizes, partner))]
    ppermute x18 -> x15, waiting for transfers between devices: 13.2 us -> 14.4 us  [send(): return lax.ppermute(value, AXES, pairs(sizes, partner))]
    pallas_call x3 -> x6, Pallas kernels: 5.12 us -> 5.61 us  [the longest x1 2.52 us: run_filter(): call(inner_kernel, [(5, 8, TILE), (5, 16, TILE), (5, 32, TILE)], scratch(...]
  transfers between devices with their start and end apart: 18 -> 15, of which waited for: 8 -> 11; matrix products, arithmetic and copies ran while one was open for 0% -> 0% of each run, Pallas kernels for 0% -> 6%
where the time goes in v3:
time: 43.2 us; the launch traced here: 43 us
  starting transfers between devices  20.3 us (47%)
  waiting for transfers between devices  14.4 us (33%)
  Pallas kernels  7.61 us (18%)
  between operations  0.71 us (2%)
    ppermute x15, starting transfers between devices, send(): return lax.ppermute(value, AXES, pairs(sizes, partner))  20.3 us
    ppermute x15, waiting for transfers between devices, send(): return lax.ppermute(value, AXES, pairs(sizes, partner))  14.4 us
    pallas_call x1, Pallas kernels, run_filter(): call(inner_kernel, [(5, 8, TILE), (5, 16, TILE), (5, 32, TILE)], scratch(...  2.52 us
    pallas_call x1, Pallas kernels, run_filter(): call(outer_kernel, [(HALF, TILE)], scratch(WIN), cost=(16, 4))  2.25 us
    pallas_call x1, Pallas kernels, per_device(): call(pack_kernel, [packed, packed], [pltpu.VMEM((8, 8), jnp.int32), pltpu...  1.17 us
  transfers between devices with their start and end apart: 15, of which 11 were waited for; matrix products, arithmetic and copies ran while one was open for 0% of the time, Pallas kernels for 6%

profile of v3, /device:TPU:1, one launch (start us, length us, event | category | flops | bytes accessed | tf_op | source)
XLA Modules:
  0.0 43.0 jit_solution(14664444403612203356)
XLA Ops:
  0.6 1.2 %shard_map.68 = (f32[520,128]{1,0:T(8,128)S(1)}, f32[520,128]{1,0:T(8,128)S(1)}) custom-call(f32[1,3,128,128]{3,2,1,0:T(8,128)} %rad.1, f32[1,128,128]{2,1,0:T(8,128)} %mom.1, f32[1,3,128,128]{3,2,1,0:T(8,128)} %nor.1, f32[1,128,128]{2,1,0:T(8,128)} %dep.1, s32[1,8,8]{2,1,0:T(8,128)} %cnt.1), custom_call_target="tpu_custom_call" | custom-call | tf_op jit(solution)/shard_map/pallas_call | solution.py:384
  1.8 3.3 %collective-permute-start = (f32[520,128]{1,0:T(8,128)S(1)}, f32[520,128]{1,0:T(8,128)S(1)}, u32[]{:S(2)}, u32[]{:S(2)}) collective-permute-start(f32[520,128]{1,0:T(8,128)S(1)} %get-tuple-element.14), channel_id=1, source_target_pairs={{0,32},{1,33},{2,34},{3,35},{4,36},{5,37},{6,38},{7,39},{8,40},{9,... | collective-permute-start | bytes 798728 | tf_op jit(solution)/shard_map/ppermute | solution.py:375
  5.1 1.2 %collective-permute-done.recv = f32[520,128]{1,0:T(8,128)S(1)} collective-permute-done((f32[520,128]{1,0:T(8,128)S(1)}, f32[520,128]{1,0:T(8,128)S(1)}, u32[]{:S(2)}, u32[]{:S(2)}) %collective-permute-start) | collective-permute-done | bytes 266272 | tf_op jit(solution)/shard_map/ppermute | solution.py:375
  6.5 2.2 %collective-permute-start.2 = (f32[136,128]{1,0:T(8,128)S(1)}, f32[136,128]{1,0:T(8,128)S(1)}, u32[]{:S(2)}, u32[]{:S(2)}) collective-permute-start(f32[136,128]{1,0:T(8,128)S(1)} %get-tuple-element.17), channel_id=1, source_target_pairs={{0,128},{1,129},{2,130},{3,131},{4,132},{5,133},{6,134},{7,135},{8... | collective-permute-start | bytes 208904 | tf_op jit(solution)/shard_map/ppermute | solution.py:375
  8.7 1.7 %collective-permute-start.3 = (f32[136,128]{1,0:T(8,128)S(1)}, f32[136,128]{1,0:T(8,128)S(1)}, u32[]{:S(2)}, u32[]{:S(2)}) collective-permute-start(f32[136,128]{1,0:T(8,128)S(1)} %get-tuple-element.18), channel_id=1, source_target_pairs={{0,192},{1,193},{2,194},{3,195},{4,196},{5,197},{6,198},{7,199},{8... | collective-permute-start | bytes 208904 | tf_op jit(solution)/shard_map/ppermute | solution.py:375
  10.4 1.9 %collective-permute-done.2.r2 = f32[136,128]{1,0:T(8,128)S(1)} collective-permute-done((f32[136,128]{1,0:T(8,128)S(1)}, f32[136,128]{1,0:T(8,128)S(1)}, u32[]{:S(2)}, u32[]{:S(2)}) %collective-permute-start.2) | collective-permute-done | bytes 69664 | tf_op jit(solution)/shard_map/ppermute | solution.py:375
  12.3 1.1 %collective-permute-done.3.r3 = f32[136,128]{1,0:T(8,128)S(1)} collective-permute-done((f32[136,128]{1,0:T(8,128)S(1)}, f32[136,128]{1,0:T(8,128)S(1)}, u32[]{:S(2)}, u32[]{:S(2)}) %collective-permute-start.3) | collective-permute-done | bytes 69664 | tf_op jit(solution)/shard_map/ppermute | solution.py:375
  13.8 1.7 %collective-permute-start.4 = (f32[128,128]{1,0:T(8,128)S(1)}, f32[128,128]{1,0:T(8,128)S(1)}, u32[]{:S(2)}, u32[]{:S(2)}) collective-permute-start(f32[128,128]{1,0:T(8,128)S(1)} %shard_map.70.mine), channel_id=1, source_target_pairs={{0,32},{1,33},{2,34},{3,35},{4,36},{5,37},{6,38},{7,39},{8,40},{9,... | collective-permute-start | bytes 196616 | tf_op jit(solution)/shard_map/ppermute | solution.py:375
  15.5 0.9 %collective-permute-done.4.theirs = f32[128,128]{1,0:T(8,128)S(1)} collective-permute-done((f32[128,128]{1,0:T(8,128)S(1)}, f32[128,128]{1,0:T(8,128)S(1)}, u32[]{:S(2)}, u32[]{:S(2)}) %collective-permute-start.4) | collective-permute-done | bytes 65568 | tf_op jit(solution)/shard_map/ppermute | solution.py:375
  16.6 1.9 %collective-permute-start.5 = (f32[128,128]{1,0:T(8,128)S(1)}, f32[128,128]{1,0:T(8,128)S(1)}, u32[]{:S(2)}, u32[]{:S(2)}) collective-permute-start(f32[128,128]{1,0:T(8,128)S(1)} %shard_map.71), channel_id=1, source_target_pairs={{1,97},{2,33},{3,99},{5,101},{6,37},{7,103},{9,105},{10,41},{11,10... | collective-permute-start | bytes 196616 | tf_op jit(solution)/shard_map/ppermute | solution.py:375
  18.5 3.7 %collective-permute-done.5.side = f32[128,128]{1,0:T(8,128)S(1)} collective-permute-done((f32[128,128]{1,0:T(8,128)S(1)}, f32[128,128]{1,0:T(8,128)S(1)}, u32[]{:S(2)}, u32[]{:S(2)}) %collective-permute-start.5) | collective-permute-done | bytes 65568 | tf_op jit(solution)/shard_map/ppermute | solution.py:375
  22.2 1.3 %collective-permute-done.6.other_side = f32[128,128]{1,0:T(8,128)S(1)} collective-permute-done((f32[128,128]{1,0:T(8,128)S(1)}, f32[128,128]{1,0:T(8,128)S(1)}, u32[]{:S(2)}, u32[]{:S(2)}) %collective-permute-start.6) | collective-permute-done | bytes 65568 | tf_op jit(solution)/shard_map/ppermute | solution.py:375
  23.7 3.6 %collective-permute-start.7 = (f32[8,32,128]{2,1,0:T(8,128)S(1)}, f32[8,32,128]{2,1,0:T(8,128)S(1)}, u32[]{:S(2)}, u32[]{:S(2)}) collective-permute-start(f32[8,32,128]{2,1,0:T(8,128)S(1)} %get-tuple-element.20), channel_id=1, source_target_pairs={{4,228},{5,229},{6,230},{7,231},{8,36},{9,37},{10,38},{11,39},{12,... | collective-permute-start | bytes 393224 | tf_op jit(solution)/shard_map/ppermute | solution.py:375
  27.3 2.5 %shard_map.73 = (f32[5,8,128]{2,1,0:T(8,128)S(1)}, f32[5,16,128]{2,1,0:T(8,128)S(1)}, f32[5,32,128]{2,1,0:T(8,128)S(1)}) custom-call(f32[8,64,128]{2,1,0:T(8,128)S(1)} %get-tuple-element.19.body), custom_call_target="tpu_custom_call" | custom-call | flops 11750400 | bytes 196608 | tf_op jit(solution)/shard_map/pallas_call | solution.py:337
  29.8 1.3 %collective-permute-done.7.edge = f32[8,32,128]{2,1,0:T(8,128)S(1)} collective-permute-done((f32[8,32,128]{2,1,0:T(8,128)S(1)}, f32[8,32,128]{2,1,0:T(8,128)S(1)}, u32[]{:S(2)}, u32[]{:S(2)}) %collective-permute-start.7) | collective-permute-done | bytes 131104 | tf_op jit(solution)/shard_map/ppermute | solution.py:375
  31.2 2.3 %shard_map.74.refs_0_ = f32[64,128]{1,0:T(8,128)S(1)} custom-call(f32[8,64,128]{2,1,0:T(8,128)S(1)} %get-tuple-element.19.body, f32[8,32,128]{2,1,0:T(8,128)S(1)} %collective-permute-done.7.edge, f32[5,8,128]{2,1,0:T(8,128)S(1)} %get-tuple-element.21.near, f32[5,16,128]{2,1,0:T(8,128)S(1)} %get-tuple-element.22.middle, f32[5,32,128]{2,1,0:T(8,128)S(1)} %get-tuple-element.23.far), custom_call_target="tpu_custom_call" | custom-call | flops 11059200 | bytes 262144 | tf_op jit(solution)/shard_map/pallas_call | solution.py:340
  33.4 0.8 %collective-permute-start.10 = (f32[64,128]{1,0:T(8,128)S(1)}, f32[64,128]{1,0:T(8,128)S(1)}, u32[]{:S(2)}, u32[]{:S(2)}) collective-permute-start(f32[64,128]{1,0:T(8,128)S(1)} %shard_map.74.refs_0_), channel_id=1, source_target_pairs={{0,192},{1,193},{2,194},{3,195},{4,196},{5,197},{6,198},{7,199},{8... | collective-permute-start | bytes 98312 | tf_op jit(solution)/shard_map/ppermute | solution.py:375
  34.2 2.5 %collective-permute-start.8 = (f32[64,128]{1,0:T(8,128)S(1)}, f32[64,128]{1,0:T(8,128)S(1)}, u32[]{:S(2)}, u32[]{:S(2)}) collective-permute-start(f32[64,128]{1,0:T(8,128)S(1)} %shard_map.74.refs_0_), channel_id=1, source_target_pairs={{0,64},{1,65},{2,66},{3,67},{4,68},{5,69},{6,70},{7,71},{8,72},{9,... | collective-permute-start | bytes 98312 | tf_op jit(solution)/shard_map/ppermute | solution.py:375
  36.7 0.7 %collective-permute-done.10.refs_3_ = f32[64,128]{1,0:T(8,128)S(1)} collective-permute-done((f32[64,128]{1,0:T(8,128)S(1)}, f32[64,128]{1,0:T(8,128)S(1)}, u32[]{:S(2)}, u32[]{:S(2)}) %collective-permute-start.10) | collective-permute-done | bytes 32800 | tf_op jit(solution)/shard_map/ppermute | solution.py:375
  37.5 1.1 %collective-permute-done.9.refs_2_ = f32[64,128]{1,0:T(8,128)S(1)} collective-permute-done((f32[64,128]{1,0:T(8,128)S(1)}, f32[64,128]{1,0:T(8,128)S(1)}, u32[]{:S(2)}, u32[]{:S(2)}) %collective-permute-start.9) | collective-permute-done | bytes 32800 | tf_op jit(solution)/shard_map/ppermute | solution.py:375
  38.5 2.5 %collective-permute-start.13 = (f32[64,128]{1,0:T(8,128)S(1)}, f32[64,128]{1,0:T(8,128)S(1)}, u32[]{:S(2)}, u32[]{:S(2)}) collective-permute-start(f32[64,128]{1,0:T(8,128)S(1)} %collective-permute-done.9.refs_2_), channel_id=1, source_target_pairs={{0,32},{1,33},{2,34},{3,35},{4,36},{5,37},{6,38},{7,39},{8,40},{9,... | collective-permute-start | bytes 98312 | tf_op jit(solution)/shard_map/ppermute | solution.py:375
  41.0 0.8 %collective-permute-done.13.refs_6_ = f32[64,128]{1,0:T(8,128)S(1)} collective-permute-done((f32[64,128]{1,0:T(8,128)S(1)}, f32[64,128]{1,0:T(8,128)S(1)}, u32[]{:S(2)}, u32[]{:S(2)}) %collective-permute-start.13) | collective-permute-done | bytes 32800 | tf_op jit(solution)/shard_map/ppermute | solution.py:375
  41.8 0.4 collective-permute-done.12.refs_5_
  42.2 0.8 %shard_map.75 = (f32[3,128,128]{2,1,0:T(8,128)}, f32[128,128]{1,0:T(8,128)}) custom-call(f32[64,128]{1,0:T(8,128)S(1)} %shard_map.74.refs_0_, f32[64,128]{1,0:T(8,128)S(1)} %collective-permute-done.8.refs_1_, f32[64,128]{1,0:T(8,128)S(1)} %collective-permute-done.9.refs_2_, f32[64,128]{1,0:T(8,128)S(1)} %collective-permute-done.10.refs_3_, ...), custom_call_target="tpu_custom_call" | custom-call | tf_op jit(solution)/shard_map/pallas_call | solution.py:408
  (14 shorter events, 1.0 us)
Async XLA Ops:
  1.8 4.5 %collective-permute-start = (f32[520,128]{1,0:T(8,128)S(1)}, f32[520,128]{1,0:T(8,128)S(1)}, u32[]{:S(2)}, u32[]{:S(2)}) collective-permute-start(f32[520,128]{1,0:T(8,128)S(1)} %get-tuple-element.14), channel_id=1, source_target_pairs={{0,32},{1,33},{2,34},{3,35},{4,36},{5,37},{6,38},{7,39},{8,40},{9,... | collective-permute-start | bytes 798728 | tf_op jit(solution)/shard_map/ppermute | solution.py:375
  6.4 3.9 %collective-permute-start.1 = (f32[136,128]{1,0:T(8,128)S(1)}, f32[136,128]{1,0:T(8,128)S(1)}, u32[]{:S(2)}, u32[]{:S(2)}) collective-permute-start(f32[136,128]{1,0:T(8,128)S(1)} %get-tuple-element.16), channel_id=1, source_target_pairs={{0,64},{1,65},{2,66},{3,67},{4,68},{5,69},{6,70},{7,71},{8,72},{9,... | collective-permute-start | bytes 208904 | tf_op jit(solution)/shard_map/ppermute | solution.py:375
  6.5 5.8 %collective-permute-start.2 = (f32[136,128]{1,0:T(8,128)S(1)}, f32[136,128]{1,0:T(8,128)S(1)}, u32[]{:S(2)}, u32[]{:S(2)}) collective-permute-start(f32[136,128]{1,0:T(8,128)S(1)} %get-tuple-element.17), channel_id=1, source_target_pairs={{0,128},{1,129},{2,130},{3,131},{4,132},{5,133},{6,134},{7,135},{8... | collective-permute-start | bytes 208904 | tf_op jit(solution)/shard_map/ppermute | solution.py:375
  8.7 4.8 %collective-permute-start.3 = (f32[136,128]{1,0:T(8,128)S(1)}, f32[136,128]{1,0:T(8,128)S(1)}, u32[]{:S(2)}, u32[]{:S(2)}) collective-permute-start(f32[136,128]{1,0:T(8,128)S(1)} %get-tuple-element.18), channel_id=1, source_target_pairs={{0,192},{1,193},{2,194},{3,195},{4,196},{5,197},{6,198},{7,199},{8... | collective-permute-start | bytes 208904 | tf_op jit(solution)/shard_map/ppermute | solution.py:375
  13.8 2.6 %collective-permute-start.4 = (f32[128,128]{1,0:T(8,128)S(1)}, f32[128,128]{1,0:T(8,128)S(1)}, u32[]{:S(2)}, u32[]{:S(2)}) collective-permute-start(f32[128,128]{1,0:T(8,128)S(1)} %shard_map.70.mine), channel_id=1, source_target_pairs={{0,32},{1,33},{2,34},{3,35},{4,36},{5,37},{6,38},{7,39},{8,40},{9,... | collective-permute-start | bytes 196616 | tf_op jit(solution)/shard_map/ppermute | solution.py:375
  16.6 5.6 %collective-permute-start.5 = (f32[128,128]{1,0:T(8,128)S(1)}, f32[128,128]{1,0:T(8,128)S(1)}, u32[]{:S(2)}, u32[]{:S(2)}) collective-permute-start(f32[128,128]{1,0:T(8,128)S(1)} %shard_map.71), channel_id=1, source_target_pairs={{1,97},{2,33},{3,99},{5,101},{6,37},{7,103},{9,105},{10,41},{11,10... | collective-permute-start | bytes 196616 | tf_op jit(solution)/shard_map/ppermute | solution.py:375
  22.2 1.3 %collective-permute-start.6 = (f32[128,128]{1,0:T(8,128)S(1)}, f32[128,128]{1,0:T(8,128)S(1)}, u32[]{:S(2)}, u32[]{:S(2)}) collective-permute-start(f32[128,128]{1,0:T(8,128)S(1)} %collective-permute-done.5.side), channel_id=1, source_target_pairs={{0,32},{1,33},{2,34},{3,35},{4,36},{5,37},{6,38},{7,39},{8,40},{9,... | collective-permute-start | bytes 196616 | tf_op jit(solution)/shard_map/ppermute | solution.py:375
  23.7 7.5 %collective-permute-start.7 = (f32[8,32,128]{2,1,0:T(8,128)S(1)}, f32[8,32,128]{2,1,0:T(8,128)S(1)}, u32[]{:S(2)}, u32[]{:S(2)}) collective-permute-start(f32[8,32,128]{2,1,0:T(8,128)S(1)} %get-tuple-element.20), channel_id=1, source_target_pairs={{4,228},{5,229},{6,230},{7,231},{8,36},{9,37},{10,38},{11,39},{12,... | collective-permute-start | bytes 393224 | tf_op jit(solution)/shard_map/ppermute | solution.py:375
  33.4 4.0 %collective-permute-start.10 = (f32[64,128]{1,0:T(8,128)S(1)}, f32[64,128]{1,0:T(8,128)S(1)}, u32[]{:S(2)}, u32[]{:S(2)}) collective-permute-start(f32[64,128]{1,0:T(8,128)S(1)} %shard_map.74.refs_0_), channel_id=1, source_target_pairs={{0,192},{1,193},{2,194},{3,195},{4,196},{5,197},{6,198},{7,199},{8... | collective-permute-start | bytes 98312 | tf_op jit(solution)/shard_map/ppermute | solution.py:375
  34.2 4.3 %collective-permute-start.9 = (f32[64,128]{1,0:T(8,128)S(1)}, f32[64,128]{1,0:T(8,128)S(1)}, u32[]{:S(2)}, u32[]{:S(2)}) collective-permute-start(f32[64,128]{1,0:T(8,128)S(1)} %shard_map.74.refs_0_), channel_id=1, source_target_pairs={{0,128},{1,129},{2,130},{3,131},{4,132},{5,133},{6,134},{7,135},{8... | collective-permute-start | bytes 98312 | tf_op jit(solution)/shard_map/ppermute | solution.py:375
  34.2 6.7 %collective-permute-start.8 = (f32[64,128]{1,0:T(8,128)S(1)}, f32[64,128]{1,0:T(8,128)S(1)}, u32[]{:S(2)}, u32[]{:S(2)}) collective-permute-start(f32[64,128]{1,0:T(8,128)S(1)} %shard_map.74.refs_0_), channel_id=1, source_target_pairs={{0,64},{1,65},{2,66},{3,67},{4,68},{5,69},{6,70},{7,71},{8,72},{9,... | collective-permute-start | bytes 98312 | tf_op jit(solution)/shard_map/ppermute | solution.py:375
  36.7 4.3 %collective-permute-start.11 = (f32[64,128]{1,0:T(8,128)S(1)}, f32[64,128]{1,0:T(8,128)S(1)}, u32[]{:S(2)}, u32[]{:S(2)}) collective-permute-start(f32[64,128]{1,0:T(8,128)S(1)} %shard_map.74.refs_0_), channel_id=1, source_target_pairs={{0,32},{1,33},{2,34},{3,35},{4,36},{5,37},{6,38},{7,39},{8,40},{9,... | collective-permute-start | bytes 98312 | tf_op jit(solution)/shard_map/ppermute | solution.py:375
  37.5 3.5 %collective-permute-start.14 = (f32[64,128]{1,0:T(8,128)S(1)}, f32[64,128]{1,0:T(8,128)S(1)}, u32[]{:S(2)}, u32[]{:S(2)}) collective-permute-start(f32[64,128]{1,0:T(8,128)S(1)} %collective-permute-done.10.refs_3_), channel_id=1, source_target_pairs={{0,32},{1,33},{2,34},{3,35},{4,36},{5,37},{6,38},{7,39},{8,40},{9,... | collective-permute-start | bytes 98312 | tf_op jit(solution)/shard_map/ppermute | solution.py:375
  38.5 3.3 %collective-permute-start.13 = (f32[64,128]{1,0:T(8,128)S(1)}, f32[64,128]{1,0:T(8,128)S(1)}, u32[]{:S(2)}, u32[]{:S(2)}) collective-permute-start(f32[64,128]{1,0:T(8,128)S(1)} %collective-permute-done.9.refs_2_), channel_id=1, source_target_pairs={{0,32},{1,33},{2,34},{3,35},{4,36},{5,37},{6,38},{7,39},{8,40},{9,... | collective-permute-start | bytes 98312 | tf_op jit(solution)/shard_map/ppermute | solution.py:375
  41.0 1.2 %collective-permute-start.12 = (f32[64,128]{1,0:T(8,128)S(1)}, f32[64,128]{1,0:T(8,128)S(1)}, u32[]{:S(2)}, u32[]{:S(2)}) collective-permute-start(f32[64,128]{1,0:T(8,128)S(1)} %collective-permute-done.8.refs_1_), channel_id=1, source_target_pairs={{0,32},{1,33},{2,34},{3,35},{4,36},{5,37},{6,38},{7,39},{8,40},{9,... | collective-permute-start | bytes 98312 | tf_op jit(solution)/shard_map/ppermute | solution.py:375

commit v4 on v3

--- a/solution.py
+++ b/solution.py
@@ -34,6 +34,10 @@
     return core, half_row, half_col, ty, tx
 
 
+def edge_of(core, half_row):
+    return lax.rem(core + half_row, 2)
+
+
 def luminance(c0, c1, c2):
     return LUMA[0] * c0 + LUMA[1] * c1 + LUMA[2] * c2
 
@@ -46,44 +50,34 @@
     return pl.multiple_of(value, 8)
 
 
-def pack_kernel(rad, mom, nor, dep, cnt, keep, send, blocks, sems):
+def pick_kernel(wanted, rad, mom, nor, dep, cnt, picked, blocks, sems):
     core = place()[0]
-    count = pltpu.make_async_copy(cnt.at[0], blocks, sems.at[8])
+    count = pltpu.make_async_copy(cnt.at[0], blocks, sems.at[4])
     count.start()
 
-    def fill(colour_ref, normal_ref):
+    def fill(first, last):
         copies = []
         for ch in range(4):
-            at = rows(ch * TILE, TILE)
-            colour, normal = (rad.at[0, ch], nor.at[0, ch]) if ch < 3 else (mom.at[0], dep.at[0])
-            copies.append(pltpu.make_async_copy(colour, colour_ref.at[at, :], sems.at[ch]))
-            copies.append(pltpu.make_async_copy(normal, normal_ref.at[at, :], sems.at[4 + ch]))
+            source = first.at[0, ch] if ch < 3 else last.at[0]
+            copies.append(
+                pltpu.make_async_copy(source, picked.at[rows(ch * TILE, TILE), :], sems.at[ch])
+            )
         for copy in copies:
             copy.start()
         for copy in copies:
             copy.wait()
 
-    @pl.when(core == 0)
+    @pl.when(core == wanted)
     def _():
-        fill(keep, send)
-
-    @pl.when(core == 1)
+        fill(rad, mom)
+
+    @pl.when(core != wanted)
     def _():
-        fill(send, keep)
+        fill(nor, dep)
 
     count.wait()
-    number = blocks[...].astype(jnp.float32)
-    for ref in (keep, send):
-        ref[4 * TILE :, :] = jnp.zeros((8, TILE), jnp.float32)
-        ref[4 * TILE :, 0:8] = number
-
-
-def side_by_side(half_col, lane, left, right):
-    return jnp.where(
-        lane < HALF,
-        jnp.where(half_col == 0, left, pltpu.roll(left, HALF, 1)),
-        jnp.where(half_col == 0, pltpu.roll(right, HALF, 1), right),
-    )
+    picked[4 * TILE :, :] = jnp.zeros((8, TILE), jnp.float32)
+    picked[4 * TILE :, 0:8] = blocks[...].astype(jnp.float32)
 
 
 def pair_kernel(keep, recv, *outs):
@@ -96,37 +90,44 @@
         for ch in range(4):
             at = rows(aligned(ch * TILE + HALF * (half_row if row == 0 else 1 - half_row)), HALF)
             total.append(keep[at, :] + recv[at, :])
+        moved = [pltpu.roll(total[3], 96 - 32 * p, 1) for p in range(3)]
         for k in range(4):
             if flips[k][0] == row:
                 col = half_col if flips[k][1] == 0 else 1 - half_col
-                for p in range(2):
-                    outs[k][p * HALF : (p + 1) * HALF, :] = side_by_side(
-                        col, lane, total[2 * p], total[2 * p + 1]
-                    )
-                outs[k][TILE:, :] = counts
-
-
-def mean_kernel(own, r1, r2, r3, field, samples):
+                free = lane // 32 == 3 - 3 * col
+                for p in range(3):
+                    outs[k][p * HALF : (p + 1) * HALF, :] = jnp.where(free, moved[p], total[p])
+                outs[k][3 * HALF :, :] = counts
+
+
+def mean_kernel(own, r1, r2, r3, field, rim, samples):
     core, half_row, half_col, _, _ = place()
     lane = lax.broadcasted_iota(jnp.int32, (8, TILE), 1)
 
     def total(at):
         return (own[at, :] + r1[at, :]) + (r2[at, :] + r3[at, :])
 
-    blocks = total(rows(TILE, 8))
+    blocks = total(rows(3 * HALF, 8))
     spread = jnp.zeros((8, TILE), jnp.float32)
     for j in range(8):
         spread = jnp.where(lane // BLK == j, blocks[:, j : j + 1], spread)
-    samples[...] = side_by_side(half_col, lane, spread, spread)
-    wide = lax.broadcasted_iota(jnp.int32, (BLK, TILE), 1)
+    samples[...] = spread
+    group = lax.broadcasted_iota(jnp.int32, (BLK, TILE), 1) // 32
     for i in range(HALF // BLK):
         count = jnp.broadcast_to(samples[rows(4 * half_row + i, 1), :], (BLK, TILE))
-        first, second = (total(rows(p * HALF + i * BLK, BLK)) / count for p in range(2))
-        luma = luminance(first, pltpu.roll(first, HALF, 1), second)
-        variance = jnp.maximum(second - jnp.square(pltpu.roll(luma, HALF, 1)), 0.0)
-        second = jnp.where((core == 0) & (wide >= HALF), variance, second)
-        field[rows(i * BLK, BLK), :] = first
-        field[rows(HALF + i * BLK, BLK), :] = second
+        sums = [total(rows(p * HALF + i * BLK, BLK)) for p in range(3)]
+        last = sums[0]
+        for p in range(3):
+            last = jnp.where(group == p + half_col, pltpu.roll(sums[p], 32 * p + 32, 1), last)
+        mean = [value / count for value in (*sums, last)]
+        variance = jnp.maximum(mean[3] - jnp.square(luminance(*mean[:3])), 0.0)
+        mean[3] = jnp.where(core == 0, variance, mean[3])
+        packed = jnp.zeros((BLK, TILE), jnp.float32)
+        for ch in range(4):
+            field[rows(ch * HALF + i * BLK, BLK), :] = mean[ch]
+            moved = pltpu.roll(mean[ch], lax.rem(32 * ch + 32 * half_col, TILE), 1)
+            packed = jnp.where(group == ch, moved, packed)
+        rim[rows(i * BLK, BLK), :] = packed
 
 
 def in_order(core, mine, theirs):
@@ -136,38 +137,23 @@
     )
 
 
-def column_kernel(mine, theirs, rim):
-    core = place()[0]
+def row_kernel(mine, theirs, side, other_side, window, edge):
+    core, half_row, half_col, _, tx = place()
+    first = aligned(32 * edge_of(core, half_row))
     lane = lax.broadcasted_iota(jnp.int32, (HALF, TILE), 1)
+    rim_lane = lane // 32 == 3 * half_col
+    outside = rim_lane & (tx == half_col * (lax.axis_size("tx") - 1))
+    rims = in_order(core, side, other_side)
     for g, field in enumerate(in_order(core, mine, theirs)):
-        packed = jnp.zeros((HALF, TILE), jnp.float32)
         for ch in range(4):
-            pair = field[(ch // 2) * HALF : (ch // 2 + 1) * HALF, :]
-            by = TILE + 32 * ch - HALF * (ch % 2) - 32 * core
-            packed = jnp.where(lane // 32 == ch, pltpu.roll(pair, lax.rem(by, TILE), 1), packed)
-        rim[g * HALF : (g + 1) * HALF, :] = packed
-
-
-def row_kernel(mine, theirs, side, other_side, window, rim):
-    core, _, half_col, _, tx = place()
-    lane = lax.broadcasted_iota(jnp.int32, (HALF, TILE), 1)
-    is_left, is_right = lane < 32, lane >= 96
-    outside = (is_left & (half_col == 0) & (tx == 0)) | (
-        is_right & (half_col == 1) & (tx == lax.axis_size("tx") - 1)
-    )
-    left, right = in_order(core, side, other_side)
-    for g, field in enumerate(in_order(core, mine, theirs)):
-        lhs, rhs = (v[g * HALF : (g + 1) * HALF, :] for v in (left, right))
-        for ch in range(4):
-            pair = field[(ch // 2) * HALF : (ch // 2 + 1) * HALF, :]
-            value = pltpu.roll(pair, 32 if ch % 2 == 0 else TILE - 32, 1)
-            value = jnp.where(is_left, pltpu.roll(lhs, (TILE - 32 * ch) % TILE, 1), value)
-            value = jnp.where(is_right, pltpu.roll(rhs, 96 - 32 * ch, 1), value)
+            value = pltpu.roll(field[ch * HALF : (ch + 1) * HALF, :], 32 + 64 * half_col, 1)
+            rim = pltpu.roll(rims[g], lax.rem(TILE - 32 * ch + 96 * half_col, TILE), 1)
+            value = jnp.where(rim_lane, rim, value)
             if g == 1 and ch == 3:
                 value = jnp.where(outside, FAR, value * (1.0 / SIGMA_DEPTH))
             window[4 * g + ch] = value
     for f in range(8):
-        rim[f] = window[f, rows(aligned(32 * core), RIM), :]
+        edge[f] = window[f, rows(first, RIM), :]
 
 
 MOVES = (-16, -8, -4, -2, -1, 1, 2, 4, 8, 16)
@@ -239,7 +225,8 @@
 
 
 def inner_kernel(body, near, middle, far, cur, geo, cur_moved, geo_moved):
-    core = place()[0]
+    core, half_row, _, _, _ = place()
+    upper = edge_of(core, half_row) == 0
     place_rows(cur, geo, rows(0, HALF), body)
     made = set()
     for level, (first, last) in enumerate(INNER):
@@ -247,8 +234,8 @@
             level, first, last, cur, geo, cur_moved, geo_moved, made, into(cur, level + 1)
         )
     for f in range(5):
-        near[f] = jnp.where(core == 0, cur[1, f, 4:12, :], cur[1, f, 52:60, :])
-        middle[f] = jnp.where(core == 0, cur[2, f, 8:24, :], cur[2, f, 40:56, :])
+        near[f] = jnp.where(upper, cur[1, f, 4:12, :], cur[1, f, 52:60, :])
+        middle[f] = jnp.where(upper, cur[2, f, 8:24, :], cur[2, f, 40:56, :])
         far[f] = cur[3, f, 16:48, :]
 
 
@@ -277,7 +264,7 @@
             run_level(level, first, last, cur, geo, cur_moved, geo_moved, made, emit)
 
     for this in range(2):
-        pl.when(core == this)(functools.partial(work, this))
+        pl.when(edge_of(core, half_row) == this)(functools.partial(work, this))
 
 
 def tile_kernel(*refs):
@@ -288,7 +275,8 @@
     for side in range(2):
         which = core if side == 0 else 1 - core
         for r in range(2):
-            row = aligned(64 * (half_row if r == 0 else 1 - half_row) + 32 * which)
+            half = half_row if r == 0 else 1 - half_row
+            row = aligned(64 * half + 32 * edge_of(which, half))
             near, other = (ins[side * 4 + k] for k in ((0, 1) if r == 0 else (3, 2)))
             for k in range(2):
                 p, q = near[k * 32 : (k + 1) * 32, :], other[k * 32 : (k + 1) * 32, :]
@@ -340,39 +328,37 @@
     return call(outer_kernel, [(HALF, TILE)], scratch(WIN), cost=(16, 4))(body, edge, *inner)[0]
 
 
-def pairs(sizes, partner):
+def pairs(sizes, partner, spare=0):
     n_samp, n_ty, n_tx = sizes
+
+    def flat(samp, ty, tx):
+        return (samp * n_ty + ty) * n_tx + tx
+
     out = []
     for samp in range(n_samp):
         for ty in range(n_ty):
             for tx in range(n_tx):
                 to = partner(samp, ty, tx)
-                if 0 <= to[1] < n_ty and 0 <= to[2] < n_tx:
-                    out.append(
-                        ((samp * n_ty + ty) * n_tx + tx, (to[0] * n_ty + to[1]) * n_tx + to[2])
-                    )
+                if not (0 <= to[1] < n_ty and 0 <= to[2] < n_tx):
+                    to = samp ^ spare, ty, tx
+                out.append((flat(samp, ty, tx), flat(*to)))
     return out
 
 
-def beside(samp, ty, tx):
-    y, core = samp // 2, samp % 2
-    half_col = ((y + 1) % 4 // 2 + tx) % 2
-    if half_col == core:
-        return samp ^ 1, ty, tx + (1 if core else -1)
-    return samp ^ 3, ty, tx
-
-
-def above(samp, ty, tx):
-    y, core = samp // 2, samp % 2
-    half_row = (y // 2 + ty) % 2
-    if half_row == core:
-        return samp ^ 1, ty + (1 if core else -1), tx
-    return samp ^ 7, ty, tx
+def across(samp, ty, tx):
+    half_col = ((samp // 2 + 1) % 4 // 2 + tx) % 2
+    return samp, ty, tx + (1 if half_col else -1)
+
+
+def beyond(samp, ty, tx):
+    if samp % 2:
+        return samp ^ 6, ty, tx
+    return samp, ty + (1 if (samp // 4 + ty) % 2 else -1), tx
 
 
 def per_device(sizes, radiance, moment, normal, depth_sum, counts):
-    def send(value, partner):
-        return lax.ppermute(value, AXES, pairs(sizes, partner))
+    def send(value, partner, spare=0):
+        return lax.ppermute(value, AXES, pairs(sizes, partner, spare))
 
     def other_core(value):
         return send(value, lambda s, ty, tx: (s ^ 1, ty, tx))
@@ -381,28 +367,33 @@
         return send(value, lambda s, ty, tx: (s ^ (2 * k), ty, tx))
 
     packed = (4 * TILE + 8, TILE)
-    keep, give = call(
-        pack_kernel,
-        [packed, packed],
-        [pltpu.VMEM((8, 8), jnp.int32), pltpu.SemaphoreType.DMA((9,))],
-        5,
-    )(
-        *(
-            pltpu.with_memory_space_constraint(value, pltpu.HBM)
-            for value in (radiance, moment, normal, depth_sum, counts)
-        )
+    inputs = [
+        pltpu.with_memory_space_constraint(value, pltpu.HBM)
+        for value in (radiance, moment, normal, depth_sum, counts)
+    ]
+
+    def pick(wanted):
+        return call(
+            functools.partial(pick_kernel, wanted),
+            [packed],
+            [pltpu.VMEM((8, 8), jnp.int32), pltpu.SemaphoreType.DMA((5,))],
+            5,
+            (1, 4),
+        )(*inputs)[0]
+
+    give = pick(1)
+    keep = pick(0)
+    part = (3 * HALF + 8, TILE)
+    parts = list(call(pair_kernel, [part] * 4)(keep, other_core(give)))
+    parts = parts[:1] + [other_y(parts[k], k) for k in (1, 2, 3)]
+    mine, rim = call(
+        mean_kernel, [(4 * HALF, TILE), (HALF, TILE)], [pltpu.VMEM((8, TILE), jnp.float32)]
+    )(*parts)
+    rim = send(rim, across, 6)
+    body, edge = call(row_kernel, [(8, HALF, TILE), (8, RIM, TILE)])(
+        mine, other_core(mine), rim, other_core(rim)
     )
-    quarter = (TILE + 8, TILE)
-    parts = list(call(pair_kernel, [quarter] * 4)(keep, other_core(give)))
-    parts = parts[:1] + [other_y(parts[k], k) for k in (1, 2, 3)]
-    (mine,) = call(mean_kernel, [(TILE, TILE)], [pltpu.VMEM((8, TILE), jnp.float32)])(*parts)
-    theirs = other_core(mine)
-    (rim,) = call(column_kernel, [(TILE, TILE)])(mine, theirs)
-    rim = send(rim, beside)
-    body, edge = call(row_kernel, [(8, HALF, TILE), (8, RIM, TILE)])(
-        mine, theirs, rim, other_core(rim)
-    )
-    done = run_filter(body, lambda: send(edge, above))
+    done = run_filter(body, lambda: send(edge, beyond, 2))
     got = [done] + [other_y(done, k) for k in (1, 2, 3)]
     theirs = [other_core(g) for g in got]
     return tuple(call(tile_kernel, [(3, TILE, TILE), (TILE, TILE)])(*got, *theirs))

time: 43.2 us -> 40.7 us (0.942)
  waiting for transfers between devices: 14.4 us -> 11.6 us
  Pallas kernels: 7.61 us -> 8.15 us
    ppermute x15, waiting for transfers between devices: 14.4 us -> 11.6 us  [send(): return lax.ppermute(value, AXES, pairs(sizes, partner, spare))]
    pallas_call x4, Pallas kernels: 1.75 us -> 2.31 us  [the longest x2 1.99 us: pick(): call(functools.partial(pick_kernel, wanted), [packed], [pltpu.VMEM((8, 8)...]
  transfers between devices with their start and end apart: 15 -> 15, of which waited for: 11 -> 10; matrix products, arithmetic and copies ran while one was open for 0% -> 0% of each run, Pallas kernels for 6% -> 9%
where the time goes in v4:
time: 40.7 us; the launch traced here: 40.5 us
  starting transfers between devices  20.1 us (49%)
  waiting for transfers between devices  11.6 us (29%)
  Pallas kernels  8.15 us (20%)
  between operations  0.7 us (2%)
    ppermute x15, starting transfers between devices, send(): return lax.ppermute(value, AXES, pairs(sizes, partner, spare))  20.1 us
    ppermute x15, waiting for transfers between devices, send(): return lax.ppermute(value, AXES, pairs(sizes, partner, spare))  11.6 us
    pallas_call x1, Pallas kernels, run_filter(): call(inner_kernel, [(5, 8, TILE), (5, 16, TILE), (5, 32, TILE)], scratch(...  2.52 us
    pallas_call x1, Pallas kernels, run_filter(): call(outer_kernel, [(HALF, TILE)], scratch(WIN), cost=(16, 4))  2.25 us
    pallas_call x2, Pallas kernels, pick(): call(functools.partial(pick_kernel, wanted), [packed], [pltpu.VMEM((8, 8)...  1.99 us
    pallas_call x1, Pallas kernels, per_device(): call(tile_kernel, [(3, TILE, TILE), (TILE, TILE)])(*got, *theirs)  0.83 us
  transfers between devices with their start and end apart: 15, of which 10 were waited for; matrix products, arithmetic and copies ran while one was open for 0% of the time, Pallas kernels for 9%

profile of v4, /device:TPU:1, one launch (start us, length us, event | category | flops | bytes accessed | tf_op | source)
XLA Modules:
  0.0 40.5 jit_solution(17020223534529235624)
XLA Ops:
  0.6 1.0 %shard_map.69 = f32[520,128]{1,0:T(8,128)S(1)} custom-call(f32[1,3,128,128]{3,2,1,0:T(8,128)} %rad.3, f32[1,128,128]{2,1,0:T(8,128)} %mom.3, f32[1,3,128,128]{3,2,1,0:T(8,128)} %nor.3, f32[1,128,128]{2,1,0:T(8,128)} %dep.3, s32[1,8,8]{2,1,0:T(8,128)} %cnt.3), custom_call_target="tpu_custom_call" | custom-call | flops 691200 | bytes 262144 | tf_op jit(solution)/shard_map/pallas_call | solution.py:376
  1.6 3.3 %collective-permute-start = (f32[520,128]{1,0:T(8,128)S(1)}, f32[520,128]{1,0:T(8,128)S(1)}, u32[]{:S(2)}, u32[]{:S(2)}) collective-permute-start(f32[520,128]{1,0:T(8,128)S(1)} %shard_map.69), channel_id=1, source_target_pairs={{0,32},{1,33},{2,34},{3,35},{4,36},{5,37},{6,38},{7,39},{8,40},{9,... | collective-permute-start | bytes 798728 | tf_op jit(solution)/shard_map/ppermute | solution.py:361
  5.0 1.0 %shard_map.68.keep = f32[520,128]{1,0:T(8,128)S(1)} custom-call(f32[1,3,128,128]{3,2,1,0:T(8,128)} %rad.3, f32[1,128,128]{2,1,0:T(8,128)} %mom.3, f32[1,3,128,128]{3,2,1,0:T(8,128)} %nor.3, f32[1,128,128]{2,1,0:T(8,128)} %dep.3, s32[1,8,8]{2,1,0:T(8,128)} %cnt.3), custom_call_target="tpu_custom_call" | custom-call | flops 691200 | bytes 262144 | tf_op jit(solution)/shard_map/pallas_call | solution.py:376
  6.4 2.2 %collective-permute-start.2 = (f32[200,128]{1,0:T(8,128)S(1)}, f32[200,128]{1,0:T(8,128)S(1)}, u32[]{:S(2)}, u32[]{:S(2)}) collective-permute-start(f32[200,128]{1,0:T(8,128)S(1)} %get-tuple-element.15), channel_id=1, source_target_pairs={{0,128},{1,129},{2,130},{3,131},{4,132},{5,133},{6,134},{7,135},{8... | collective-permute-start | bytes 307208 | tf_op jit(solution)/shard_map/ppermute | solution.py:361
  8.5 1.7 %collective-permute-start.3 = (f32[200,128]{1,0:T(8,128)S(1)}, f32[200,128]{1,0:T(8,128)S(1)}, u32[]{:S(2)}, u32[]{:S(2)}) collective-permute-start(f32[200,128]{1,0:T(8,128)S(1)} %get-tuple-element.16), channel_id=1, source_target_pairs={{0,192},{1,193},{2,194},{3,195},{4,196},{5,197},{6,198},{7,199},{8... | collective-permute-start | bytes 307208 | tf_op jit(solution)/shard_map/ppermute | solution.py:361
  10.4 2.9 %collective-permute-done.2.r2 = f32[200,128]{1,0:T(8,128)S(1)} collective-permute-done((f32[200,128]{1,0:T(8,128)S(1)}, f32[200,128]{1,0:T(8,128)S(1)}, u32[]{:S(2)}, u32[]{:S(2)}) %collective-permute-start.2) | collective-permute-done | bytes 102432 | tf_op jit(solution)/shard_map/ppermute | solution.py:361
  13.4 2.6 %collective-permute-done.3.r3 = f32[200,128]{1,0:T(8,128)S(1)} collective-permute-done((f32[200,128]{1,0:T(8,128)S(1)}, f32[200,128]{1,0:T(8,128)S(1)}, u32[]{:S(2)}, u32[]{:S(2)}) %collective-permute-start.3) | collective-permute-done | bytes 102432 | tf_op jit(solution)/shard_map/ppermute | solution.py:361
  16.1 0.7 %collective-permute-start.4 = (f32[256,128]{1,0:T(8,128)S(1)}, f32[256,128]{1,0:T(8,128)S(1)}, u32[]{:S(2)}, u32[]{:S(2)}) collective-permute-start(f32[256,128]{1,0:T(8,128)S(1)} %get-tuple-element.17.mine), channel_id=1, source_target_pairs={{0,32},{1,33},{2,34},{3,35},{4,36},{5,37},{6,38},{7,39},{8,40},{9,... | collective-permute-start | bytes 393224 | tf_op jit(solution)/shard_map/ppermute | solution.py:361
  16.9 1.7 %collective-permute-start.5 = (f32[64,128]{1,0:T(8,128)S(1)}, f32[64,128]{1,0:T(8,128)S(1)}, u32[]{:S(2)}, u32[]{:S(2)}) collective-permute-start(f32[64,128]{1,0:T(8,128)S(1)} %get-tuple-element.18), channel_id=1, source_target_pairs={{0,192},{1,2},{2,1},{3,195},{4,196},{5,6},{6,5},{7,199},{8,200},{9... | collective-permute-start | bytes 98312 | tf_op jit(solution)/shard_map/ppermute | solution.py:361
  18.6 2.3 %collective-permute-done.5.side = f32[64,128]{1,0:T(8,128)S(1)} collective-permute-done((f32[64,128]{1,0:T(8,128)S(1)}, f32[64,128]{1,0:T(8,128)S(1)}, u32[]{:S(2)}, u32[]{:S(2)}) %collective-permute-start.5) | collective-permute-done | bytes 32800 | tf_op jit(solution)/shard_map/ppermute | solution.py:361
  20.9 1.2 %collective-permute-start.6 = (f32[64,128]{1,0:T(8,128)S(1)}, f32[64,128]{1,0:T(8,128)S(1)}, u32[]{:S(2)}, u32[]{:S(2)}) collective-permute-start(f32[64,128]{1,0:T(8,128)S(1)} %collective-permute-done.5.side), channel_id=1, source_target_pairs={{0,32},{1,33},{2,34},{3,35},{4,36},{5,37},{6,38},{7,39},{8,40},{9,... | collective-permute-start | bytes 98312 | tf_op jit(solution)/shard_map/ppermute | solution.py:361
  22.1 0.9 %collective-permute-done.6.other_side = f32[64,128]{1,0:T(8,128)S(1)} collective-permute-done((f32[64,128]{1,0:T(8,128)S(1)}, f32[64,128]{1,0:T(8,128)S(1)}, u32[]{:S(2)}, u32[]{:S(2)}) %collective-permute-start.6) | collective-permute-done | bytes 32800 | tf_op jit(solution)/shard_map/ppermute | solution.py:361
  23.2 1.8 %collective-permute-start.7 = (f32[8,32,128]{2,1,0:T(8,128)S(1)}, f32[8,32,128]{2,1,0:T(8,128)S(1)}, u32[]{:S(2)}, u32[]{:S(2)}) collective-permute-start(f32[8,32,128]{2,1,0:T(8,128)S(1)} %get-tuple-element.20), channel_id=1, source_target_pairs={{0,64},{1,65},{2,66},{3,67},{4,8},{5,9},{6,10},{7,11},{8,4},{9,5},... | collective-permute-start | bytes 393224 | tf_op jit(solution)/shard_map/ppermute | solution.py:361
  25.0 2.5 %shard_map.73 = (f32[5,8,128]{2,1,0:T(8,128)S(1)}, f32[5,16,128]{2,1,0:T(8,128)S(1)}, f32[5,32,128]{2,1,0:T(8,128)S(1)}) custom-call(f32[8,64,128]{2,1,0:T(8,128)S(1)} %get-tuple-element.19.body), custom_call_target="tpu_custom_call" | custom-call | flops 11750400 | bytes 196608 | tf_op jit(solution)/shard_map/pallas_call | solution.py:325
  27.5 0.8 %collective-permute-done.7.edge = f32[8,32,128]{2,1,0:T(8,128)S(1)} collective-permute-done((f32[8,32,128]{2,1,0:T(8,128)S(1)}, f32[8,32,128]{2,1,0:T(8,128)S(1)}, u32[]{:S(2)}, u32[]{:S(2)}) %collective-permute-start.7) | collective-permute-done | bytes 131104 | tf_op jit(solution)/shard_map/ppermute | solution.py:361
  28.3 2.3 %shard_map.74.refs_0_ = f32[64,128]{1,0:T(8,128)S(1)} custom-call(f32[8,64,128]{2,1,0:T(8,128)S(1)} %get-tuple-element.19.body, f32[8,32,128]{2,1,0:T(8,128)S(1)} %collective-permute-done.7.edge, f32[5,8,128]{2,1,0:T(8,128)S(1)} %get-tuple-element.21.near, f32[5,16,128]{2,1,0:T(8,128)S(1)} %get-tuple-element.22.middle, f32[5,32,128]{2,1,0:T(8,128)S(1)} %get-tuple-element.23.far), custom_call_target="tpu_custom_call" | custom-call | flops 11059200 | bytes 262144 | tf_op jit(solution)/shard_map/pallas_call | solution.py:328
  30.6 1.9 %collective-permute-start.10 = (f32[64,128]{1,0:T(8,128)S(1)}, f32[64,128]{1,0:T(8,128)S(1)}, u32[]{:S(2)}, u32[]{:S(2)}) collective-permute-start(f32[64,128]{1,0:T(8,128)S(1)} %shard_map.74.refs_0_), channel_id=1, source_target_pairs={{0,192},{1,193},{2,194},{3,195},{4,196},{5,197},{6,198},{7,199},{8... | collective-permute-start | bytes 98312 | tf_op jit(solution)/shard_map/ppermute | solution.py:361
  32.5 1.6 %collective-permute-start.8 = (f32[64,128]{1,0:T(8,128)S(1)}, f32[64,128]{1,0:T(8,128)S(1)}, u32[]{:S(2)}, u32[]{:S(2)}) collective-permute-start(f32[64,128]{1,0:T(8,128)S(1)} %shard_map.74.refs_0_), channel_id=1, source_target_pairs={{0,64},{1,65},{2,66},{3,67},{4,68},{5,69},{6,70},{7,71},{8,72},{9,... | collective-permute-start | bytes 98312 | tf_op jit(solution)/shard_map/ppermute | solution.py:361
  34.1 1.1 %collective-permute-start.11 = (f32[64,128]{1,0:T(8,128)S(1)}, f32[64,128]{1,0:T(8,128)S(1)}, u32[]{:S(2)}, u32[]{:S(2)}) collective-permute-start(f32[64,128]{1,0:T(8,128)S(1)} %shard_map.74.refs_0_), channel_id=1, source_target_pairs={{0,32},{1,33},{2,34},{3,35},{4,36},{5,37},{6,38},{7,39},{8,40},{9,... | collective-permute-start | bytes 98312 | tf_op jit(solution)/shard_map/ppermute | solution.py:361
  35.2 1.0 %collective-permute-start.14 = (f32[64,128]{1,0:T(8,128)S(1)}, f32[64,128]{1,0:T(8,128)S(1)}, u32[]{:S(2)}, u32[]{:S(2)}) collective-permute-start(f32[64,128]{1,0:T(8,128)S(1)} %collective-permute-done.10.refs_3_), channel_id=1, source_target_pairs={{0,32},{1,33},{2,34},{3,35},{4,36},{5,37},{6,38},{7,39},{8,40},{9,... | collective-permute-start | bytes 98312 | tf_op jit(solution)/shard_map/ppermute | solution.py:361
  36.2 0.5 %collective-permute-done.9.refs_2_ = f32[64,128]{1,0:T(8,128)S(1)} collective-permute-done((f32[64,128]{1,0:T(8,128)S(1)}, f32[64,128]{1,0:T(8,128)S(1)}, u32[]{:S(2)}, u32[]{:S(2)}) %collective-permute-start.9) | collective-permute-done | bytes 32800 | tf_op jit(solution)/shard_map/ppermute | solution.py:361
  36.7 1.7 %collective-permute-start.13 = (f32[64,128]{1,0:T(8,128)S(1)}, f32[64,128]{1,0:T(8,128)S(1)}, u32[]{:S(2)}, u32[]{:S(2)}) collective-permute-start(f32[64,128]{1,0:T(8,128)S(1)} %collective-permute-done.9.refs_2_), channel_id=1, source_target_pairs={{0,32},{1,33},{2,34},{3,35},{4,36},{5,37},{6,38},{7,39},{8,40},{9,... | collective-permute-start | bytes 98312 | tf_op jit(solution)/shard_map/ppermute | solution.py:361
  38.5 0.8 %collective-permute-done.13.refs_6_ = f32[64,128]{1,0:T(8,128)S(1)} collective-permute-done((f32[64,128]{1,0:T(8,128)S(1)}, f32[64,128]{1,0:T(8,128)S(1)}, u32[]{:S(2)}, u32[]{:S(2)}) %collective-permute-start.13) | collective-permute-done | bytes 32800 | tf_op jit(solution)/shard_map/ppermute | solution.py:361
  39.7 0.8 %shard_map.75 = (f32[3,128,128]{2,1,0:T(8,128)}, f32[128,128]{1,0:T(8,128)}) custom-call(f32[64,128]{1,0:T(8,128)S(1)} %shard_map.74.refs_0_, f32[64,128]{1,0:T(8,128)S(1)} %collective-permute-done.8.refs_1_, f32[64,128]{1,0:T(8,128)S(1)} %collective-permute-done.9.refs_2_, f32[64,128]{1,0:T(8,128)S(1)} %collective-permute-done.10.refs_3_, ...), custom_call_target="tpu_custom_call" | custom-call | tf_op jit(solution)/shard_map/pallas_call | solution.py:399
  (14 shorter events, 1.4 us)
Async XLA Ops:
  1.6 4.5 %collective-permute-start = (f32[520,128]{1,0:T(8,128)S(1)}, f32[520,128]{1,0:T(8,128)S(1)}, u32[]{:S(2)}, u32[]{:S(2)}) collective-permute-start(f32[520,128]{1,0:T(8,128)S(1)} %shard_map.69), channel_id=1, source_target_pairs={{0,32},{1,33},{2,34},{3,35},{4,36},{5,37},{6,38},{7,39},{8,40},{9,... | collective-permute-start | bytes 798728 | tf_op jit(solution)/shard_map/ppermute | solution.py:361
  6.3 4.2 %collective-permute-start.1 = (f32[200,128]{1,0:T(8,128)S(1)}, f32[200,128]{1,0:T(8,128)S(1)}, u32[]{:S(2)}, u32[]{:S(2)}) collective-permute-start(f32[200,128]{1,0:T(8,128)S(1)} %get-tuple-element.14), channel_id=1, source_target_pairs={{0,64},{1,65},{2,66},{3,67},{4,68},{5,69},{6,70},{7,71},{8,72},{9,... | collective-permute-start | bytes 307208 | tf_op jit(solution)/shard_map/ppermute | solution.py:361
  6.4 7.0 %collective-permute-start.2 = (f32[200,128]{1,0:T(8,128)S(1)}, f32[200,128]{1,0:T(8,128)S(1)}, u32[]{:S(2)}, u32[]{:S(2)}) collective-permute-start(f32[200,128]{1,0:T(8,128)S(1)} %get-tuple-element.15), channel_id=1, source_target_pairs={{0,128},{1,129},{2,130},{3,131},{4,132},{5,133},{6,134},{7,135},{8... | collective-permute-start | bytes 307208 | tf_op jit(solution)/shard_map/ppermute | solution.py:361
  8.5 7.4 %collective-permute-start.3 = (f32[200,128]{1,0:T(8,128)S(1)}, f32[200,128]{1,0:T(8,128)S(1)}, u32[]{:S(2)}, u32[]{:S(2)}) collective-permute-start(f32[200,128]{1,0:T(8,128)S(1)} %get-tuple-element.16), channel_id=1, source_target_pairs={{0,192},{1,193},{2,194},{3,195},{4,196},{5,197},{6,198},{7,199},{8... | collective-permute-start | bytes 307208 | tf_op jit(solution)/shard_map/ppermute | solution.py:361
  16.1 6.8 %collective-permute-start.4 = (f32[256,128]{1,0:T(8,128)S(1)}, f32[256,128]{1,0:T(8,128)S(1)}, u32[]{:S(2)}, u32[]{:S(2)}) collective-permute-start(f32[256,128]{1,0:T(8,128)S(1)} %get-tuple-element.17.mine), channel_id=1, source_target_pairs={{0,32},{1,33},{2,34},{3,35},{4,36},{5,37},{6,38},{7,39},{8,40},{9,... | collective-permute-start | bytes 393224 | tf_op jit(solution)/shard_map/ppermute | solution.py:361
  16.9 4.0 %collective-permute-start.5 = (f32[64,128]{1,0:T(8,128)S(1)}, f32[64,128]{1,0:T(8,128)S(1)}, u32[]{:S(2)}, u32[]{:S(2)}) collective-permute-start(f32[64,128]{1,0:T(8,128)S(1)} %get-tuple-element.18), channel_id=1, source_target_pairs={{0,192},{1,2},{2,1},{3,195},{4,196},{5,6},{6,5},{7,199},{8,200},{9... | collective-permute-start | bytes 98312 | tf_op jit(solution)/shard_map/ppermute | solution.py:361
  20.9 2.1 %collective-permute-start.6 = (f32[64,128]{1,0:T(8,128)S(1)}, f32[64,128]{1,0:T(8,128)S(1)}, u32[]{:S(2)}, u32[]{:S(2)}) collective-permute-start(f32[64,128]{1,0:T(8,128)S(1)} %collective-permute-done.5.side), channel_id=1, source_target_pairs={{0,32},{1,33},{2,34},{3,35},{4,36},{5,37},{6,38},{7,39},{8,40},{9,... | collective-permute-start | bytes 98312 | tf_op jit(solution)/shard_map/ppermute | solution.py:361
  23.2 5.1 %collective-permute-start.7 = (f32[8,32,128]{2,1,0:T(8,128)S(1)}, f32[8,32,128]{2,1,0:T(8,128)S(1)}, u32[]{:S(2)}, u32[]{:S(2)}) collective-permute-start(f32[8,32,128]{2,1,0:T(8,128)S(1)} %get-tuple-element.20), channel_id=1, source_target_pairs={{0,64},{1,65},{2,66},{3,67},{4,8},{5,9},{6,10},{7,11},{8,4},{9,5},... | collective-permute-start | bytes 393224 | tf_op jit(solution)/shard_map/ppermute | solution.py:361
  30.6 4.6 %collective-permute-start.10 = (f32[64,128]{1,0:T(8,128)S(1)}, f32[64,128]{1,0:T(8,128)S(1)}, u32[]{:S(2)}, u32[]{:S(2)}) collective-permute-start(f32[64,128]{1,0:T(8,128)S(1)} %shard_map.74.refs_0_), channel_id=1, source_target_pairs={{0,192},{1,193},{2,194},{3,195},{4,196},{5,197},{6,198},{7,199},{8... | collective-permute-start | bytes 98312 | tf_op jit(solution)/shard_map/ppermute | solution.py:361
  32.5 4.3 %collective-permute-start.9 = (f32[64,128]{1,0:T(8,128)S(1)}, f32[64,128]{1,0:T(8,128)S(1)}, u32[]{:S(2)}, u32[]{:S(2)}) collective-permute-start(f32[64,128]{1,0:T(8,128)S(1)} %shard_map.74.refs_0_), channel_id=1, source_target_pairs={{0,128},{1,129},{2,130},{3,131},{4,132},{5,133},{6,134},{7,135},{8... | collective-permute-start | bytes 98312 | tf_op jit(solution)/shard_map/ppermute | solution.py:361
  32.5 6.0 %collective-permute-start.8 = (f32[64,128]{1,0:T(8,128)S(1)}, f32[64,128]{1,0:T(8,128)S(1)}, u32[]{:S(2)}, u32[]{:S(2)}) collective-permute-start(f32[64,128]{1,0:T(8,128)S(1)} %shard_map.74.refs_0_), channel_id=1, source_target_pairs={{0,64},{1,65},{2,66},{3,67},{4,68},{5,69},{6,70},{7,71},{8,72},{9,... | collective-permute-start | bytes 98312 | tf_op jit(solution)/shard_map/ppermute | solution.py:361
  34.1 4.4 %collective-permute-start.11 = (f32[64,128]{1,0:T(8,128)S(1)}, f32[64,128]{1,0:T(8,128)S(1)}, u32[]{:S(2)}, u32[]{:S(2)}) collective-permute-start(f32[64,128]{1,0:T(8,128)S(1)} %shard_map.74.refs_0_), channel_id=1, source_target_pairs={{0,32},{1,33},{2,34},{3,35},{4,36},{5,37},{6,38},{7,39},{8,40},{9,... | collective-permute-start | bytes 98312 | tf_op jit(solution)/shard_map/ppermute | solution.py:361
  35.2 3.3 %collective-permute-start.14 = (f32[64,128]{1,0:T(8,128)S(1)}, f32[64,128]{1,0:T(8,128)S(1)}, u32[]{:S(2)}, u32[]{:S(2)}) collective-permute-start(f32[64,128]{1,0:T(8,128)S(1)} %collective-permute-done.10.refs_3_), channel_id=1, source_target_pairs={{0,32},{1,33},{2,34},{3,35},{4,36},{5,37},{6,38},{7,39},{8,40},{9,... | collective-permute-start | bytes 98312 | tf_op jit(solution)/shard_map/ppermute | solution.py:361
  36.7 2.6 %collective-permute-start.13 = (f32[64,128]{1,0:T(8,128)S(1)}, f32[64,128]{1,0:T(8,128)S(1)}, u32[]{:S(2)}, u32[]{:S(2)}) collective-permute-start(f32[64,128]{1,0:T(8,128)S(1)} %collective-permute-done.9.refs_2_), channel_id=1, source_target_pairs={{0,32},{1,33},{2,34},{3,35},{4,36},{5,37},{6,38},{7,39},{8,40},{9,... | collective-permute-start | bytes 98312 | tf_op jit(solution)/shard_map/ppermute | solution.py:361
  38.5 1.2 %collective-permute-start.12 = (f32[64,128]{1,0:T(8,128)S(1)}, f32[64,128]{1,0:T(8,128)S(1)}, u32[]{:S(2)}, u32[]{:S(2)}) collective-permute-start(f32[64,128]{1,0:T(8,128)S(1)} %collective-permute-done.8.refs_1_), channel_id=1, source_target_pairs={{0,32},{1,33},{2,34},{3,35},{4,36},{5,37},{6,38},{7,39},{8,40},{9,... | collective-permute-start | bytes 98312 | tf_op jit(solution)/shard_map/ppermute | solution.py:361

commit v5 on v4

--- a/solution.py
+++ b/solution.py
@@ -100,7 +100,7 @@
                 outs[k][3 * HALF :, :] = counts
 
 
-def mean_kernel(own, r1, r2, r3, field, rim, samples):
+def mean_kernel(wants_rim, own, r1, r2, r3, out, samples):
     core, half_row, half_col, _, _ = place()
     lane = lax.broadcasted_iota(jnp.int32, (8, TILE), 1)
 
@@ -124,36 +124,41 @@
         mean[3] = jnp.where(core == 0, variance, mean[3])
         packed = jnp.zeros((BLK, TILE), jnp.float32)
         for ch in range(4):
-            field[rows(ch * HALF + i * BLK, BLK), :] = mean[ch]
-            moved = pltpu.roll(mean[ch], lax.rem(32 * ch + 32 * half_col, TILE), 1)
-            packed = jnp.where(group == ch, moved, packed)
-        rim[rows(i * BLK, BLK), :] = packed
-
-
-def in_order(core, mine, theirs):
-    return (
-        jnp.where(core == 0, mine[...], theirs[...]),
-        jnp.where(core == 0, theirs[...], mine[...]),
-    )
-
-
-def row_kernel(mine, theirs, side, other_side, window, edge):
+            if wants_rim:
+                moved = pltpu.roll(mean[ch], lax.rem(32 * ch + 32 * half_col, TILE), 1)
+                packed = jnp.where(group == ch, moved, packed)
+            else:
+                out[rows(ch * HALF + i * BLK, BLK), :] = mean[ch]
+        if wants_rim:
+            out[rows(i * BLK, BLK), :] = packed
+
+
+def row_kernel(wants_edge, mine, theirs, side, other_side, out):
     core, half_row, half_col, _, tx = place()
-    first = aligned(32 * edge_of(core, half_row))
-    lane = lax.broadcasted_iota(jnp.int32, (HALF, TILE), 1)
-    rim_lane = lane // 32 == 3 * half_col
+    count = RIM if wants_edge else HALF
+    first = aligned(32 * edge_of(core, half_row)) if wants_edge else 0
+    rim_lane = lax.broadcasted_iota(jnp.int32, (count, TILE), 1) // 32 == 3 * half_col
     outside = rim_lane & (tx == half_col * (lax.axis_size("tx") - 1))
-    rims = in_order(core, side, other_side)
-    for g, field in enumerate(in_order(core, mine, theirs)):
-        for ch in range(4):
-            value = pltpu.roll(field[ch * HALF : (ch + 1) * HALF, :], 32 + 64 * half_col, 1)
-            rim = pltpu.roll(rims[g], lax.rem(TILE - 32 * ch + 96 * half_col, TILE), 1)
-            value = jnp.where(rim_lane, rim, value)
-            if g == 1 and ch == 3:
-                value = jnp.where(outside, FAR, value * (1.0 / SIGMA_DEPTH))
-            window[4 * g + ch] = value
-    for f in range(8):
-        edge[f] = window[f, rows(first, RIM), :]
+
+    def fill(colour, normal, colour_rim, normal_rim):
+        for g, (field, rims) in enumerate(((colour, colour_rim), (normal, normal_rim))):
+            for ch in range(4):
+                at = ch * HALF + first
+                value = field[rows(aligned(at) if wants_edge else at, count), :]
+                value = pltpu.roll(value, 32 + 64 * half_col, 1)
+                by = lax.rem(TILE - 32 * ch + 96 * half_col, TILE)
+                value = jnp.where(rim_lane, pltpu.roll(rims[rows(first, count), :], by, 1), value)
+                if g == 1 and ch == 3:
+                    value = jnp.where(outside, FAR, value * (1.0 / SIGMA_DEPTH))
+                out[4 * g + ch] = value
+
+    @pl.when(core == 0)
+    def _():
+        fill(mine, theirs, side, other_side)
+
+    @pl.when(core == 1)
+    def _():
+        fill(theirs, mine, other_side, side)
 
 
 MOVES = (-16, -8, -4, -2, -1, 1, 2, 4, 8, 16)
@@ -386,14 +391,25 @@
     part = (3 * HALF + 8, TILE)
     parts = list(call(pair_kernel, [part] * 4)(keep, other_core(give)))
     parts = parts[:1] + [other_y(parts[k], k) for k in (1, 2, 3)]
-    mine, rim = call(
-        mean_kernel, [(4 * HALF, TILE), (HALF, TILE)], [pltpu.VMEM((8, TILE), jnp.float32)]
-    )(*parts)
-    rim = send(rim, across, 6)
-    body, edge = call(row_kernel, [(8, HALF, TILE), (8, RIM, TILE)])(
-        mine, other_core(mine), rim, other_core(rim)
-    )
-    done = run_filter(body, lambda: send(edge, beyond, 2))
+
+    def means(wants_rim):
+        return call(
+            functools.partial(mean_kernel, wants_rim),
+            [(HALF if wants_rim else 4 * HALF, TILE)],
+            [pltpu.VMEM((8, TILE), jnp.float32)],
+            cost=(1, 4),
+        )(*parts)[0]
+
+    rim = send(means(True), across, 6)
+    mine, rim = lax.optimization_barrier((means(False), rim))
+    sides = (mine, other_core(mine), rim, other_core(rim))
+
+    def joined(wants_edge, count):
+        kernel = functools.partial(row_kernel, wants_edge)
+        return call(kernel, [(8, count, TILE)], cost=(1, 8))(*sides)[0]
+
+    edge = send(joined(True, RIM), beyond, 2)
+    done = run_filter(joined(False, HALF), lambda: edge)
     got = [done] + [other_y(done, k) for k in (1, 2, 3)]
     theirs = [other_core(g) for g in got]
     return tuple(call(tile_kernel, [(3, TILE, TILE), (TILE, TILE)])(*got, *theirs))

time: 40.7 us -> 40.5 us (level)
  starting transfers between devices: 20.1 us -> 19.5 us
    ppermute x15, starting transfers between devices: 20.1 us -> 19.5 us  [send(): return lax.ppermute(value, AXES, pairs(sizes, partner, spare))]
  transfers between devices with their start and end apart: 15 -> 15, of which waited for: 10 -> 10; matrix products, arithmetic and copies ran while one was open for 0% -> 0% of each run, Pallas kernels for 9% -> 10%
where the time goes in v5:
time: 40.5 us; the launch traced here: 40.3 us
  starting transfers between devices  19.5 us (48%)
  waiting for transfers between devices  11.8 us (29%)
  Pallas kernels  8.37 us (21%)
  between operations  0.72 us (2%)
    ppermute x15, starting transfers between devices, send(): return lax.ppermute(value, AXES, pairs(sizes, partner, spare))  19.5 us
    ppermute x15, waiting for transfers between devices, send(): return lax.ppermute(value, AXES, pairs(sizes, partner, spare))  11.8 us
    pallas_call x1, Pallas kernels, run_filter(): call(inner_kernel, [(5, 8, TILE), (5, 16, TILE), (5, 32, TILE)], scratch(...  2.53 us
    pallas_call x1, Pallas kernels, run_filter(): call(outer_kernel, [(HALF, TILE)], scratch(WIN), cost=(16, 4))  2.25 us
    pallas_call x2, Pallas kernels, pick(): call(functools.partial(pick_kernel, wanted), [packed], [pltpu.VMEM((8, 8)...  1.99 us
    pallas_call x1, Pallas kernels, per_device(): call(tile_kernel, [(3, TILE, TILE), (TILE, TILE)])(*got, *theirs)  0.83 us
  transfers between devices with their start and end apart: 15, of which 10 were waited for; matrix products, arithmetic and copies ran while one was open for 0% of the time, Pallas kernels for 10%

profile of v5, /device:TPU:1, one launch (start us, length us, event | category | flops | bytes accessed | tf_op | source)
XLA Modules:
  0.0 40.3 jit_solution(5170989443488553729)
XLA Ops:
  0.6 1.0 %shard_map.69 = f32[520,128]{1,0:T(8,128)S(1)} custom-call(f32[1,3,128,128]{3,2,1,0:T(8,128)} %rad.3, f32[1,128,128]{2,1,0:T(8,128)} %mom.3, f32[1,3,128,128]{3,2,1,0:T(8,128)} %nor.3, f32[1,128,128]{2,1,0:T(8,128)} %dep.3, s32[1,8,8]{2,1,0:T(8,128)} %cnt.3), custom_call_target="tpu_custom_call" | custom-call | flops 691200 | bytes 262144 | tf_op jit(solution)/shard_map/pallas_call | solution.py:381
  1.6 3.3 %collective-permute-start = (f32[520,128]{1,0:T(8,128)S(1)}, f32[520,128]{1,0:T(8,128)S(1)}, u32[]{:S(2)}, u32[]{:S(2)}) collective-permute-start(f32[520,128]{1,0:T(8,128)S(1)} %shard_map.69), channel_id=1, source_target_pairs={{0,32},{1,33},{2,34},{3,35},{4,36},{5,37},{6,38},{7,39},{8,40},{9,... | collective-permute-start | bytes 798728 | tf_op jit(solution)/shard_map/ppermute | solution.py:366
  5.0 1.0 %shard_map.68.keep = f32[520,128]{1,0:T(8,128)S(1)} custom-call(f32[1,3,128,128]{3,2,1,0:T(8,128)} %rad.3, f32[1,128,128]{2,1,0:T(8,128)} %mom.3, f32[1,3,128,128]{3,2,1,0:T(8,128)} %nor.3, f32[1,128,128]{2,1,0:T(8,128)} %dep.3, s32[1,8,8]{2,1,0:T(8,128)} %cnt.3), custom_call_target="tpu_custom_call" | custom-call | flops 691200 | bytes 262144 | tf_op jit(solution)/shard_map/pallas_call | solution.py:381
  6.4 2.2 %collective-permute-start.2 = (f32[200,128]{1,0:T(8,128)S(1)}, f32[200,128]{1,0:T(8,128)S(1)}, u32[]{:S(2)}, u32[]{:S(2)}) collective-permute-start(f32[200,128]{1,0:T(8,128)S(1)} %get-tuple-element.13), channel_id=1, source_target_pairs={{0,128},{1,129},{2,130},{3,131},{4,132},{5,133},{6,134},{7,135},{8... | collective-permute-start | bytes 307208 | tf_op jit(solution)/shard_map/ppermute | solution.py:366
  8.5 1.7 %collective-permute-start.3 = (f32[200,128]{1,0:T(8,128)S(1)}, f32[200,128]{1,0:T(8,128)S(1)}, u32[]{:S(2)}, u32[]{:S(2)}) collective-permute-start(f32[200,128]{1,0:T(8,128)S(1)} %get-tuple-element.14), channel_id=1, source_target_pairs={{0,192},{1,193},{2,194},{3,195},{4,196},{5,197},{6,198},{7,199},{8... | collective-permute-start | bytes 307208 | tf_op jit(solution)/shard_map/ppermute | solution.py:366
  10.5 2.9 %collective-permute-done.2.r2 = f32[200,128]{1,0:T(8,128)S(1)} collective-permute-done((f32[200,128]{1,0:T(8,128)S(1)}, f32[200,128]{1,0:T(8,128)S(1)}, u32[]{:S(2)}, u32[]{:S(2)}) %collective-permute-start.2) | collective-permute-done | bytes 102432 | tf_op jit(solution)/shard_map/ppermute | solution.py:366
  13.4 2.6 %collective-permute-done.3.r3 = f32[200,128]{1,0:T(8,128)S(1)} collective-permute-done((f32[200,128]{1,0:T(8,128)S(1)}, f32[200,128]{1,0:T(8,128)S(1)}, u32[]{:S(2)}, u32[]{:S(2)}) %collective-permute-start.3) | collective-permute-done | bytes 102432 | tf_op jit(solution)/shard_map/ppermute | solution.py:366
  16.1 1.8 %collective-permute-start.4 = (f32[64,128]{1,0:T(8,128)S(1)}, f32[64,128]{1,0:T(8,128)S(1)}, u32[]{:S(2)}, u32[]{:S(2)}) collective-permute-start(f32[64,128]{1,0:T(8,128)S(1)} %shard_map.72), channel_id=1, source_target_pairs={{0,192},{1,2},{2,1},{3,195},{4,196},{5,6},{6,5},{7,199},{8,200},{9... | collective-permute-start | bytes 98312 | tf_op jit(solution)/shard_map/ppermute | solution.py:366
  18.0 2.2 %collective-permute-done.4.side = f32[64,128]{1,0:T(8,128)S(1)} collective-permute-done((f32[64,128]{1,0:T(8,128)S(1)}, f32[64,128]{1,0:T(8,128)S(1)}, u32[]{:S(2)}, u32[]{:S(2)}) %collective-permute-start.4) | collective-permute-done | bytes 32800 | tf_op jit(solution)/shard_map/ppermute | solution.py:366
  20.2 1.8 %collective-permute-start.5 = (f32[256,128]{1,0:T(8,128)S(1)}, f32[256,128]{1,0:T(8,128)S(1)}, u32[]{:S(2)}, u32[]{:S(2)}) collective-permute-start(f32[256,128]{1,0:T(8,128)S(1)} %shard_map.71.mine), channel_id=1, source_target_pairs={{0,32},{1,33},{2,34},{3,35},{4,36},{5,37},{6,38},{7,39},{8,40},{9,... | collective-permute-start | bytes 393224 | tf_op jit(solution)/shard_map/ppermute | solution.py:366
  22.0 1.2 %collective-permute-done.6.other_side = f32[64,128]{1,0:T(8,128)S(1)} collective-permute-done((f32[64,128]{1,0:T(8,128)S(1)}, f32[64,128]{1,0:T(8,128)S(1)}, u32[]{:S(2)}, u32[]{:S(2)}) %collective-permute-start.6) | collective-permute-done | bytes 32800 | tf_op jit(solution)/shard_map/ppermute | solution.py:366
  23.4 1.8 %collective-permute-start.7 = (f32[8,32,128]{2,1,0:T(8,128)S(1)}, f32[8,32,128]{2,1,0:T(8,128)S(1)}, u32[]{:S(2)}, u32[]{:S(2)}) collective-permute-start(f32[8,32,128]{2,1,0:T(8,128)S(1)} %shard_map.74), channel_id=1, source_target_pairs={{0,64},{1,65},{2,66},{3,67},{4,8},{5,9},{6,10},{7,11},{8,4},{9,5},... | collective-permute-start | bytes 393224 | tf_op jit(solution)/shard_map/ppermute | solution.py:366
  25.3 2.5 %shard_map.75 = (f32[5,8,128]{2,1,0:T(8,128)S(1)}, f32[5,16,128]{2,1,0:T(8,128)S(1)}, f32[5,32,128]{2,1,0:T(8,128)S(1)}) custom-call(f32[8,64,128]{2,1,0:T(8,128)S(1)} %shard_map.73.body), custom_call_target="tpu_custom_call" | custom-call | flops 11750400 | bytes 196608 | tf_op jit(solution)/shard_map/pallas_call | solution.py:330
  27.9 0.6 %collective-permute-done.7.edge = f32[8,32,128]{2,1,0:T(8,128)S(1)} collective-permute-done((f32[8,32,128]{2,1,0:T(8,128)S(1)}, f32[8,32,128]{2,1,0:T(8,128)S(1)}, u32[]{:S(2)}, u32[]{:S(2)}) %collective-permute-start.7) | collective-permute-done | bytes 131104 | tf_op jit(solution)/shard_map/ppermute | solution.py:366
  28.5 2.2 %shard_map.76.refs_0_ = f32[64,128]{1,0:T(8,128)S(1)} custom-call(f32[8,64,128]{2,1,0:T(8,128)S(1)} %shard_map.73.body, f32[8,32,128]{2,1,0:T(8,128)S(1)} %collective-permute-done.7.edge, f32[5,8,128]{2,1,0:T(8,128)S(1)} %get-tuple-element.17.near, f32[5,16,128]{2,1,0:T(8,128)S(1)} %get-tuple-element.18.middle, f32[5,32,128]{2,1,0:T(8,128)S(1)} %get-tuple-element.19.far), custom_call_target="tpu_custom_call" | custom-call | flops 11059200 | bytes 262144 | tf_op jit(solution)/shard_map/pallas_call | solution.py:333
  30.7 1.9 %collective-permute-start.10 = (f32[64,128]{1,0:T(8,128)S(1)}, f32[64,128]{1,0:T(8,128)S(1)}, u32[]{:S(2)}, u32[]{:S(2)}) collective-permute-start(f32[64,128]{1,0:T(8,128)S(1)} %shard_map.76.refs_0_), channel_id=1, source_target_pairs={{0,192},{1,193},{2,194},{3,195},{4,196},{5,197},{6,198},{7,199},{8... | collective-permute-start | bytes 98312 | tf_op jit(solution)/shard_map/ppermute | solution.py:366
  32.6 1.4 %collective-permute-start.8 = (f32[64,128]{1,0:T(8,128)S(1)}, f32[64,128]{1,0:T(8,128)S(1)}, u32[]{:S(2)}, u32[]{:S(2)}) collective-permute-start(f32[64,128]{1,0:T(8,128)S(1)} %shard_map.76.refs_0_), channel_id=1, source_target_pairs={{0,64},{1,65},{2,66},{3,67},{4,68},{5,69},{6,70},{7,71},{8,72},{9,... | collective-permute-start | bytes 98312 | tf_op jit(solution)/shard_map/ppermute | solution.py:366
  34.0 1.1 %collective-permute-start.11 = (f32[64,128]{1,0:T(8,128)S(1)}, f32[64,128]{1,0:T(8,128)S(1)}, u32[]{:S(2)}, u32[]{:S(2)}) collective-permute-start(f32[64,128]{1,0:T(8,128)S(1)} %shard_map.76.refs_0_), channel_id=1, source_target_pairs={{0,32},{1,33},{2,34},{3,35},{4,36},{5,37},{6,38},{7,39},{8,40},{9,... | collective-permute-start | bytes 98312 | tf_op jit(solution)/shard_map/ppermute | solution.py:366
  35.2 1.0 %collective-permute-start.14 = (f32[64,128]{1,0:T(8,128)S(1)}, f32[64,128]{1,0:T(8,128)S(1)}, u32[]{:S(2)}, u32[]{:S(2)}) collective-permute-start(f32[64,128]{1,0:T(8,128)S(1)} %collective-permute-done.10.refs_3_), channel_id=1, source_target_pairs={{0,32},{1,33},{2,34},{3,35},{4,36},{5,37},{6,38},{7,39},{8,40},{9,... | collective-permute-start | bytes 98312 | tf_op jit(solution)/shard_map/ppermute | solution.py:366
  36.2 0.7 %collective-permute-done.9.refs_2_ = f32[64,128]{1,0:T(8,128)S(1)} collective-permute-done((f32[64,128]{1,0:T(8,128)S(1)}, f32[64,128]{1,0:T(8,128)S(1)}, u32[]{:S(2)}, u32[]{:S(2)}) %collective-permute-start.9) | collective-permute-done | bytes 32800 | tf_op jit(solution)/shard_map/ppermute | solution.py:366
  36.9 1.4 %collective-permute-start.13 = (f32[64,128]{1,0:T(8,128)S(1)}, f32[64,128]{1,0:T(8,128)S(1)}, u32[]{:S(2)}, u32[]{:S(2)}) collective-permute-start(f32[64,128]{1,0:T(8,128)S(1)} %collective-permute-done.9.refs_2_), channel_id=1, source_target_pairs={{0,32},{1,33},{2,34},{3,35},{4,36},{5,37},{6,38},{7,39},{8,40},{9,... | collective-permute-start | bytes 98312 | tf_op jit(solution)/shard_map/ppermute | solution.py:366
  38.3 0.8 %collective-permute-done.13.refs_6_ = f32[64,128]{1,0:T(8,128)S(1)} collective-permute-done((f32[64,128]{1,0:T(8,128)S(1)}, f32[64,128]{1,0:T(8,128)S(1)}, u32[]{:S(2)}, u32[]{:S(2)}) %collective-permute-start.13) | collective-permute-done | bytes 32800 | tf_op jit(solution)/shard_map/ppermute | solution.py:366
  39.2 0.4 collective-permute-done.12.refs_5_
  39.5 0.8 %shard_map.77 = (f32[3,128,128]{2,1,0:T(8,128)}, f32[128,128]{1,0:T(8,128)}) custom-call(f32[64,128]{1,0:T(8,128)S(1)} %shard_map.76.refs_0_, f32[64,128]{1,0:T(8,128)S(1)} %collective-permute-done.8.refs_1_, f32[64,128]{1,0:T(8,128)S(1)} %collective-permute-done.9.refs_2_, f32[64,128]{1,0:T(8,128)S(1)} %collective-permute-done.10.refs_3_, ...), custom_call_target="tpu_custom_call" | custom-call | tf_op jit(solution)/shard_map/pallas_call | solution.py:415
  (16 shorter events, 1.3 us)
Async XLA Ops:
  1.6 4.5 %collective-permute-start = (f32[520,128]{1,0:T(8,128)S(1)}, f32[520,128]{1,0:T(8,128)S(1)}, u32[]{:S(2)}, u32[]{:S(2)}) collective-permute-start(f32[520,128]{1,0:T(8,128)S(1)} %shard_map.69), channel_id=1, source_target_pairs={{0,32},{1,33},{2,34},{3,35},{4,36},{5,37},{6,38},{7,39},{8,40},{9,... | collective-permute-start | bytes 798728 | tf_op jit(solution)/shard_map/ppermute | solution.py:366
  6.3 4.2 %collective-permute-start.1 = (f32[200,128]{1,0:T(8,128)S(1)}, f32[200,128]{1,0:T(8,128)S(1)}, u32[]{:S(2)}, u32[]{:S(2)}) collective-permute-start(f32[200,128]{1,0:T(8,128)S(1)} %get-tuple-element.12), channel_id=1, source_target_pairs={{0,64},{1,65},{2,66},{3,67},{4,68},{5,69},{6,70},{7,71},{8,72},{9,... | collective-permute-start | bytes 307208 | tf_op jit(solution)/shard_map/ppermute | solution.py:366
  6.4 7.0 %collective-permute-start.2 = (f32[200,128]{1,0:T(8,128)S(1)}, f32[200,128]{1,0:T(8,128)S(1)}, u32[]{:S(2)}, u32[]{:S(2)}) collective-permute-start(f32[200,128]{1,0:T(8,128)S(1)} %get-tuple-element.13), channel_id=1, source_target_pairs={{0,128},{1,129},{2,130},{3,131},{4,132},{5,133},{6,134},{7,135},{8... | collective-permute-start | bytes 307208 | tf_op jit(solution)/shard_map/ppermute | solution.py:366
  8.5 7.4 %collective-permute-start.3 = (f32[200,128]{1,0:T(8,128)S(1)}, f32[200,128]{1,0:T(8,128)S(1)}, u32[]{:S(2)}, u32[]{:S(2)}) collective-permute-start(f32[200,128]{1,0:T(8,128)S(1)} %get-tuple-element.14), channel_id=1, source_target_pairs={{0,192},{1,193},{2,194},{3,195},{4,196},{5,197},{6,198},{7,199},{8... | collective-permute-start | bytes 307208 | tf_op jit(solution)/shard_map/ppermute | solution.py:366
  16.1 4.1 %collective-permute-start.4 = (f32[64,128]{1,0:T(8,128)S(1)}, f32[64,128]{1,0:T(8,128)S(1)}, u32[]{:S(2)}, u32[]{:S(2)}) collective-permute-start(f32[64,128]{1,0:T(8,128)S(1)} %shard_map.72), channel_id=1, source_target_pairs={{0,192},{1,2},{2,1},{3,195},{4,196},{5,6},{6,5},{7,199},{8,200},{9... | collective-permute-start | bytes 98312 | tf_op jit(solution)/shard_map/ppermute | solution.py:366
  20.2 3.0 %collective-permute-start.5 = (f32[256,128]{1,0:T(8,128)S(1)}, f32[256,128]{1,0:T(8,128)S(1)}, u32[]{:S(2)}, u32[]{:S(2)}) collective-permute-start(f32[256,128]{1,0:T(8,128)S(1)} %shard_map.71.mine), channel_id=1, source_target_pairs={{0,32},{1,33},{2,34},{3,35},{4,36},{5,37},{6,38},{7,39},{8,40},{9,... | collective-permute-start | bytes 393224 | tf_op jit(solution)/shard_map/ppermute | solution.py:366
  22.0 1.2 %collective-permute-start.6 = (f32[64,128]{1,0:T(8,128)S(1)}, f32[64,128]{1,0:T(8,128)S(1)}, u32[]{:S(2)}, u32[]{:S(2)}) collective-permute-start(f32[64,128]{1,0:T(8,128)S(1)} %collective-permute-done.4.side), channel_id=1, source_target_pairs={{0,32},{1,33},{2,34},{3,35},{4,36},{5,37},{6,38},{7,39},{8,40},{9,... | collective-permute-start | bytes 98312 | tf_op jit(solution)/shard_map/ppermute | solution.py:366
  23.4 5.1 %collective-permute-start.7 = (f32[8,32,128]{2,1,0:T(8,128)S(1)}, f32[8,32,128]{2,1,0:T(8,128)S(1)}, u32[]{:S(2)}, u32[]{:S(2)}) collective-permute-start(f32[8,32,128]{2,1,0:T(8,128)S(1)} %shard_map.74), channel_id=1, source_target_pairs={{0,64},{1,65},{2,66},{3,67},{4,8},{5,9},{6,10},{7,11},{8,4},{9,5},... | collective-permute-start | bytes 393224 | tf_op jit(solution)/shard_map/ppermute | solution.py:366
  30.7 4.4 %collective-permute-start.10 = (f32[64,128]{1,0:T(8,128)S(1)}, f32[64,128]{1,0:T(8,128)S(1)}, u32[]{:S(2)}, u32[]{:S(2)}) collective-permute-start(f32[64,128]{1,0:T(8,128)S(1)} %shard_map.76.refs_0_), channel_id=1, source_target_pairs={{0,192},{1,193},{2,194},{3,195},{4,196},{5,197},{6,198},{7,199},{8... | collective-permute-start | bytes 98312 | tf_op jit(solution)/shard_map/ppermute | solution.py:366
  32.6 4.3 %collective-permute-start.9 = (f32[64,128]{1,0:T(8,128)S(1)}, f32[64,128]{1,0:T(8,128)S(1)}, u32[]{:S(2)}, u32[]{:S(2)}) collective-permute-start(f32[64,128]{1,0:T(8,128)S(1)} %shard_map.76.refs_0_), channel_id=1, source_target_pairs={{0,128},{1,129},{2,130},{3,131},{4,132},{5,133},{6,134},{7,135},{8... | collective-permute-start | bytes 98312 | tf_op jit(solution)/shard_map/ppermute | solution.py:366
  32.6 5.7 %collective-permute-start.8 = (f32[64,128]{1,0:T(8,128)S(1)}, f32[64,128]{1,0:T(8,128)S(1)}, u32[]{:S(2)}, u32[]{:S(2)}) collective-permute-start(f32[64,128]{1,0:T(8,128)S(1)} %shard_map.76.refs_0_), channel_id=1, source_target_pairs={{0,64},{1,65},{2,66},{3,67},{4,68},{5,69},{6,70},{7,71},{8,72},{9,... | collective-permute-start | bytes 98312 | tf_op jit(solution)/shard_map/ppermute | solution.py:366
  34.0 4.3 %collective-permute-start.11 = (f32[64,128]{1,0:T(8,128)S(1)}, f32[64,128]{1,0:T(8,128)S(1)}, u32[]{:S(2)}, u32[]{:S(2)}) collective-permute-start(f32[64,128]{1,0:T(8,128)S(1)} %shard_map.76.refs_0_), channel_id=1, source_target_pairs={{0,32},{1,33},{2,34},{3,35},{4,36},{5,37},{6,38},{7,39},{8,40},{9,... | collective-permute-start | bytes 98312 | tf_op jit(solution)/shard_map/ppermute | solution.py:366
  35.2 3.1 %collective-permute-start.14 = (f32[64,128]{1,0:T(8,128)S(1)}, f32[64,128]{1,0:T(8,128)S(1)}, u32[]{:S(2)}, u32[]{:S(2)}) collective-permute-start(f32[64,128]{1,0:T(8,128)S(1)} %collective-permute-done.10.refs_3_), channel_id=1, source_target_pairs={{0,32},{1,33},{2,34},{3,35},{4,36},{5,37},{6,38},{7,39},{8,40},{9,... | collective-permute-start | bytes 98312 | tf_op jit(solution)/shard_map/ppermute | solution.py:366
  36.9 2.3 %collective-permute-start.13 = (f32[64,128]{1,0:T(8,128)S(1)}, f32[64,128]{1,0:T(8,128)S(1)}, u32[]{:S(2)}, u32[]{:S(2)}) collective-permute-start(f32[64,128]{1,0:T(8,128)S(1)} %collective-permute-done.9.refs_2_), channel_id=1, source_target_pairs={{0,32},{1,33},{2,34},{3,35},{4,36},{5,37},{6,38},{7,39},{8,40},{9,... | collective-permute-start | bytes 98312 | tf_op jit(solution)/shard_map/ppermute | solution.py:366
  38.3 1.2 %collective-permute-start.12 = (f32[64,128]{1,0:T(8,128)S(1)}, f32[64,128]{1,0:T(8,128)S(1)}, u32[]{:S(2)}, u32[]{:S(2)}) collective-permute-start(f32[64,128]{1,0:T(8,128)S(1)} %collective-permute-done.8.refs_1_), channel_id=1, source_target_pairs={{0,32},{1,33},{2,34},{3,35},{4,36},{5,37},{6,38},{7,39},{8,40},{9,... | collective-permute-start | bytes 98312 | tf_op jit(solution)/shard_map/ppermute | solution.py:366

commit v6 on v5

--- a/solution.py
+++ b/solution.py
@@ -400,9 +400,12 @@
             cost=(1, 4),
         )(*parts)[0]
 
-    rim = send(means(True), across, 6)
-    mine, rim = lax.optimization_barrier((means(False), rim))
-    sides = (mine, other_core(mine), rim, other_core(rim))
+    rim = means(True)
+    mine = means(False)
+    theirs = other_core(mine)
+    near_rim = send(rim, across, 6)
+    cross_rim = send(rim, lambda s, ty, tx: (across(s, ty, tx)[0] ^ 1, *across(s, ty, tx)[1:]), 7)
+    sides = (mine, theirs, near_rim, cross_rim)
 
     def joined(wants_edge, count):
         kernel = functools.partial(row_kernel, wants_edge)

time: 40.5 us -> 40.7 us (level)
  starting transfers between devices: 19.5 us -> 20.1 us
  waiting for transfers between devices: 11.8 us -> 11.3 us
    ppermute x15, starting transfers between devices: 19.5 us -> 20.1 us  [send(): return lax.ppermute(value, AXES, pairs(sizes, partner, spare))]
    ppermute x15, waiting for transfers between devices: 11.8 us -> 11.3 us  [send(): return lax.ppermute(value, AXES, pairs(sizes, partner, spare))]
  transfers between devices with their start and end apart: 15 -> 15, of which waited for: 10 -> 9; matrix products, arithmetic and copies ran while one was open for 0% -> 0% of each run, Pallas kernels for 10% -> 10%
where the time goes in v6:
time: 40.7 us; the launch traced here: 40.6 us
  starting transfers between devices  20.1 us (49%)
  waiting for transfers between devices  11.3 us (28%)
  Pallas kernels  8.38 us (21%)
  between operations  0.72 us (2%)
    ppermute x15, starting transfers between devices, send(): return lax.ppermute(value, AXES, pairs(sizes, partner, spare))  20.1 us
    ppermute x15, waiting for transfers between devices, send(): return lax.ppermute(value, AXES, pairs(sizes, partner, spare))  11.3 us
    pallas_call x1, Pallas kernels, run_filter(): call(inner_kernel, [(5, 8, TILE), (5, 16, TILE), (5, 32, TILE)], scratch(...  2.53 us
    pallas_call x1, Pallas kernels, run_filter(): call(outer_kernel, [(HALF, TILE)], scratch(WIN), cost=(16, 4))  2.25 us
    pallas_call x2, Pallas kernels, pick(): call(functools.partial(pick_kernel, wanted), [packed], [pltpu.VMEM((8, 8)...  1.99 us
    pallas_call x1, Pallas kernels, per_device(): call(tile_kernel, [(3, TILE, TILE), (TILE, TILE)])(*got, *theirs)  0.83 us
  transfers between devices with their start and end apart: 15, of which 9 were waited for; matrix products, arithmetic and copies ran while one was open for 0% of the time, Pallas kernels for 10%

profile of v6, /device:TPU:1, one launch (start us, length us, event | category | flops | bytes accessed | tf_op | source)
XLA Modules:
  0.0 40.6 jit_solution(5211451532351278681)
XLA Ops:
  0.6 1.0 %shard_map.69 = f32[520,128]{1,0:T(8,128)S(1)} custom-call(f32[1,3,128,128]{3,2,1,0:T(8,128)} %rad.3, f32[1,128,128]{2,1,0:T(8,128)} %mom.3, f32[1,3,128,128]{3,2,1,0:T(8,128)} %nor.3, f32[1,128,128]{2,1,0:T(8,128)} %dep.3, s32[1,8,8]{2,1,0:T(8,128)} %cnt.3), custom_call_target="tpu_custom_call" | custom-call | flops 691200 | bytes 262144 | tf_op jit(solution)/shard_map/pallas_call | solution.py:381
  1.6 3.3 %collective-permute-start = (f32[520,128]{1,0:T(8,128)S(1)}, f32[520,128]{1,0:T(8,128)S(1)}, u32[]{:S(2)}, u32[]{:S(2)}) collective-permute-start(f32[520,128]{1,0:T(8,128)S(1)} %shard_map.69), channel_id=1, source_target_pairs={{0,32},{1,33},{2,34},{3,35},{4,36},{5,37},{6,38},{7,39},{8,40},{9,... | collective-permute-start | bytes 798728 | tf_op jit(solution)/shard_map/ppermute | solution.py:366
  5.0 1.0 %shard_map.68.keep = f32[520,128]{1,0:T(8,128)S(1)} custom-call(f32[1,3,128,128]{3,2,1,0:T(8,128)} %rad.3, f32[1,128,128]{2,1,0:T(8,128)} %mom.3, f32[1,3,128,128]{3,2,1,0:T(8,128)} %nor.3, f32[1,128,128]{2,1,0:T(8,128)} %dep.3, s32[1,8,8]{2,1,0:T(8,128)} %cnt.3), custom_call_target="tpu_custom_call" | custom-call | flops 691200 | bytes 262144 | tf_op jit(solution)/shard_map/pallas_call | solution.py:381
  6.4 2.2 %collective-permute-start.2 = (f32[200,128]{1,0:T(8,128)S(1)}, f32[200,128]{1,0:T(8,128)S(1)}, u32[]{:S(2)}, u32[]{:S(2)}) collective-permute-start(f32[200,128]{1,0:T(8,128)S(1)} %get-tuple-element.11), channel_id=1, source_target_pairs={{0,128},{1,129},{2,130},{3,131},{4,132},{5,133},{6,134},{7,135},{8... | collective-permute-start | bytes 307208 | tf_op jit(solution)/shard_map/ppermute | solution.py:366
  8.5 1.7 %collective-permute-start.3 = (f32[200,128]{1,0:T(8,128)S(1)}, f32[200,128]{1,0:T(8,128)S(1)}, u32[]{:S(2)}, u32[]{:S(2)}) collective-permute-start(f32[200,128]{1,0:T(8,128)S(1)} %get-tuple-element.12), channel_id=1, source_target_pairs={{0,192},{1,193},{2,194},{3,195},{4,196},{5,197},{6,198},{7,199},{8... | collective-permute-start | bytes 307208 | tf_op jit(solution)/shard_map/ppermute | solution.py:366
  10.5 2.9 %collective-permute-done.2.r2 = f32[200,128]{1,0:T(8,128)S(1)} collective-permute-done((f32[200,128]{1,0:T(8,128)S(1)}, f32[200,128]{1,0:T(8,128)S(1)}, u32[]{:S(2)}, u32[]{:S(2)}) %collective-permute-start.2) | collective-permute-done | bytes 102432 | tf_op jit(solution)/shard_map/ppermute | solution.py:366
  13.4 2.6 %collective-permute-done.3.r3 = f32[200,128]{1,0:T(8,128)S(1)} collective-permute-done((f32[200,128]{1,0:T(8,128)S(1)}, f32[200,128]{1,0:T(8,128)S(1)}, u32[]{:S(2)}, u32[]{:S(2)}) %collective-permute-start.3) | collective-permute-done | bytes 102432 | tf_op jit(solution)/shard_map/ppermute | solution.py:366
  16.1 0.7 %collective-permute-start.4 = (f32[256,128]{1,0:T(8,128)S(1)}, f32[256,128]{1,0:T(8,128)S(1)}, u32[]{:S(2)}, u32[]{:S(2)}) collective-permute-start(f32[256,128]{1,0:T(8,128)S(1)} %shard_map.71.mine), channel_id=1, source_target_pairs={{0,32},{1,33},{2,34},{3,35},{4,36},{5,37},{6,38},{7,39},{8,40},{9,... | collective-permute-start | bytes 393224 | tf_op jit(solution)/shard_map/ppermute | solution.py:366
  17.0 1.7 %collective-permute-start.6 = (f32[64,128]{1,0:T(8,128)S(1)}, f32[64,128]{1,0:T(8,128)S(1)}, u32[]{:S(2)}, u32[]{:S(2)}) collective-permute-start(f32[64,128]{1,0:T(8,128)S(1)} %shard_map.72), channel_id=1, source_target_pairs={{0,224},{1,34},{2,33},{3,227},{4,228},{5,38},{6,37},{7,231},{8,232... | collective-permute-start | bytes 98312 | tf_op jit(solution)/shard_map/ppermute | solution.py:366
  18.7 1.0 %collective-permute-start.5 = (f32[64,128]{1,0:T(8,128)S(1)}, f32[64,128]{1,0:T(8,128)S(1)}, u32[]{:S(2)}, u32[]{:S(2)}) collective-permute-start(f32[64,128]{1,0:T(8,128)S(1)} %shard_map.72), channel_id=1, source_target_pairs={{0,192},{1,2},{2,1},{3,195},{4,196},{5,6},{6,5},{7,199},{8,200},{9... | collective-permute-start | bytes 98312 | tf_op jit(solution)/shard_map/ppermute | solution.py:366
  19.7 2.0 %collective-permute-done.6.other_side = f32[64,128]{1,0:T(8,128)S(1)} collective-permute-done((f32[64,128]{1,0:T(8,128)S(1)}, f32[64,128]{1,0:T(8,128)S(1)}, u32[]{:S(2)}, u32[]{:S(2)}) %collective-permute-start.6) | collective-permute-done | bytes 32800 | tf_op jit(solution)/shard_map/ppermute | solution.py:366
  21.7 1.0 %collective-permute-done.5.side = f32[64,128]{1,0:T(8,128)S(1)} collective-permute-done((f32[64,128]{1,0:T(8,128)S(1)}, f32[64,128]{1,0:T(8,128)S(1)}, u32[]{:S(2)}, u32[]{:S(2)}) %collective-permute-start.5) | collective-permute-done | bytes 32800 | tf_op jit(solution)/shard_map/ppermute | solution.py:366
  22.8 1.1 %collective-permute-start.7 = (f32[8,32,128]{2,1,0:T(8,128)S(1)}, f32[8,32,128]{2,1,0:T(8,128)S(1)}, u32[]{:S(2)}, u32[]{:S(2)}) collective-permute-start(f32[8,32,128]{2,1,0:T(8,128)S(1)} %shard_map.74), channel_id=1, source_target_pairs={{0,64},{1,65},{2,66},{3,67},{4,8},{5,9},{6,10},{7,11},{8,4},{9,5},... | collective-permute-start | bytes 393224 | tf_op jit(solution)/shard_map/ppermute | solution.py:366
  24.1 2.5 %shard_map.75 = (f32[5,8,128]{2,1,0:T(8,128)S(1)}, f32[5,16,128]{2,1,0:T(8,128)S(1)}, f32[5,32,128]{2,1,0:T(8,128)S(1)}) custom-call(f32[8,64,128]{2,1,0:T(8,128)S(1)} %shard_map.73.body), custom_call_target="tpu_custom_call" | custom-call | flops 11750400 | bytes 196608 | tf_op jit(solution)/shard_map/pallas_call | solution.py:330
  26.6 1.3 %collective-permute-done.7.edge = f32[8,32,128]{2,1,0:T(8,128)S(1)} collective-permute-done((f32[8,32,128]{2,1,0:T(8,128)S(1)}, f32[8,32,128]{2,1,0:T(8,128)S(1)}, u32[]{:S(2)}, u32[]{:S(2)}) %collective-permute-start.7) | collective-permute-done | bytes 131104 | tf_op jit(solution)/shard_map/ppermute | solution.py:366
  27.9 2.3 %shard_map.76.refs_0_ = f32[64,128]{1,0:T(8,128)S(1)} custom-call(f32[8,64,128]{2,1,0:T(8,128)S(1)} %shard_map.73.body, f32[8,32,128]{2,1,0:T(8,128)S(1)} %collective-permute-done.7.edge, f32[5,8,128]{2,1,0:T(8,128)S(1)} %get-tuple-element.13.near, f32[5,16,128]{2,1,0:T(8,128)S(1)} %get-tuple-element.14.middle, f32[5,32,128]{2,1,0:T(8,128)S(1)} %get-tuple-element.15.far), custom_call_target="tpu_custom_call" | custom-call | flops 11059200 | bytes 262144 | tf_op jit(solution)/shard_map/pallas_call | solution.py:333
  30.2 1.2 %collective-permute-start.10 = (f32[64,128]{1,0:T(8,128)S(1)}, f32[64,128]{1,0:T(8,128)S(1)}, u32[]{:S(2)}, u32[]{:S(2)}) collective-permute-start(f32[64,128]{1,0:T(8,128)S(1)} %shard_map.76.refs_0_), channel_id=1, source_target_pairs={{0,192},{1,193},{2,194},{3,195},{4,196},{5,197},{6,198},{7,199},{8... | collective-permute-start | bytes 98312 | tf_op jit(solution)/shard_map/ppermute | solution.py:366
  31.4 2.1 %collective-permute-start.8 = (f32[64,128]{1,0:T(8,128)S(1)}, f32[64,128]{1,0:T(8,128)S(1)}, u32[]{:S(2)}, u32[]{:S(2)}) collective-permute-start(f32[64,128]{1,0:T(8,128)S(1)} %shard_map.76.refs_0_), channel_id=1, source_target_pairs={{0,64},{1,65},{2,66},{3,67},{4,68},{5,69},{6,70},{7,71},{8,72},{9,... | collective-permute-start | bytes 98312 | tf_op jit(solution)/shard_map/ppermute | solution.py:366
  33.5 2.6 %collective-permute-start.11 = (f32[64,128]{1,0:T(8,128)S(1)}, f32[64,128]{1,0:T(8,128)S(1)}, u32[]{:S(2)}, u32[]{:S(2)}) collective-permute-start(f32[64,128]{1,0:T(8,128)S(1)} %shard_map.76.refs_0_), channel_id=1, source_target_pairs={{0,32},{1,33},{2,34},{3,35},{4,36},{5,37},{6,38},{7,39},{8,40},{9,... | collective-permute-start | bytes 98312 | tf_op jit(solution)/shard_map/ppermute | solution.py:366
  36.1 1.0 %collective-permute-start.14 = (f32[64,128]{1,0:T(8,128)S(1)}, f32[64,128]{1,0:T(8,128)S(1)}, u32[]{:S(2)}, u32[]{:S(2)}) collective-permute-start(f32[64,128]{1,0:T(8,128)S(1)} %collective-permute-done.10.refs_3_), channel_id=1, source_target_pairs={{0,32},{1,33},{2,34},{3,35},{4,36},{5,37},{6,38},{7,39},{8,40},{9,... | collective-permute-start | bytes 98312 | tf_op jit(solution)/shard_map/ppermute | solution.py:366
  37.1 1.4 %collective-permute-start.13 = (f32[64,128]{1,0:T(8,128)S(1)}, f32[64,128]{1,0:T(8,128)S(1)}, u32[]{:S(2)}, u32[]{:S(2)}) collective-permute-start(f32[64,128]{1,0:T(8,128)S(1)} %collective-permute-done.9.refs_2_), channel_id=1, source_target_pairs={{0,32},{1,33},{2,34},{3,35},{4,36},{5,37},{6,38},{7,39},{8,40},{9,... | collective-permute-start | bytes 98312 | tf_op jit(solution)/shard_map/ppermute | solution.py:366
  38.5 0.8 %collective-permute-done.13.refs_6_ = f32[64,128]{1,0:T(8,128)S(1)} collective-permute-done((f32[64,128]{1,0:T(8,128)S(1)}, f32[64,128]{1,0:T(8,128)S(1)}, u32[]{:S(2)}, u32[]{:S(2)}) %collective-permute-start.13) | collective-permute-done | bytes 32800 | tf_op jit(solution)/shard_map/ppermute | solution.py:366
  39.4 0.4 collective-permute-done.12.refs_5_
  39.7 0.8 %shard_map.77 = (f32[3,128,128]{2,1,0:T(8,128)}, f32[128,128]{1,0:T(8,128)}) custom-call(f32[64,128]{1,0:T(8,128)S(1)} %shard_map.76.refs_0_, f32[64,128]{1,0:T(8,128)S(1)} %collective-permute-done.8.refs_1_, f32[64,128]{1,0:T(8,128)S(1)} %collective-permute-done.9.refs_2_, f32[64,128]{1,0:T(8,128)S(1)} %collective-permute-done.10.refs_3_, ...), custom_call_target="tpu_custom_call" | custom-call | tf_op jit(solution)/shard_map/pallas_call | solution.py:418
  (16 shorter events, 1.3 us)
Async XLA Ops:
  1.6 4.5 %collective-permute-start = (f32[520,128]{1,0:T(8,128)S(1)}, f32[520,128]{1,0:T(8,128)S(1)}, u32[]{:S(2)}, u32[]{:S(2)}) collective-permute-start(f32[520,128]{1,0:T(8,128)S(1)} %shard_map.69), channel_id=1, source_target_pairs={{0,32},{1,33},{2,34},{3,35},{4,36},{5,37},{6,38},{7,39},{8,40},{9,... | collective-permute-start | bytes 798728 | tf_op jit(solution)/shard_map/ppermute | solution.py:366
  6.3 4.2 %collective-permute-start.1 = (f32[200,128]{1,0:T(8,128)S(1)}, f32[200,128]{1,0:T(8,128)S(1)}, u32[]{:S(2)}, u32[]{:S(2)}) collective-permute-start(f32[200,128]{1,0:T(8,128)S(1)} %get-tuple-element.10), channel_id=1, source_target_pairs={{0,64},{1,65},{2,66},{3,67},{4,68},{5,69},{6,70},{7,71},{8,72},{9,... | collective-permute-start | bytes 307208 | tf_op jit(solution)/shard_map/ppermute | solution.py:366
  6.4 7.0 %collective-permute-start.2 = (f32[200,128]{1,0:T(8,128)S(1)}, f32[200,128]{1,0:T(8,128)S(1)}, u32[]{:S(2)}, u32[]{:S(2)}) collective-permute-start(f32[200,128]{1,0:T(8,128)S(1)} %get-tuple-element.11), channel_id=1, source_target_pairs={{0,128},{1,129},{2,130},{3,131},{4,132},{5,133},{6,134},{7,135},{8... | collective-permute-start | bytes 307208 | tf_op jit(solution)/shard_map/ppermute | solution.py:366
  8.5 7.4 %collective-permute-start.3 = (f32[200,128]{1,0:T(8,128)S(1)}, f32[200,128]{1,0:T(8,128)S(1)}, u32[]{:S(2)}, u32[]{:S(2)}) collective-permute-start(f32[200,128]{1,0:T(8,128)S(1)} %get-tuple-element.12), channel_id=1, source_target_pairs={{0,192},{1,193},{2,194},{3,195},{4,196},{5,197},{6,198},{7,199},{8... | collective-permute-start | bytes 307208 | tf_op jit(solution)/shard_map/ppermute | solution.py:366
  16.1 6.6 %collective-permute-start.4 = (f32[256,128]{1,0:T(8,128)S(1)}, f32[256,128]{1,0:T(8,128)S(1)}, u32[]{:S(2)}, u32[]{:S(2)}) collective-permute-start(f32[256,128]{1,0:T(8,128)S(1)} %shard_map.71.mine), channel_id=1, source_target_pairs={{0,32},{1,33},{2,34},{3,35},{4,36},{5,37},{6,38},{7,39},{8,40},{9,... | collective-permute-start | bytes 393224 | tf_op jit(solution)/shard_map/ppermute | solution.py:366
  17.0 4.6 %collective-permute-start.6 = (f32[64,128]{1,0:T(8,128)S(1)}, f32[64,128]{1,0:T(8,128)S(1)}, u32[]{:S(2)}, u32[]{:S(2)}) collective-permute-start(f32[64,128]{1,0:T(8,128)S(1)} %shard_map.72), channel_id=1, source_target_pairs={{0,224},{1,34},{2,33},{3,227},{4,228},{5,38},{6,37},{7,231},{8,232... | collective-permute-start | bytes 98312 | tf_op jit(solution)/shard_map/ppermute | solution.py:366
  18.7 4.0 %collective-permute-start.5 = (f32[64,128]{1,0:T(8,128)S(1)}, f32[64,128]{1,0:T(8,128)S(1)}, u32[]{:S(2)}, u32[]{:S(2)}) collective-permute-start(f32[64,128]{1,0:T(8,128)S(1)} %shard_map.72), channel_id=1, source_target_pairs={{0,192},{1,2},{2,1},{3,195},{4,196},{5,6},{6,5},{7,199},{8,200},{9... | collective-permute-start | bytes 98312 | tf_op jit(solution)/shard_map/ppermute | solution.py:366
  22.8 5.1 %collective-permute-start.7 = (f32[8,32,128]{2,1,0:T(8,128)S(1)}, f32[8,32,128]{2,1,0:T(8,128)S(1)}, u32[]{:S(2)}, u32[]{:S(2)}) collective-permute-start(f32[8,32,128]{2,1,0:T(8,128)S(1)} %shard_map.74), channel_id=1, source_target_pairs={{0,64},{1,65},{2,66},{3,67},{4,8},{5,9},{6,10},{7,11},{8,4},{9,5},... | collective-permute-start | bytes 393224 | tf_op jit(solution)/shard_map/ppermute | solution.py:366
  30.2 5.9 %collective-permute-start.10 = (f32[64,128]{1,0:T(8,128)S(1)}, f32[64,128]{1,0:T(8,128)S(1)}, u32[]{:S(2)}, u32[]{:S(2)}) collective-permute-start(f32[64,128]{1,0:T(8,128)S(1)} %shard_map.76.refs_0_), channel_id=1, source_target_pairs={{0,192},{1,193},{2,194},{3,195},{4,196},{5,197},{6,198},{7,199},{8... | collective-permute-start | bytes 98312 | tf_op jit(solution)/shard_map/ppermute | solution.py:366
  31.4 5.7 %collective-permute-start.9 = (f32[64,128]{1,0:T(8,128)S(1)}, f32[64,128]{1,0:T(8,128)S(1)}, u32[]{:S(2)}, u32[]{:S(2)}) collective-permute-start(f32[64,128]{1,0:T(8,128)S(1)} %shard_map.76.refs_0_), channel_id=1, source_target_pairs={{0,128},{1,129},{2,130},{3,131},{4,132},{5,133},{6,134},{7,135},{8... | collective-permute-start | bytes 98312 | tf_op jit(solution)/shard_map/ppermute | solution.py:366
  31.4 7.1 %collective-permute-start.8 = (f32[64,128]{1,0:T(8,128)S(1)}, f32[64,128]{1,0:T(8,128)S(1)}, u32[]{:S(2)}, u32[]{:S(2)}) collective-permute-start(f32[64,128]{1,0:T(8,128)S(1)} %shard_map.76.refs_0_), channel_id=1, source_target_pairs={{0,64},{1,65},{2,66},{3,67},{4,68},{5,69},{6,70},{7,71},{8,72},{9,... | collective-permute-start | bytes 98312 | tf_op jit(solution)/shard_map/ppermute | solution.py:366
  33.5 5.0 %collective-permute-start.11 = (f32[64,128]{1,0:T(8,128)S(1)}, f32[64,128]{1,0:T(8,128)S(1)}, u32[]{:S(2)}, u32[]{:S(2)}) collective-permute-start(f32[64,128]{1,0:T(8,128)S(1)} %shard_map.76.refs_0_), channel_id=1, source_target_pairs={{0,32},{1,33},{2,34},{3,35},{4,36},{5,37},{6,38},{7,39},{8,40},{9,... | collective-permute-start | bytes 98312 | tf_op jit(solution)/shard_map/ppermute | solution.py:366
  36.1 2.5 %collective-permute-start.14 = (f32[64,128]{1,0:T(8,128)S(1)}, f32[64,128]{1,0:T(8,128)S(1)}, u32[]{:S(2)}, u32[]{:S(2)}) collective-permute-start(f32[64,128]{1,0:T(8,128)S(1)} %collective-permute-done.10.refs_3_), channel_id=1, source_target_pairs={{0,32},{1,33},{2,34},{3,35},{4,36},{5,37},{6,38},{7,39},{8,40},{9,... | collective-permute-start | bytes 98312 | tf_op jit(solution)/shard_map/ppermute | solution.py:366
  37.1 2.3 %collective-permute-start.13 = (f32[64,128]{1,0:T(8,128)S(1)}, f32[64,128]{1,0:T(8,128)S(1)}, u32[]{:S(2)}, u32[]{:S(2)}) collective-permute-start(f32[64,128]{1,0:T(8,128)S(1)} %collective-permute-done.9.refs_2_), channel_id=1, source_target_pairs={{0,32},{1,33},{2,34},{3,35},{4,36},{5,37},{6,38},{7,39},{8,40},{9,... | collective-permute-start | bytes 98312 | tf_op jit(solution)/shard_map/ppermute | solution.py:366
  38.5 1.2 %collective-permute-start.12 = (f32[64,128]{1,0:T(8,128)S(1)}, f32[64,128]{1,0:T(8,128)S(1)}, u32[]{:S(2)}, u32[]{:S(2)}) collective-permute-start(f32[64,128]{1,0:T(8,128)S(1)} %collective-permute-done.8.refs_1_), channel_id=1, source_target_pairs={{0,32},{1,33},{2,34},{3,35},{4,36},{5,37},{6,38},{7,39},{8,40},{9,... | collective-permute-start | bytes 98312 | tf_op jit(solution)/shard_map/ppermute | solution.py:366
